TPU v7x, 512 devices: a whole 4x8x8 slice. The times are simulated.
512 devices in a mesh: panel: 2 (over core), lon: 32 (over x, y), lat: 8 (over z).
Axes of the slice: x: 4, y: 8, z: 8, core: 2. Of those that a mesh axis runs over, the one named last changes fastest.
Arguments:
- fields: float32 [2, 24, 1024, 1024], P('panel', None, 'lon', 'lat'), may hold values from -6 to 6
- offsets: int32 [2, 2, 128, 8], P('panel', None, 'lon', 'lat'), may hold values from -7 to 7
- fractions: float32 [2, 2, 1024, 1024], P('panel', None, 'lon', 'lat'), may hold values from 0 to 1
- send_count: int32 [2, 32, 8], P('panel', 'lon', 'lat'), may hold values from 0 to 16, as said below
- send_owner: int32 [2, 32, 8, 16], P('panel', 'lon', 'lat'), may hold values from 0 to 31, as said below
- send_cell: int32 [2, 32, 8, 16], P('panel', 'lon', 'lat'), may hold values from 0 to 3966, as said below
- send_target: int32 [2, 32, 8, 16], P('panel', 'lon', 'lat'), may hold values from 0 to 127, as said below
- send_frac: float32 [2, 32, 8, 2, 16], P('panel', 'lon', 'lat'), may hold values from 0 to 1
Outputs:
- advected_fields: float32 [2, 24, 1024, 1024], P('panel', None, 'lon', 'lat')
Inputs may be any that keep to these rules, and one draw needn't show every extreme that they name: `send_count`: 16 on the devices that give donor values and 0 elsewhere; in each row of devices along longitude (one panel, one latitude index) the donors are the first 16 or the last 16 longitude indices. `send_owner`: the receiving device lies on the other panel at the same latitude index and is at the first or the last longitude index; the live slots of a donor name each of the two exactly 8 times. `send_cell`: lon_row * 128 + lat_col with lon_row < 31 and lat_col < 127. `send_target`: over the live slots of all donors that fill one receiving device, every value from 0 to 127 appears exactly once.
All inputs are finite; a program needn't handle non-finite values.
Results may differ from a plain program's by a relative error of at most 0.00002.
Values sent between devices are 32-bit elements; how exact they have to be, the bound alone decides.
No kernel may reach another device: no remote copies, remote signals or barrier semaphores. Data moves between devices by JAX's collectives and lax.ppermute only.
A program may use at most 64 MiB of HBM per device.

v0:
```python
import jax
import jax.numpy as jnp
from jax import lax
from jax.sharding import PartitionSpec as P

TILE = 8
BLOCK = 128
HALO = 9


def with_halo(cells, sides, width):
    for axis, dim in sides:
        count = lax.axis_size(axis)
        ends = count - 1
        head = lax.slice_in_dim(cells, 0, width, axis=dim)
        tail = lax.slice_in_dim(cells, cells.shape[dim] - width, cells.shape[dim], axis=dim)
        cells = jnp.concatenate(
            [
                lax.ppermute(tail, axis, [(i, (i + 1) % count) for i in range(ends)]),
                cells,
                lax.ppermute(head, axis, [((i + 1) % count, i) for i in range(ends)]),
            ],
            axis=dim,
        )
    return cells


def lagrange(x):
    return (
        -x * (x - 1.0) * (x - 2.0) / 6.0,
        (x + 1.0) * (x - 1.0) * (x - 2.0) / 2.0,
        -(x + 1.0) * x * (x - 2.0) / 2.0,
        (x + 1.0) * x * (x - 1.0) / 6.0,
    )


def interpolate(window, frac_lon, frac_lat):
    lon_weights = lagrange(frac_lon)
    lat_weights = lagrange(frac_lat)
    summed = jnp.zeros((window.shape[0], TILE, BLOCK), jnp.float32)
    for a in range(4):
        inner_sum = jnp.zeros((window.shape[0], TILE, BLOCK), jnp.float32)
        for b in range(4):
            inner_sum = inner_sum + lat_weights[b] * window[:, a : a + TILE, b : b + BLOCK]
        summed = summed + lon_weights[a] * inner_sum
    return summed


def advect(padded, offsets, fractions, halo_width):
    tiles_lon = offsets.shape[1]
    tiles_lat = offsets.shape[2]
    channels = padded.shape[0]

    def one_row(t):

        def one_tile(u):
            start_lon = t * TILE + halo_width + offsets[0, t, u] - 1
            start_lat = u * BLOCK + halo_width + offsets[1, t, u] - 1
            window = lax.dynamic_slice(
                padded, (jnp.int32(0), start_lon, start_lat), (channels, TILE + 3, BLOCK + 3)
            )
            frac_tile = lax.dynamic_slice(
                fractions, (jnp.int32(0), t * TILE, u * BLOCK), (2, TILE, BLOCK)
            )
            return interpolate(window, frac_tile[0], frac_tile[1])

        return jax.vmap(one_tile)(jnp.arange(tiles_lat, dtype=jnp.int32))

    tiled = lax.map(one_row, jnp.arange(tiles_lon, dtype=jnp.int32))
    return tiled.transpose(2, 0, 3, 1, 4).reshape(channels, tiles_lon * TILE, tiles_lat * BLOCK)


def bilinear(base_val, lat_next, lon_next, diagonal_next, a, b):
    return (
        (1.0 - a) * (1.0 - b) * base_val
        + (1.0 - a) * b * lat_next
        + a * (1.0 - b) * lon_next
        + a * b * diagonal_next
    )


def body(fields, offsets, fractions, send_count, send_owner, send_cell, send_target, send_frac):
    local_block = fields[0]
    channels, row_count, col_count = local_block.shape
    padded = with_halo(local_block, (("lon", 1), ("lat", 2)), HALO)
    advected = advect(padded, offsets[0], fractions[0], HALO)
    slot_count = send_owner.shape[-1]
    capacity = slot_count // 2
    lon_count = lax.axis_size("lon")
    owner_lon = send_owner[0, 0, 0]
    donor_cell = send_cell[0, 0, 0]
    target = send_target[0, 0, 0]
    weights = send_frac[0, 0, 0]
    flattened = advected.reshape(channels, row_count * col_count)
    donor = bilinear(
        flattened[:, donor_cell],
        flattened[:, donor_cell + 1],
        flattened[:, donor_cell + col_count],
        flattened[:, donor_cell + col_count + 1],
        weights[0],
        weights[1],
    )
    slot_index = jnp.arange(slot_count, dtype=jnp.int32)
    is_live = slot_index < send_count[0, 0, 0]
    same_owner = (
        (owner_lon[:, None] == owner_lon[None, :])
        & (slot_index[None, :] < slot_index[:, None])
        & is_live[None, :]
    )
    position = jnp.sum(same_owner.astype(jnp.int32), axis=1)
    other_panel = 1 - lax.axis_index("panel")
    buckets = 2 * lon_count * capacity
    destination = (other_panel * lon_count + owner_lon) * capacity + position
    destination = jnp.where(is_live, destination, buckets)
    send_values = (
        jnp.zeros((buckets, channels), jnp.float32).at[destination].set(donor.T, mode="drop")
    )
    send_places = (
        jnp.full((buckets,), col_count, jnp.int32).at[destination].set(target, mode="drop")
    )
    received, recv_target = (
        lax.all_to_all(
            send_values.reshape(2 * lon_count, capacity, channels),
            ("panel", "lon"),
            split_axis=0,
            concat_axis=0,
            tiled=True,
        ),
        lax.all_to_all(
            send_places.reshape(2 * lon_count, capacity),
            ("panel", "lon"),
            split_axis=0,
            concat_axis=0,
            tiled=True,
        ),
    )
    received = received.reshape(-1, channels)
    recv_target = recv_target.reshape(-1)
    rim_values = (
        jnp.zeros((col_count, channels), jnp.float32).at[recv_target].set(received, mode="drop").T
    )
    lon_index = lax.axis_index("lon")
    first_row = jnp.where(lon_index == 0, rim_values, advected[:, 0, :])
    last_row = jnp.where(lon_index == lon_count - 1, rim_values, advected[:, row_count - 1, :])
    advected = advected.at[:, 0, :].set(first_row).at[:, row_count - 1, :].set(last_row)
    return advected[None]


def solution(mesh):
    placed = (
        P("panel", None, "lon", "lat"),
        P("panel", None, "lon", "lat"),
        P("panel", None, "lon", "lat"),
        P("panel", "lon", "lat"),
        P("panel", "lon", "lat", None),
        P("panel", "lon", "lat", None),
        P("panel", "lon", "lat", None),
        P("panel", "lon", "lat", None, None),
    )
    return jax.shard_map(
        body, mesh=mesh, in_specs=placed, out_specs=P("panel", None, "lon", "lat"), check_vma=False
    )
```

profile of v0, /device:TPU:192, one launch (start us, length us, event | category | flops | bytes accessed | tf_op | source)
XLA Modules:
  0.0 99.1 jit_solution(3361628313032984476)
XLA Ops:
  0.0 1.3 %copy.62 = f32[1,24,32,128]{3,1,2,0:T(8,128)S(1)} copy(f32[1,24,32,128]{3,2,1,0:T(8,128)} %param.14) | data formatting | bytes 786432 | tf_op args[0]
  1.3 3.5 %collective-permute-start = (f32[24,9,128]{2,0,1:T(8,128)S(1)}, f32[24,9,128]{2,0,1:T(8,128)S(1)}, u32[]{:S(2)}, u32[]{:S(2)}) collective-permute-start(f32[24,9,128]{2,0,1:T(8,128)S(1)} %get-tuple-element.283), channel_id=1, source_target_pairs={{0,8},{8,16},{16,24},{24,32},{32,40},{40,48},{48,56},{56,64},{64,7... | collective-permute-start | bytes 331784 | tf_op jit(solution)/shard_map/ppermute | solution.py:19
  4.8 1.3 %collective-permute-start.1 = (f32[24,9,128]{2,0,1:T(8,128)S(1)}, f32[24,9,128]{2,0,1:T(8,128)S(1)}, u32[]{:S(2)}, u32[]{:S(2)}) collective-permute-start(f32[24,9,128]{2,0,1:T(8,128)S(1)} %get-tuple-element.284), channel_id=1, source_target_pairs={{8,0},{16,8},{24,16},{32,24},{40,32},{48,40},{56,48},{64,56},{72,6... | collective-permute-start | bytes 331784 | tf_op jit(solution)/shard_map/ppermute | solution.py:21
  7.0 0.8 scatter_custom_fusion
  7.7 0.7 all_to_all.9
  8.4 12.8 %all-to-all-start = ((s32[64,1,8]{2,1,0:T(1,128)}), s32[64,1,8]{2,1,0:T(1,128)S(1)}, u32[]{:S(2)}, u32[]{:S(2)}) async-start(s32[64,1,8]{2,1,0:T(1,128)} %bitcast.30), calls=%async_computation | async-start | bytes 65536 | tf_op jit(solution)/shard_map/all_to_all | solution.py:129
  21.4 9.4 %all-to-all-done = s32[64,1,8]{2,1,0:T(1,128)S(1)} async-done(((s32[64,1,8]{2,1,0:T(1,128)}), s32[64,1,8]{2,1,0:T(1,128)S(1)}, u32[]{:S(2)}, u32[]{:S(2)}) %all-to-all-start) | async-done | bytes 2080 | tf_op jit(solution)/shard_map/all_to_all | solution.py:129
  31.3 0.7 reduce.7
  32.8 5.5 %collective-permute-start.2 = (f32[24,50,9]{1,0,2:T(8,128)S(1)}, f32[24,50,9]{1,0,2:T(8,128)S(1)}, u32[]{:S(2)}, u32[]{:S(2)}) collective-permute-start(f32[24,50,9]{1,0,2:T(8,128)S(1)} %copy.56), channel_id=1, source_target_pairs={{0,1},{1,2},{2,3},{3,4},{4,5},{5,6},{6,7},{8,9},{9,10},{10,11},{11... | collective-permute-start | bytes 129608 | tf_op jit(solution)/shard_map/ppermute | solution.py:19
  38.6 1.9 %collective-permute-start.3 = (f32[24,50,9]{1,0,2:T(8,128)S(1)}, f32[24,50,9]{1,0,2:T(8,128)S(1)}, u32[]{:S(2)}, u32[]{:S(2)}) collective-permute-start(f32[24,50,9]{1,0,2:T(8,128)S(1)} %copy.57), channel_id=1, source_target_pairs={{1,0},{2,1},{3,2},{4,3},{5,4},{6,5},{7,6},{9,8},{10,9},{11,10},{12... | collective-permute-start | bytes 129608 | tf_op jit(solution)/shard_map/ppermute | solution.py:21
  40.9 5.5 %collective-permute-done.3 = f32[24,50,9]{1,0,2:T(8,128)S(1)} collective-permute-done((f32[24,50,9]{1,0,2:T(8,128)S(1)}, f32[24,50,9]{1,0,2:T(8,128)S(1)}, u32[]{:S(2)}, u32[]{:S(2)}) %collective-permute-start.3) | collective-permute-done | bytes 43232 | tf_op jit(solution)/shard_map/ppermute | solution.py:21
  47.5 28.6 %while.21 = (s32[]{:T(128)}, f32[4,1,24,8,128]{4,3,2,1,0:T(8,128)S(1)}, s32[4]{0:T(128)S(1)}, f32[2,32,128]{2,1,0:T(8,128)}, s32[2,4,1]{1,2,0:T(1,128)S(1)}, /*i...) while((s32[]{:T(128)}, ...), condition=%wide.region_1.2_spmd, body=%wide.region_0.1_spmd.sunk | while | flops 894995 | bytes 2315025 | solution.py:69
  53.5 0.7 dynamic-slice_bitcast_fusion.2
  60.7 0.7 dynamic-slice_bitcast_fusion.2
  67.8 0.7 dynamic-slice_bitcast_fusion.2
  75.0 0.7 dynamic-slice_bitcast_fusion.2
  76.7 0.9 scatter_custom_fusion.1
  77.6 0.9 reshape.676
  78.4 4.6 %all-to-all-start.1 = ((f32[64,1,192]{2,1,0:T(1,128)}), f32[64,1,192]{2,1,0:T(1,128)S(1)}, u32[]{:S(2)}, u32[]{:S(2)}) async-start(f32[64,1,192]{2,1,0:T(1,128)} %reshape.676), calls=%async_computation.1 | async-start | bytes 131072 | tf_op jit(solution)/shard_map/all_to_all | solution.py:122
  83.1 10.2 %all-to-all-done.1 = f32[64,1,192]{2,1,0:T(1,128)S(1)} async-done(((f32[64,1,192]{2,1,0:T(1,128)}), f32[64,1,192]{2,1,0:T(1,128)S(1)}, u32[]{:S(2)}, u32[]{:S(2)}) %all-to-all-start.1) | async-done | bytes 49184 | tf_op jit(solution)/shard_map/all_to_all | solution.py:122
  93.9 0.8 reduce.8
  94.8 1.7 %scatter_custom_fusion.2 = f32[128,24]{1,0:T(8,128)S(1)} fusion(s32[512]{0:T(512)S(1)} %bitcast.165, f32[64,8,24]{2,1,0:T(8,128)S(1)} %reshape.677, f32[]{:T(128)} %constant.263.clone.1), kind=kCustom, calls=%fused_computation.81 | custom fusion | bytes 274436 | tf_op jit(solution)/shard_map/scatter | solution.py:140
  96.8 0.7 copy-done
  97.5 1.6 %scatter.35 = f32[1,24,32,128]{3,2,1,0:T(8,128)} dynamic-update-slice(f32[1,24,32,128]{3,2,1,0:T(8,128)} %copy-done, f32[1,24,1,128]{3,2,1,0:T(1,128)S(1)} %copy.54, s32[]{:T(128)} %constant.262.clone.1, s32[]{:T(128)} %constant.262.clone.1, s32[]{:T(128)} %constant.279.clone.1, s32[]{:T(128)} %constant.262.clone.1) | dynamic-update-slice | bytes 24580 | tf_op jit(solution)/shard_map/scatter | solution.py:145
  (64 shorter events, 12.2 us)
Async XLA Ops:
  0.0 6.8 %copy-start.2 = (s32[1,1,1,16]{3,2,1,0:T(1,128)S(1)}, s32[1,1,1,16]{3,2,1,0:T(1,128)}, u32[]{:S(2)}) copy-start(s32[1,1,1,16]{3,2,1,0:T(1,128)} %param.18) | copy-start | bytes 196
  0.0 21.3 %copy-start.4 = (s32[1,1,1,16]{3,2,1,0:T(1,128)S(1)}, s32[1,1,1,16]{3,2,1,0:T(1,128)}, u32[]{:S(2)}) copy-start(s32[1,1,1,16]{3,2,1,0:T(1,128)} %param.19) | copy-start | bytes 196
  0.0 21.3 %copy-start.3 = (f32[1,1,1,2,16]{4,3,2,1,0:T(2,128)S(1)}, f32[1,1,1,2,16]{4,3,2,1,0:T(2,128)}, u32[]{:S(2)}) copy-start(f32[1,1,1,2,16]{4,3,2,1,0:T(2,128)} %param.21) | copy-start | bytes 388
  1.3 30.8 %collective-permute-start = (f32[24,9,128]{2,0,1:T(8,128)S(1)}, f32[24,9,128]{2,0,1:T(8,128)S(1)}, u32[]{:S(2)}, u32[]{:S(2)}) collective-permute-start(f32[24,9,128]{2,0,1:T(8,128)S(1)} %get-tuple-element.283), channel_id=1, source_target_pairs={{0,8},{8,16},{16,24},{24,32},{32,40},{40,48},{48,56},{56,64},{64,7... | collective-permute-start | bytes 331784 | tf_op jit(solution)/shard_map/ppermute | solution.py:19
  4.8 27.4 %collective-permute-start.1 = (f32[24,9,128]{2,0,1:T(8,128)S(1)}, f32[24,9,128]{2,0,1:T(8,128)S(1)}, u32[]{:S(2)}, u32[]{:S(2)}) collective-permute-start(f32[24,9,128]{2,0,1:T(8,128)S(1)} %get-tuple-element.284), channel_id=1, source_target_pairs={{8,0},{16,8},{24,16},{32,24},{40,32},{48,40},{56,48},{64,56},{72,6... | collective-permute-start | bytes 331784 | tf_op jit(solution)/shard_map/ppermute | solution.py:21
  8.4 22.4 %all-to-all-start = ((s32[64,1,8]{2,1,0:T(1,128)}), s32[64,1,8]{2,1,0:T(1,128)S(1)}, u32[]{:S(2)}, u32[]{:S(2)}) async-start(s32[64,1,8]{2,1,0:T(1,128)} %bitcast.30), calls=%async_computation | async-start | bytes 65536 | tf_op jit(solution)/shard_map/all_to_all | solution.py:129
  32.8 7.8 %collective-permute-start.2 = (f32[24,50,9]{1,0,2:T(8,128)S(1)}, f32[24,50,9]{1,0,2:T(8,128)S(1)}, u32[]{:S(2)}, u32[]{:S(2)}) collective-permute-start(f32[24,50,9]{1,0,2:T(8,128)S(1)} %copy.56), channel_id=1, source_target_pairs={{0,1},{1,2},{2,3},{3,4},{4,5},{5,6},{6,7},{8,9},{9,10},{10,11},{11... | collective-permute-start | bytes 129608 | tf_op jit(solution)/shard_map/ppermute | solution.py:19
  38.6 7.9 %collective-permute-start.3 = (f32[24,50,9]{1,0,2:T(8,128)S(1)}, f32[24,50,9]{1,0,2:T(8,128)S(1)}, u32[]{:S(2)}, u32[]{:S(2)}) collective-permute-start(f32[24,50,9]{1,0,2:T(8,128)S(1)} %copy.57), channel_id=1, source_target_pairs={{1,0},{2,1},{3,2},{4,3},{5,4},{6,5},{7,6},{9,8},{10,9},{11,10},{12... | collective-permute-start | bytes 129608 | tf_op jit(solution)/shard_map/ppermute | solution.py:21
  46.8 0.7 copy-start.1
  78.4 14.9 %all-to-all-start.1 = ((f32[64,1,192]{2,1,0:T(1,128)}), f32[64,1,192]{2,1,0:T(1,128)S(1)}, u32[]{:S(2)}, u32[]{:S(2)}) async-start(f32[64,1,192]{2,1,0:T(1,128)} %reshape.676), calls=%async_computation.1 | async-start | bytes 131072 | tf_op jit(solution)/shard_map/all_to_all | solution.py:122
  96.8 0.7 copy-start
where the time goes:
time: 99.9 us; the launch traced here: 99.1 us
  starting transfers between devices  29.7 us (30%)
  waiting for transfers between devices  25.2 us (25%)
  local copies, waits for them, and re-layouts  20.2 us (20%)
  loops' own time  18.3 us (18%)
  other arithmetic  4.79 us (5%)
    another operation x1, loops' own time, advect(): tiled = lax.map(one_row, jnp.arange(tiles_lon, dtype=jnp.int32))  18.3 us
    all_to_all x1, starting transfers between devices, body(): lax.all_to_all(send_places.reshape(2 * lon_count, capacity), ('panel', 'l...  12.8 us
    all_to_all x1, waiting for transfers between devices, body(): lax.all_to_all(send_values.reshape(2 * lon_count, capacity, channels), ('...  10.2 us
    all_to_all x1, waiting for transfers between devices, body(): lax.all_to_all(send_places.reshape(2 * lon_count, capacity), ('panel', 'l...  9.42 us
    ppermute x2, starting transfers between devices, with_halo(): lax.ppermute(tail, axis, [(i, (i + 1) % count) for i in range(ends)])  8.98 us
    ppermute x2, waiting for transfers between devices, with_halo(): lax.ppermute(head, axis, [((i + 1) % count, i) for i in range(ends)])  5.51 us
    all_to_all x1, starting transfers between devices, body(): lax.all_to_all(send_values.reshape(2 * lon_count, capacity, channels), ('...  4.62 us
    unnamed x15, local copies, waits for them, and re-layouts  3.74 us
  transfers between devices with their start and end apart: 6, of which 4 were waited for; matrix products, arithmetic and copies ran while one was open for 3% of the time, Pallas kernels for 0%

commit v1 on v0

v1 whole, which is shorter than its diff:
```python
import jax
import jax.numpy as jnp
from jax import lax
from jax.experimental import pallas as pl
from jax.experimental.pallas import tpu as pltpu
from jax.sharding import PartitionSpec as P

TILE = 8
LOW = 8
HIGH = 9
WINDOW = TILE + 3
LANES = 128
PITCH = 16
GROUP = LANES // PITCH
FIELD = 32

VMEM = pl.BlockSpec(memory_space=pltpu.VMEM)
SMEM = pl.BlockSpec(memory_space=pltpu.SMEM)
ANY = pl.BlockSpec(memory_space=pl.ANY)


def lane_iota(shape):
    return lax.broadcasted_iota(jnp.int32, shape, len(shape) - 1)


def pack_kernel(cells_ref, rows_ref, first_ref, last_ref):
    channels, lanes = rows_ref.shape[1:]
    row_count = rows_ref.shape[0]
    lane = lane_iota((channels, lanes))
    for m in range(row_count // GROUP):
        first = last = None
        for s in range(GROUP):
            i = m * GROUP + s
            row = cells_ref[pl.ds(i, channels, stride=row_count), :]
            rows_ref[i] = row
            turned = row if s == 0 else pltpu.roll(row, PITCH * s, 1)
            if s == 0:
                first = last = turned
            else:
                base = PITCH * s
                first = jnp.where((lane >= base) & (lane < base + HIGH), turned, first)
                last = jnp.where((lane >= base - LOW) & (lane < base), turned, last)
        first_ref[m] = first
        last_ref[m] = last


def weight_kernel(fractions_ref, weights_ref):
    for axis in range(2):
        x = fractions_ref[axis]
        weights_ref[4 * axis] = -x * (x - 1.0) * (x - 2.0) / 6.0
        weights_ref[4 * axis + 1] = (x + 1.0) * (x - 1.0) * (x - 2.0) / 2.0
        weights_ref[4 * axis + 2] = -(x + 1.0) * x * (x - 2.0) / 2.0
        weights_ref[4 * axis + 3] = (x + 1.0) * x * (x - 1.0) / 6.0


def edge_kernel(rows_ref, west_ref, east_ref, to_next_ref, to_prev_ref):
    row_count, channels, lanes = rows_ref.shape
    to_next_ref[0:LOW] = rows_ref[row_count - LOW : row_count]
    to_next_ref[LOW] = west_ref[row_count // GROUP - 1]
    to_next_ref[LOW + 1] = east_ref[row_count // GROUP - 1]
    to_prev_ref[0:HIGH] = rows_ref[0:HIGH]
    to_prev_ref[HIGH] = west_ref[0]
    to_prev_ref[HIGH + 1] = east_ref[0]
    lane = lane_iota((channels, lanes))
    to_prev_ref[HIGH + 2] = jnp.where(lane < lanes // 2, east_ref[1], west_ref[1])


def advect_kernel(
    offsets_ref, count_ref, owner_ref, cell_ref, target_ref, frac_ref,
    rows_ref, west_ref, east_ref, prev_ref, next_ref, weights_ref,
    advected_ref, message_ref,
    ext_ref, west_ext_ref, east_ext_ref, shifted_ref,
):
    row_count, channels, lanes = rows_ref.shape
    groups = row_count // GROUP
    ext_ref[0:LOW] = prev_ref[0:LOW]
    ext_ref[LOW : LOW + row_count] = rows_ref[...]
    ext_ref[LOW + row_count : LOW + row_count + HIGH] = next_ref[0:HIGH]
    west_ext_ref[0] = prev_ref[LOW]
    east_ext_ref[0] = prev_ref[LOW + 1]
    west_ext_ref[1 : 1 + groups] = west_ref[...]
    east_ext_ref[1 : 1 + groups] = east_ref[...]
    west_ext_ref[1 + groups] = next_ref[HIGH]
    east_ext_ref[1 + groups] = next_ref[HIGH + 1]
    west_ext_ref[2 + groups] = next_ref[HIGH + 2]
    east_ext_ref[2 + groups] = next_ref[HIGH + 2]

    lane = lane_iota((channels, lanes))
    within = lane & (PITCH - 1)
    for t in range(row_count // TILE):
        offset_lon = offsets_ref[0, 0, t]
        offset_lat = offsets_ref[1, 0, t]
        start = t * TILE + LOW - 1 + offset_lon
        from_east = within < LOW + jnp.where(offset_lat == HIGH - 2, 1, 0)
        for j in range(WINDOW):
            e = start + j
            center = ext_ref[e]
            packed = jnp.where(from_east, east_ext_ref[e >> 3], west_ext_ref[e >> 3])
            halo = pltpu.roll(packed, (LANES - PITCH * (e & 7)) & (LANES - 1), 1)
            for b in range(4):
                shift = offset_lat - 1 + b
                inside = (lane >= shift) & (lane < LANES + shift)
                shifted_ref[t, b, j] = pltpu.roll(
                    jnp.where(inside, center, halo), (LANES - shift) & (LANES - 1), 1
                )
        for i in range(TILE):
            row = t * TILE + i
            lat_weights = [weights_ref[4 + b, row : row + 1, :] for b in range(4)]
            total = None
            for a in range(4):
                inner = lat_weights[0] * shifted_ref[t, 0, i + a]
                for b in range(1, 4):
                    inner = inner + lat_weights[b] * shifted_ref[t, b, i + a]
                part = weights_ref[a, row : row + 1, :] * inner
                total = part if total is None else total + part
            advected_ref[row] = total

    channel = lax.broadcasted_iota(jnp.int32, (channels, lanes), 0)
    one_lane = lane_iota((1, lanes))
    slots = owner_ref.shape[1]
    capacity = slots // 2
    halves = capacity * FIELD // lanes
    per_row = lanes // FIELD
    sums = [jnp.zeros((channels, lanes), jnp.float32) for _ in range(2 * halves)]
    empty = jnp.where((one_lane & (FIELD - 1)) == channels, jnp.float32(lanes), jnp.float32(0.0))
    places = [empty for _ in range(2 * halves)]
    taken = [jnp.int32(0), jnp.int32(0)]
    for k in range(slots):
        cell = cell_ref[0, k]
        r, c = cell >> 7, cell & (lanes - 1)
        a, b = frac_ref[0, k], frac_ref[1, k]
        near = jnp.where(one_lane == c, 1.0 - b, jnp.where(one_lane == c + 1, b, 0.0))
        value = jnp.sum(
            advected_ref[r] * ((1.0 - a) * near) + advected_ref[r + 1] * (a * near),
            axis=1,
            keepdims=True,
        )
        live = k < count_ref[0, 0]
        side = (owner_ref[0, k] != 0).astype(jnp.int32)
        target = target_ref[0, k].astype(jnp.float32)
        position = jnp.where(side == 0, taken[0], taken[1])
        taken[0] = taken[0] + jnp.where(live & (side == 0), 1, 0)
        taken[1] = taken[1] + jnp.where(live & (side == 1), 1, 0)
        base = (position % per_row) * FIELD
        here = jnp.where(live, side * halves + position // per_row, -1)
        at_value = lane - channel
        for h in range(2 * halves):
            lane_base = jnp.where(here == h, base, -lanes)
            sums[h] = jnp.where(at_value == lane_base, value, sums[h])
            places[h] = jnp.where(one_lane == lane_base + channels, target, places[h])
    lon_count = message_ref.shape[0] // 2
    other = (1 - lax.axis_index("panel")) * lon_count
    message_ref[...] = jnp.zeros_like(message_ref)
    for side in range(2):
        parts = []
        for h in range(halves):
            n = side * halves + h
            parts.append(jnp.sum(sums[n], axis=0, keepdims=True) + places[n])
        message_ref[other + side * (lon_count - 1)] = jnp.concatenate(parts, axis=1)


def column_kernel(advected_ref, out_ref):
    row_count, channels, _ = advected_ref.shape
    for i in range(row_count):
        out_ref[pl.ds(i, channels, stride=row_count), :] = advected_ref[i]


def rim_kernel(received_ref, given_ref, out_ref, rim_ref, sem):
    del given_ref
    channels, row_count, lanes = out_ref.shape
    lon = lax.axis_index("lon")
    lon_count = lax.axis_size("lon")

    @pl.when((lon == 0) | (lon == lon_count - 1))
    def _():
        other = (1 - lax.axis_index("panel")) * lon_count
        values = received_ref[pl.ds(other, lon_count)].reshape(lon_count, received_ref.shape[2])
        lane = lane_iota((lon_count, lanes))
        rim = jnp.zeros((FIELD, lanes), jnp.float32)
        for q in range(received_ref.shape[2] // FIELD):
            entry = values[:, q * FIELD : (q + 1) * FIELD]
            place = entry[:, channels : channels + 1].astype(jnp.int32)
            rim = rim + lax.dot_general(
                entry,
                jnp.where(lane == place, 1.0, 0.0),
                (((0,), (0,)), ((), ())),
                precision=lax.Precision.HIGHEST,
                preferred_element_type=jnp.float32,
            )
        rim_ref[...] = rim[0:channels].reshape(channels, 1, lanes)

        @pl.when(lon == 0)
        def _():
            copy = pltpu.make_async_copy(rim_ref, out_ref.at[:, pl.ds(0, 1), :], sem)
            copy.start()
            copy.wait()

        @pl.when(lon == lon_count - 1)
        def _():
            copy = pltpu.make_async_copy(rim_ref, out_ref.at[:, pl.ds(row_count - 1, 1), :], sem)
            copy.start()
            copy.wait()


def f32(*shape):
    return jax.ShapeDtypeStruct(shape, jnp.float32)


def up(array, axis):
    count = lax.axis_size(axis)
    return lax.ppermute(array, axis, [(i, i + 1) for i in range(count - 1)])


def down(array, axis):
    count = lax.axis_size(axis)
    return lax.ppermute(array, axis, [(i + 1, i) for i in range(count - 1)])


def body(fields, offsets, fractions, send_count, send_owner, send_cell, send_target, send_frac):
    _, channels, row_count, lanes = fields.shape
    groups = row_count // GROUP
    lon_count = lax.axis_size("lon")
    slots = send_owner.shape[-1]
    width = slots // 2 * FIELD
    ext = LOW + row_count + HIGH

    rows, first, last = pl.pallas_call(
        pack_kernel,
        out_shape=(
            f32(row_count, channels, lanes),
            f32(groups, channels, lanes),
            f32(groups, channels, lanes),
        ),
        in_specs=[VMEM],
        out_specs=(VMEM, VMEM, VMEM),
        name="pack",
    )(fields.reshape(channels * row_count, lanes))
    west = up(last, "lat")
    east = down(first, "lat")
    weights = pl.pallas_call(
        weight_kernel,
        out_shape=f32(8, row_count, lanes),
        in_specs=[VMEM],
        out_specs=VMEM,
        cost_estimate=pl.CostEstimate(flops=200000, bytes_accessed=200000, transcendentals=0),
        name="weights",
    )(fractions[0])
    to_next, to_prev = pl.pallas_call(
        edge_kernel,
        out_shape=(f32(LOW + 2, channels, lanes), f32(HIGH + 3, channels, lanes)),
        in_specs=[VMEM] * 3,
        out_specs=(VMEM, VMEM),
        name="edges",
    )(rows, west, east)
    from_prev = up(to_next, "lon")
    from_next = down(to_prev, "lon")
    advected, message = pl.pallas_call(
        advect_kernel,
        out_shape=(f32(row_count, channels, lanes), f32(2 * lon_count, 1, width)),
        in_specs=[SMEM] * 6 + [VMEM] * 6,
        out_specs=(VMEM, VMEM),
        scratch_shapes=[
            pltpu.VMEM((ext, channels, lanes), jnp.float32),
            pltpu.VMEM((groups + 3, channels, lanes), jnp.float32),
            pltpu.VMEM((groups + 3, channels, lanes), jnp.float32),
            pltpu.VMEM((row_count // TILE, 4, WINDOW, channels, lanes), jnp.float32),
        ],
        compiler_params=pltpu.CompilerParams(vmem_limit_bytes=24 * 1024 * 1024),
        name="advect",
    )(
        offsets[0].transpose(0, 2, 1),
        send_count[0],
        send_owner[0, 0],
        send_cell[0, 0],
        send_target[0, 0],
        send_frac[0, 0, 0],
        rows,
        west,
        east,
        from_prev,
        from_next,
        weights,
    )
    received = lax.all_to_all(message, ("panel", "lon"), split_axis=0, concat_axis=0, tiled=True)
    columns = pl.pallas_call(
        column_kernel,
        out_shape=f32(channels * row_count, lanes),
        in_specs=[VMEM],
        out_specs=VMEM,
        cost_estimate=pl.CostEstimate(flops=0, bytes_accessed=2000000, transcendentals=0),
        name="columns",
    )(advected)
    out = pl.pallas_call(
        rim_kernel,
        out_shape=f32(channels, row_count, lanes),
        in_specs=[VMEM, ANY],
        out_specs=ANY,
        scratch_shapes=[
            pltpu.VMEM((channels, 1, lanes), jnp.float32),
            pltpu.SemaphoreType.DMA(()),
        ],
        input_output_aliases={1: 0},
        name="rim",
    )(received, columns.reshape(channels, row_count, lanes))
    return out[None]


def solution(mesh):
    placed = (
        P("panel", None, "lon", "lat"),
        P("panel", None, "lon", "lat"),
        P("panel", None, "lon", "lat"),
        P("panel", "lon", "lat"),
        P("panel", "lon", "lat", None),
        P("panel", "lon", "lat", None),
        P("panel", "lon", "lat", None),
        P("panel", "lon", "lat", None, None),
    )
    return jax.shard_map(
        body, mesh=mesh, in_specs=placed, out_specs=P("panel", None, "lon", "lat"), check_vma=False
    )
```

time: 99.9 us -> 59.3 us (0.59)
  loops' own time: 18.3 us -> 0 us
  local copies, waits for them, and re-layouts: 20.2 us -> 3.54 us
  Pallas kernels: 0 us -> 14.4 us
  waiting for transfers between devices: 25.2 us -> 14.2 us
  other arithmetic: 4.79 us -> 0 us
  starting transfers between devices: 29.7 us -> 25.9 us
    another operation x1 -> x0, loops' own time: 18.3 us -> none  [advect(): tiled = lax.map(one_row, jnp.arange(tiles_lon, dtype=jnp.int32))]
    pallas_call x0 -> x6, Pallas kernels: none -> 14.4 us  [the longest x1 4.58 us: body(): pl.pallas_call(advect_kernel, out_shape=(f32(row_count, channels, lanes),...]
    all_to_all x2 -> x1, waiting for transfers between devices: 19.6 us -> 8.17 us  [body(): lax.all_to_all(message, ('panel', 'lon'), split_axis=0, concat_axis=0, ti...]
    all_to_all x2 -> x1, starting transfers between devices: 17.5 us -> 12.5 us  [body(): lax.all_to_all(message, ('panel', 'lon'), split_axis=0, concat_axis=0, ti...]
    scatter x4 -> x0, local copies, waits for them, and re-layouts: 4.15 us -> none  [the longest x1 1.74 us: body(): jnp.zeros((col_count, channels), jnp.float32).at[recv_target]]
    while x12 -> x0, local copies, waits for them, and re-layouts: 3.59 us -> none  [the longest x4 2.63 us: one_tile(): start_lat = u * BLOCK + halo_width + offsets[1, t, u] - 1]
    gather x4 -> x0, local copies, waits for them, and re-layouts: 2.81 us -> none  [one_tile(): lax.dynamic_slice(fractions, (jnp.int32(0), t * TILE, u * BLOCK), (2, TIL...]
    dynamic_slice x4 -> x0, local copies, waits for them, and re-layouts: 2.34 us -> none  [advect(): tiled = lax.map(one_row, jnp.arange(tiles_lon, dtype=jnp.int32))]
  transfers between devices with their start and end apart: 6 -> 5, of which waited for: 4 -> 4; matrix products, arithmetic and copies ran while one was open for 3% -> 0% of each run, Pallas kernels for 0% -> 6%
where the time goes in v1:
time: 59.3 us; the launch traced here: 58.8 us
  starting transfers between devices  25.9 us (44%)
  Pallas kernels  14.4 us (24%)
  waiting for transfers between devices  14.2 us (24%)
  local copies, waits for them, and re-layouts  3.54 us (6%)
  between operations  0.81 us (1%)
    all_to_all x1, starting transfers between devices, body(): lax.all_to_all(message, ('panel', 'lon'), split_axis=0, concat_axis=0, ti...  12.5 us
    ppermute x2, starting transfers between devices, up(): return lax.ppermute(array, axis, [(i, i + 1) for i in range(count - 1)])  10.2 us
    all_to_all x1, waiting for transfers between devices, body(): lax.all_to_all(message, ('panel', 'lon'), split_axis=0, concat_axis=0, ti...  8.17 us
    ppermute x2, waiting for transfers between devices, down(): return lax.ppermute(array, axis, [(i + 1, i) for i in range(count - 1)])  5.36 us
    pallas_call x1, Pallas kernels, body(): pl.pallas_call(advect_kernel, out_shape=(f32(row_count, channels, lanes),...  4.58 us
    unnamed x26, local copies, waits for them, and re-layouts  3.54 us
    ppermute x2, starting transfers between devices, down(): return lax.ppermute(array, axis, [(i + 1, i) for i in range(count - 1)])  3.2 us
    pallas_call x1, Pallas kernels, body(): pl.pallas_call(rim_kernel, out_shape=f32(channels, row_count, lanes), in_...  2.51 us
  transfers between devices with their start and end apart: 5, of which 4 were waited for; matrix products, arithmetic and copies ran while one was open for 0% of the time, Pallas kernels for 6%

profile of v1, /device:TPU:192, one launch (start us, length us, event | category | flops | bytes accessed | tf_op | source)
XLA Modules:
  0.0 58.8 jit_solution(4134074025082765141)
XLA Ops:
  0.0 2.0 %pack.1 = (f32[32,24,128]{2,1,0:T(8,128)}, f32[4,24,128]{2,1,0:T(8,128)}, f32[4,24,128]{2,1,0:T(8,128)}) custom-call(f32[768,128]{1,0:T(8,128)} %bitcast.19), custom_call_target="tpu_custom_call" | custom-call | tf_op jit(solution)/shard_map/pack/pallas_call | solution.py:227
  2.0 5.6 %collective-permute-start = (f32[4,24,128]{2,1,0:T(8,128)}, f32[4,24,128]{2,1,0:T(8,128)S(1)}, u32[]{:S(2)}, u32[]{:S(2)}) collective-permute-start(f32[4,24,128]{2,1,0:T(8,128)} %get-tuple-element.13), channel_id=1, source_target_pairs={{0,1},{1,2},{2,3},{3,4},{4,5},{5,6},{6,7},{8,9},{9,10},{10,11},{11... | collective-permute-start | bytes 147464 | tf_op jit(solution)/shard_map/ppermute | solution.py:211
  7.6 1.9 %collective-permute-start.1 = (f32[4,24,128]{2,1,0:T(8,128)}, f32[4,24,128]{2,1,0:T(8,128)S(1)}, u32[]{:S(2)}, u32[]{:S(2)}) collective-permute-start(f32[4,24,128]{2,1,0:T(8,128)} %get-tuple-element.14), channel_id=1, source_target_pairs={{1,0},{2,1},{3,2},{4,3},{5,4},{6,5},{7,6},{9,8},{10,9},{11,10},{12... | collective-permute-start | bytes 147464 | tf_op jit(solution)/shard_map/ppermute | solution.py:216
  9.5 0.1 collective-permute-done.west_ref
  9.7 5.4 %collective-permute-done.1.east_ref = f32[4,24,128]{2,1,0:T(8,128)S(1)} collective-permute-done((f32[4,24,128]{2,1,0:T(8,128)}, f32[4,24,128]{2,1,0:T(8,128)S(1)}, u32[]{:S(2)}, u32[]{:S(2)}) %collective-permute-start.1) | collective-permute-done | bytes 49184 | tf_op jit(solution)/shard_map/ppermute | solution.py:216
  15.0 0.0 copy-done.3
  15.0 0.6 %copy-done.5 = f32[4,24,128]{2,1,0:T(8,128)} copy-done((f32[4,24,128]{2,1,0:T(8,128)}, f32[4,24,128]{2,1,0:T(8,128)S(1)}, u32[]{:S(2)}) %copy-start.5) | copy-done | bytes 49176
  15.6 1.7 %edges.1 = (f32[10,24,128]{2,1,0:T(8,128)}, f32[12,24,128]{2,1,0:T(8,128)}) custom-call(f32[32,24,128]{2,1,0:T(8,128)} %get-tuple-element.12.rows_ref, f32[4,24,128]{2,1,0:T(8,128)} %copy-done.3, f32[4,24,128]{2,1,0:T(8,128)} %copy-done.5), custom_call_target="tpu_custom_call" | custom-call | tf_op jit(solution)/shard_map/edges/pallas_call | solution.py:248
  17.4 1.3 %collective-permute-start.3 = (f32[12,24,128]{2,1,0:T(8,128)}, f32[12,24,128]{2,1,0:T(8,128)S(1)}, u32[]{:S(2)}, u32[]{:S(2)}) collective-permute-start(f32[12,24,128]{2,1,0:T(8,128)} %get-tuple-element.16), channel_id=1, source_target_pairs={{8,0},{16,8},{24,16},{32,24},{40,32},{48,40},{56,48},{64,56},{72,6... | collective-permute-start | bytes 442376 | tf_op jit(solution)/shard_map/ppermute | solution.py:216
  18.7 4.6 %collective-permute-start.2 = (f32[10,24,128]{2,1,0:T(8,128)}, f32[10,24,128]{2,1,0:T(8,128)S(1)}, u32[]{:S(2)}, u32[]{:S(2)}) collective-permute-start(f32[10,24,128]{2,1,0:T(8,128)} %get-tuple-element.15), channel_id=1, source_target_pairs={{0,8},{8,16},{16,24},{24,32},{32,40},{40,48},{48,56},{56,64},{64,7... | collective-permute-start | bytes 368648 | tf_op jit(solution)/shard_map/ppermute | solution.py:211
  23.2 0.0 copy-start.4
  23.2 1.5 %weights.1.weights_ref = f32[8,32,128]{2,1,0:T(8,128)} custom-call(f32[2,32,128]{2,1,0:T(8,128)} %bitcast.20), custom_call_target="tpu_custom_call" | custom-call | flops 200000 | bytes 200000 | tf_op jit(solution)/shard_map/weights/pallas_call | solution.py:240
  25.4 0.6 collective-permute-done.2.prev_ref
  26.0 0.0 collective-permute-done.3.next_ref
  26.0 0.0 copy-done
  26.0 0.6 %copy-done.7 = s32[1,2,4,1]{2,3,1,0:T(1,128)S(1)} copy-done((s32[1,2,4,1]{2,3,1,0:T(1,128)S(1)}, s32[1,2,4,1]{2,3,1,0:T(1,128)}, u32[]{:S(2)}) %copy-start.7) | copy-done | bytes 56
  26.6 0.9 %copy-done.1 = f32[8,32,128]{2,1,0:T(8,128)S(1)} copy-done((f32[8,32,128]{2,1,0:T(8,128)S(1)}, f32[8,32,128]{2,1,0:T(8,128)}, u32[]{:S(2)}) %copy-start.1) | copy-done | bytes 131096
  27.6 4.6 %advect.1 = (f32[32,24,128]{2,1,0:T(8,128)S(1)}, f32[64,1,256]{2,1,0:T(1,128)}) custom-call(s32[2,1,4]{2,1,0:T(1,128)S(1)} %bitcast.13, s32[1,1]{1,0:T(1,128)} %bitcast.12.count_ref, s32[1,16]{1,0:T(1,128)S(1)} %bitcast.15, s32[1,16]{1,0:T(1,128)S(1)} %bitcast.16, s32[1,16]{1,0:T(1,128)S(1)} %bitcast.17, f32[2,16]{1,0:T(2,128)S(1)} %bitcast.14, ...), custom_call_target="tpu_custom_call" | custom-call | tf_op jit(solution)/shard_map/advect/pallas_call | solution.py:257
  32.1 0.7 %copy-done.2 = f32[32,24,128]{2,1,0:T(8,128)} copy-done((f32[32,24,128]{2,1,0:T(8,128)}, f32[32,24,128]{2,1,0:T(8,128)S(1)}, u32[]{:S(2)}) %copy-start.2) | copy-done | bytes 393240
  32.9 12.5 %all-to-all-start = ((f32[64,1,256]{2,1,0:T(1,128)}), f32[64,1,256]{2,1,0:T(1,128)S(1)}, u32[]{:S(2)}, u32[]{:S(2)}) async-start(f32[64,1,256]{2,1,0:T(1,128)} %get-tuple-element.17), calls=%async_computation | async-start | bytes 131072 | tf_op jit(solution)/shard_map/all_to_all | solution.py:284
  45.4 2.1 %columns.1 = f32[768,128]{1,0:T(8,128)} custom-call(f32[32,24,128]{2,1,0:T(8,128)} %copy-done.2), custom_call_target="tpu_custom_call" | custom-call | bytes 2000000 | tf_op jit(solution)/shard_map/columns/pallas_call | solution.py:285
  47.5 8.2 %all-to-all-done.received_ref = f32[64,1,256]{2,1,0:T(1,128)S(1)} async-done(((f32[64,1,256]{2,1,0:T(1,128)}), f32[64,1,256]{2,1,0:T(1,128)S(1)}, u32[]{:S(2)}, u32[]{:S(2)}) %all-to-all-start) | async-done | bytes 65568 | tf_op jit(solution)/shard_map/all_to_all | solution.py:284
  55.7 0.6 %copy-done.12 = f32[64,1,256]{2,1,0:T(1,128)} copy-done((f32[64,1,256]{2,1,0:T(1,128)}, f32[64,1,256]{2,1,0:T(1,128)S(1)}, u32[]{:S(2)}) %copy-start.12) | copy-done | bytes 65560
  56.3 2.5 %rim.1 = f32[24,32,128]{2,1,0:T(8,128)} custom-call(f32[64,1,256]{2,1,0:T(1,128)} %copy-done.12, f32[24,32,128]{2,1,0:T(8,128)} %bitcast.18), custom_call_target="tpu_custom_call", output_to_operand_aliasing={{}: (1, {})} | custom-call | tf_op jit(solution)/shard_map/rim/pallas_call | solution.py:293
  (18 shorter events, 0.0 us)
Async XLA Ops:
  2.0 24.0 %copy-start = (f32[32,24,128]{2,1,0:T(8,128)S(1)}, f32[32,24,128]{2,1,0:T(8,128)}, u32[]{:S(2)}) copy-start(f32[32,24,128]{2,1,0:T(8,128)} %get-tuple-element.12.rows_ref) | copy-start | bytes 1179652
  2.0 7.7 %collective-permute-start = (f32[4,24,128]{2,1,0:T(8,128)}, f32[4,24,128]{2,1,0:T(8,128)S(1)}, u32[]{:S(2)}, u32[]{:S(2)}) collective-permute-start(f32[4,24,128]{2,1,0:T(8,128)} %get-tuple-element.13), channel_id=1, source_target_pairs={{0,1},{1,2},{2,3},{3,4},{4,5},{5,6},{6,7},{8,9},{9,10},{10,11},{11... | collective-permute-start | bytes 147464 | tf_op jit(solution)/shard_map/ppermute | solution.py:211
  7.6 7.4 %collective-permute-start.1 = (f32[4,24,128]{2,1,0:T(8,128)}, f32[4,24,128]{2,1,0:T(8,128)S(1)}, u32[]{:S(2)}, u32[]{:S(2)}) collective-permute-start(f32[4,24,128]{2,1,0:T(8,128)} %get-tuple-element.14), channel_id=1, source_target_pairs={{1,0},{2,1},{3,2},{4,3},{5,4},{6,5},{7,6},{9,8},{10,9},{11,10},{12... | collective-permute-start | bytes 147464 | tf_op jit(solution)/shard_map/ppermute | solution.py:216
  9.7 5.4 %copy-start.3 = (f32[4,24,128]{2,1,0:T(8,128)}, f32[4,24,128]{2,1,0:T(8,128)S(1)}, u32[]{:S(2)}) copy-start(f32[4,24,128]{2,1,0:T(8,128)S(1)} %collective-permute-done.west_ref) | copy-start | bytes 147460
  15.0 0.6 %copy-start.5 = (f32[4,24,128]{2,1,0:T(8,128)}, f32[4,24,128]{2,1,0:T(8,128)S(1)}, u32[]{:S(2)}) copy-start(f32[4,24,128]{2,1,0:T(8,128)S(1)} %collective-permute-done.1.east_ref) | copy-start | bytes 147460
  17.4 8.6 %collective-permute-start.3 = (f32[12,24,128]{2,1,0:T(8,128)}, f32[12,24,128]{2,1,0:T(8,128)S(1)}, u32[]{:S(2)}, u32[]{:S(2)}) collective-permute-start(f32[12,24,128]{2,1,0:T(8,128)} %get-tuple-element.16), channel_id=1, source_target_pairs={{8,0},{16,8},{24,16},{32,24},{40,32},{48,40},{56,48},{64,56},{72,6... | collective-permute-start | bytes 442376 | tf_op jit(solution)/shard_map/ppermute | solution.py:216
  18.7 7.3 %collective-permute-start.2 = (f32[10,24,128]{2,1,0:T(8,128)}, f32[10,24,128]{2,1,0:T(8,128)S(1)}, u32[]{:S(2)}, u32[]{:S(2)}) collective-permute-start(f32[10,24,128]{2,1,0:T(8,128)} %get-tuple-element.15), channel_id=1, source_target_pairs={{0,8},{8,16},{16,24},{24,32},{32,40},{40,48},{48,56},{56,64},{64,7... | collective-permute-start | bytes 368648 | tf_op jit(solution)/shard_map/ppermute | solution.py:211
  23.2 2.8 %copy-start.4 = (f32[4,24,128]{2,1,0:T(8,128)S(1)}, f32[4,24,128]{2,1,0:T(8,128)}, u32[]{:S(2)}) copy-start(f32[4,24,128]{2,1,0:T(8,128)} %copy-done.3) | copy-start | bytes 147460
  23.2 2.8 %copy-start.6 = (f32[4,24,128]{2,1,0:T(8,128)S(1)}, f32[4,24,128]{2,1,0:T(8,128)}, u32[]{:S(2)}) copy-start(f32[4,24,128]{2,1,0:T(8,128)} %copy-done.5) | copy-start | bytes 147460
  24.7 1.3 %copy-start.8 = (f32[1,1,1,2,16]{4,3,2,1,0:T(2,128)S(1)}, f32[1,1,1,2,16]{4,3,2,1,0:T(2,128)}, u32[]{:S(2)}) copy-start(f32[1,1,1,2,16]{4,3,2,1,0:T(2,128)} %param.15) | copy-start | bytes 388
  24.7 1.3 %copy-start.10 = (s32[1,1,1,16]{3,2,1,0:T(1,128)S(1)}, s32[1,1,1,16]{3,2,1,0:T(1,128)}, u32[]{:S(2)}) copy-start(s32[1,1,1,16]{3,2,1,0:T(1,128)} %param.13) | copy-start | bytes 196
  24.7 1.3 %copy-start.11 = (s32[1,1,1,16]{3,2,1,0:T(1,128)S(1)}, s32[1,1,1,16]{3,2,1,0:T(1,128)}, u32[]{:S(2)}) copy-start(s32[1,1,1,16]{3,2,1,0:T(1,128)} %param.14) | copy-start | bytes 196
  26.0 0.7 %copy-start.7 = (s32[1,2,4,1]{2,3,1,0:T(1,128)S(1)}, s32[1,2,4,1]{2,3,1,0:T(1,128)}, u32[]{:S(2)}) copy-start(s32[1,2,4,1]{2,3,1,0:T(1,128)} %param.9) | copy-start | bytes 100
  26.0 0.7 %copy-start.9 = (s32[1,1,1,16]{3,2,1,0:T(1,128)S(1)}, s32[1,1,1,16]{3,2,1,0:T(1,128)}, u32[]{:S(2)}) copy-start(s32[1,1,1,16]{3,2,1,0:T(1,128)} %param.12) | copy-start | bytes 196
  26.6 0.9 %copy-start.1 = (f32[8,32,128]{2,1,0:T(8,128)S(1)}, f32[8,32,128]{2,1,0:T(8,128)}, u32[]{:S(2)}) copy-start(f32[8,32,128]{2,1,0:T(8,128)} %weights.1.weights_ref) | copy-start | bytes 393220
  32.1 0.8 %copy-start.2 = (f32[32,24,128]{2,1,0:T(8,128)}, f32[32,24,128]{2,1,0:T(8,128)S(1)}, u32[]{:S(2)}) copy-start(f32[32,24,128]{2,1,0:T(8,128)S(1)} %get-tuple-element.18.advected_ref) | copy-start | bytes 1179652
  32.9 22.8 %all-to-all-start = ((f32[64,1,256]{2,1,0:T(1,128)}), f32[64,1,256]{2,1,0:T(1,128)S(1)}, u32[]{:S(2)}, u32[]{:S(2)}) async-start(f32[64,1,256]{2,1,0:T(1,128)} %get-tuple-element.17), calls=%async_computation | async-start | bytes 131072 | tf_op jit(solution)/shard_map/all_to_all | solution.py:284
  55.7 0.6 %copy-start.12 = (f32[64,1,256]{2,1,0:T(1,128)}, f32[64,1,256]{2,1,0:T(1,128)S(1)}, u32[]{:S(2)}) copy-start(f32[64,1,256]{2,1,0:T(1,128)S(1)} %all-to-all-done.received_ref) | copy-start | bytes 196612

commit v2 on v1

--- a/solution.py
+++ b/solution.py
@@ -233,6 +233,7 @@
         ),
         in_specs=[VMEM],
         out_specs=(VMEM, VMEM, VMEM),
+        compiler_params=pltpu.CompilerParams(vmem_limit_bytes=4 * 1024 * 1024),
         name="pack",
     )(fields.reshape(channels * row_count, lanes))
     west = up(last, "lat")
@@ -243,6 +244,7 @@
         in_specs=[VMEM],
         out_specs=VMEM,
         cost_estimate=pl.CostEstimate(flops=200000, bytes_accessed=200000, transcendentals=0),
+        compiler_params=pltpu.CompilerParams(vmem_limit_bytes=2 * 1024 * 1024),
         name="weights",
     )(fractions[0])
     to_next, to_prev = pl.pallas_call(
@@ -250,6 +252,7 @@
         out_shape=(f32(LOW + 2, channels, lanes), f32(HIGH + 3, channels, lanes)),
         in_specs=[VMEM] * 3,
         out_specs=(VMEM, VMEM),
+        compiler_params=pltpu.CompilerParams(vmem_limit_bytes=2 * 1024 * 1024),
         name="edges",
     )(rows, west, east)
     from_prev = up(to_next, "lon")
@@ -265,7 +268,7 @@
             pltpu.VMEM((groups + 3, channels, lanes), jnp.float32),
             pltpu.VMEM((row_count // TILE, 4, WINDOW, channels, lanes), jnp.float32),
         ],
-        compiler_params=pltpu.CompilerParams(vmem_limit_bytes=24 * 1024 * 1024),
+        compiler_params=pltpu.CompilerParams(vmem_limit_bytes=8 * 1024 * 1024),
         name="advect",
     )(
         offsets[0].transpose(0, 2, 1),
@@ -288,6 +291,7 @@
         in_specs=[VMEM],
         out_specs=VMEM,
         cost_estimate=pl.CostEstimate(flops=0, bytes_accessed=2000000, transcendentals=0),
+        compiler_params=pltpu.CompilerParams(vmem_limit_bytes=2 * 1024 * 1024),
         name="columns",
     )(advected)
     out = pl.pallas_call(
@@ -300,6 +304,7 @@
             pltpu.SemaphoreType.DMA(()),
         ],
         input_output_aliases={1: 0},
+        compiler_params=pltpu.CompilerParams(vmem_limit_bytes=2 * 1024 * 1024),
         name="rim",
     )(received, columns.reshape(channels, row_count, lanes))
     return out[None]

time: 59.3 us -> 52.5 us (0.89)
  Pallas kernels: 14.4 us -> 7.68 us
  waiting for transfers between devices: 14.2 us -> 16.1 us
  local copies, waits for them, and re-layouts: 3.54 us -> 1.67 us
    unnamed x26 -> x14, local copies, waits for them, and re-layouts: 3.54 us -> 1.67 us
    pallas_call x1, Pallas kernels: 2 us -> 0.27 us  [body(): pl.pallas_call(pack_kernel, out_shape=(f32(row_count, channels, lanes), f...]
    pallas_call x1, Pallas kernels: 1.74 us -> 0.02 us  [body(): pl.pallas_call(edge_kernel, out_shape=(f32(LOW + 2, channels, lanes), f32...]
    pallas_call x1, Pallas kernels: 1.45 us -> 0.02 us  [body(): pl.pallas_call(weight_kernel, out_shape=f32(8, row_count, lanes), in_spec...]
    ppermute x2, waiting for transfers between devices: 0.68 us -> 1.68 us  [up(): return lax.ppermute(array, axis, [(i, i + 1) for i in range(count - 1)])]
    all_to_all x1, waiting for transfers between devices: 8.17 us -> 9.17 us  [body(): lax.all_to_all(message, ('panel', 'lon'), split_axis=0, concat_axis=0, ti...]
    pallas_call x1, Pallas kernels: 2.1 us -> 1.1 us  [body(): pl.pallas_call(column_kernel, out_shape=f32(channels * row_count, lanes),...]
    pallas_call x1, Pallas kernels: 2.51 us -> 1.68 us  [body(): pl.pallas_call(rim_kernel, out_shape=f32(channels, row_count, lanes), in_...]
  transfers between devices with their start and end apart: 5 -> 5, of which waited for: 4 -> 3; matrix products, arithmetic and copies ran while one was open for 0% -> 0% of each run, Pallas kernels for 6% -> 2%
where the time goes in v2:
time: 52.5 us; the launch traced here: 52.1 us
  starting transfers between devices  25.9 us (49%)
  waiting for transfers between devices  16.1 us (31%)
  Pallas kernels  7.68 us (15%)
  local copies, waits for them, and re-layouts  1.67 us (3%)
  between operations  0.79 us (2%)
    all_to_all x1, starting transfers between devices, body(): lax.all_to_all(message, ('panel', 'lon'), split_axis=0, concat_axis=0, ti...  12.6 us
    ppermute x2, starting transfers between devices, up(): return lax.ppermute(array, axis, [(i, i + 1) for i in range(count - 1)])  10 us
    all_to_all x1, waiting for transfers between devices, body(): lax.all_to_all(message, ('panel', 'lon'), split_axis=0, concat_axis=0, ti...  9.17 us
    ppermute x2, waiting for transfers between devices, down(): return lax.ppermute(array, axis, [(i + 1, i) for i in range(count - 1)])  5.26 us
    pallas_call x1, Pallas kernels, body(): pl.pallas_call(advect_kernel, out_shape=(f32(row_count, channels, lanes),...  4.59 us
    ppermute x2, starting transfers between devices, down(): return lax.ppermute(array, axis, [(i + 1, i) for i in range(count - 1)])  3.21 us
    ppermute x2, waiting for transfers between devices, up(): return lax.ppermute(array, axis, [(i, i + 1) for i in range(count - 1)])  1.68 us
    pallas_call x1, Pallas kernels, body(): pl.pallas_call(rim_kernel, out_shape=f32(channels, row_count, lanes), in_...  1.68 us
  transfers between devices with their start and end apart: 5, of which 3 were waited for; matrix products, arithmetic and copies ran while one was open for 0% of the time, Pallas kernels for 2%

profile of v2, /device:TPU:192, one launch (start us, length us, event | category | flops | bytes accessed | tf_op | source)
XLA Modules:
  0.0 52.1 jit_solution(18137727688775914596)
XLA Ops:
  0.0 1.0 %copy-done = f32[1,24,32,128]{3,2,1,0:T(8,128)S(1)} copy-done((f32[1,24,32,128]{3,2,1,0:T(8,128)S(1)}, f32[1,24,32,128]{3,2,1,0:T(8,128)}, u32[]{:S(2)}) %copy-start) | copy-done | bytes 393240
  1.0 0.3 pack.1
  1.3 5.5 %collective-permute-start = (f32[4,24,128]{2,1,0:T(8,128)S(1)}, f32[4,24,128]{2,1,0:T(8,128)S(1)}, u32[]{:S(2)}, u32[]{:S(2)}) collective-permute-start(f32[4,24,128]{2,1,0:T(8,128)S(1)} %get-tuple-element.13), channel_id=1, source_target_pairs={{0,1},{1,2},{2,3},{3,4},{4,5},{5,6},{6,7},{8,9},{9,10},{10,11},{11... | collective-permute-start | bytes 147464 | tf_op jit(solution)/shard_map/ppermute | solution.py:211
  6.8 1.9 %collective-permute-start.1 = (f32[4,24,128]{2,1,0:T(8,128)S(1)}, f32[4,24,128]{2,1,0:T(8,128)S(1)}, u32[]{:S(2)}, u32[]{:S(2)}) collective-permute-start(f32[4,24,128]{2,1,0:T(8,128)S(1)} %get-tuple-element.14), channel_id=1, source_target_pairs={{1,0},{2,1},{3,2},{4,3},{5,4},{6,5},{7,6},{9,8},{10,9},{11,10},{12... | collective-permute-start | bytes 147464 | tf_op jit(solution)/shard_map/ppermute | solution.py:216
  8.7 0.0 collective-permute-done.west_ref
  8.7 5.3 %collective-permute-done.1.east_ref = f32[4,24,128]{2,1,0:T(8,128)S(1)} collective-permute-done((f32[4,24,128]{2,1,0:T(8,128)S(1)}, f32[4,24,128]{2,1,0:T(8,128)S(1)}, u32[]{:S(2)}, u32[]{:S(2)}) %collective-permute-start.1) | collective-permute-done | bytes 49184 | tf_op jit(solution)/shard_map/ppermute | solution.py:216
  14.0 1.3 %collective-permute-start.3 = (f32[12,24,128]{2,1,0:T(8,128)S(1)}, f32[12,24,128]{2,1,0:T(8,128)S(1)}, u32[]{:S(2)}, u32[]{:S(2)}) collective-permute-start(f32[12,24,128]{2,1,0:T(8,128)S(1)} %get-tuple-element.16), channel_id=1, source_target_pairs={{8,0},{16,8},{24,16},{32,24},{40,32},{48,40},{56,48},{64,56},{72,6... | collective-permute-start | bytes 442376 | tf_op jit(solution)/shard_map/ppermute | solution.py:216
  15.3 4.6 %collective-permute-start.2 = (f32[10,24,128]{2,1,0:T(8,128)S(1)}, f32[10,24,128]{2,1,0:T(8,128)S(1)}, u32[]{:S(2)}, u32[]{:S(2)}) collective-permute-start(f32[10,24,128]{2,1,0:T(8,128)S(1)} %get-tuple-element.15), channel_id=1, source_target_pairs={{0,8},{8,16},{16,24},{24,32},{32,40},{40,48},{48,56},{56,64},{64,7... | collective-permute-start | bytes 368648 | tf_op jit(solution)/shard_map/ppermute | solution.py:211
  19.9 0.0 copy-done.1
  19.9 0.0 copy-start.3
  19.9 0.0 copy-start.5
  19.9 0.0 copy-start.6
  20.6 1.7 %collective-permute-done.2.prev_ref = f32[10,24,128]{2,1,0:T(8,128)S(1)} collective-permute-done((f32[10,24,128]{2,1,0:T(8,128)S(1)}, f32[10,24,128]{2,1,0:T(8,128)S(1)}, u32[]{:S(2)}, u32[]{:S(2)}) %collective-permute-start.2) | collective-permute-done | bytes 122912 | tf_op jit(solution)/shard_map/ppermute | solution.py:211
  22.3 0.0 collective-permute-done.3.next_ref
  22.3 0.0 copy-done.3
  22.3 0.0 copy-done.5
  22.3 0.0 copy-done.6
  22.3 0.7 %copy-done.2 = s32[1,2,4,1]{2,3,1,0:T(1,128)S(1)} copy-done((s32[1,2,4,1]{2,3,1,0:T(1,128)S(1)}, s32[1,2,4,1]{2,3,1,0:T(1,128)}, u32[]{:S(2)}) %copy-start.2) | copy-done | bytes 56
  23.0 0.0 copy-done.4
  23.0 4.6 %advect.1 = (f32[32,24,128]{2,1,0:T(8,128)S(1)}, f32[64,1,256]{2,1,0:T(1,128)}) custom-call(s32[2,1,4]{2,1,0:T(1,128)S(1)} %bitcast.15, s32[1,1]{1,0:T(1,128)} %bitcast.12.count_ref, s32[1,16]{1,0:T(1,128)S(1)} %bitcast.17, s32[1,16]{1,0:T(1,128)S(1)} %bitcast.18, s32[1,16]{1,0:T(1,128)S(1)} %bitcast.19, f32[2,16]{1,0:T(2,128)S(1)} %bitcast.16, ...), custom_call_target="tpu_custom_call" | custom-call | tf_op jit(solution)/shard_map/advect/pallas_call | solution.py:260
  27.6 12.6 %all-to-all-start = ((f32[64,1,256]{2,1,0:T(1,128)}), f32[64,1,256]{2,1,0:T(1,128)S(1)}, u32[]{:S(2)}, u32[]{:S(2)}) async-start(f32[64,1,256]{2,1,0:T(1,128)} %get-tuple-element.17), calls=%async_computation | async-start | bytes 131072 | tf_op jit(solution)/shard_map/all_to_all | solution.py:287
  40.2 1.1 %columns.1 = f32[768,128]{1,0:T(8,128)} custom-call(f32[32,24,128]{2,1,0:T(8,128)S(1)} %get-tuple-element.18.advected_ref), custom_call_target="tpu_custom_call" | custom-call | bytes 2000000 | tf_op jit(solution)/shard_map/columns/pallas_call | solution.py:288
  41.3 9.2 %all-to-all-done.received_ref = f32[64,1,256]{2,1,0:T(1,128)S(1)} async-done(((f32[64,1,256]{2,1,0:T(1,128)}), f32[64,1,256]{2,1,0:T(1,128)S(1)}, u32[]{:S(2)}, u32[]{:S(2)}) %all-to-all-start) | async-done | bytes 65568 | tf_op jit(solution)/shard_map/all_to_all | solution.py:287
  50.5 1.7 %rim.1 = f32[24,32,128]{2,1,0:T(8,128)} custom-call(f32[64,1,256]{2,1,0:T(1,128)S(1)} %all-to-all-done.received_ref, f32[24,32,128]{2,1,0:T(8,128)} %bitcast.20), custom_call_target="tpu_custom_call", output_to_operand_aliasing={{}: (1, {})} | custom-call | tf_op jit(solution)/shard_map/rim/pallas_call | solution.py:297
  (6 shorter events, 0.0 us)
Async XLA Ops:
  0.0 1.0 %copy-start = (f32[1,24,32,128]{3,2,1,0:T(8,128)S(1)}, f32[1,24,32,128]{3,2,1,0:T(8,128)}, u32[]{:S(2)}) copy-start(f32[1,24,32,128]{3,2,1,0:T(8,128)} %param.8) | copy-start | bytes 1179652
  1.3 7.4 %collective-permute-start = (f32[4,24,128]{2,1,0:T(8,128)S(1)}, f32[4,24,128]{2,1,0:T(8,128)S(1)}, u32[]{:S(2)}, u32[]{:S(2)}) collective-permute-start(f32[4,24,128]{2,1,0:T(8,128)S(1)} %get-tuple-element.13), channel_id=1, source_target_pairs={{0,1},{1,2},{2,3},{3,4},{4,5},{5,6},{6,7},{8,9},{9,10},{10,11},{11... | collective-permute-start | bytes 147464 | tf_op jit(solution)/shard_map/ppermute | solution.py:211
  6.8 7.2 %collective-permute-start.1 = (f32[4,24,128]{2,1,0:T(8,128)S(1)}, f32[4,24,128]{2,1,0:T(8,128)S(1)}, u32[]{:S(2)}, u32[]{:S(2)}) collective-permute-start(f32[4,24,128]{2,1,0:T(8,128)S(1)} %get-tuple-element.14), channel_id=1, source_target_pairs={{1,0},{2,1},{3,2},{4,3},{5,4},{6,5},{7,6},{9,8},{10,9},{11,10},{12... | collective-permute-start | bytes 147464 | tf_op jit(solution)/shard_map/ppermute | solution.py:216
  14.0 5.9 %copy-start.1 = (f32[1,2,32,128]{3,2,1,0:T(8,128)S(1)}, f32[1,2,32,128]{3,2,1,0:T(8,128)}, u32[]{:S(2)}) copy-start(f32[1,2,32,128]{3,2,1,0:T(8,128)} %param.10) | copy-start | bytes 98308
  14.0 8.3 %collective-permute-start.3 = (f32[12,24,128]{2,1,0:T(8,128)S(1)}, f32[12,24,128]{2,1,0:T(8,128)S(1)}, u32[]{:S(2)}, u32[]{:S(2)}) collective-permute-start(f32[12,24,128]{2,1,0:T(8,128)S(1)} %get-tuple-element.16), channel_id=1, source_target_pairs={{8,0},{16,8},{24,16},{32,24},{40,32},{48,40},{56,48},{64,56},{72,6... | collective-permute-start | bytes 442376 | tf_op jit(solution)/shard_map/ppermute | solution.py:216
  15.3 7.0 %collective-permute-start.2 = (f32[10,24,128]{2,1,0:T(8,128)S(1)}, f32[10,24,128]{2,1,0:T(8,128)S(1)}, u32[]{:S(2)}, u32[]{:S(2)}) collective-permute-start(f32[10,24,128]{2,1,0:T(8,128)S(1)} %get-tuple-element.15), channel_id=1, source_target_pairs={{0,8},{8,16},{16,24},{24,32},{32,40},{40,48},{48,56},{56,64},{64,7... | collective-permute-start | bytes 368648 | tf_op jit(solution)/shard_map/ppermute | solution.py:211
  19.9 2.4 %copy-start.3 = (f32[1,1,1,2,16]{4,3,2,1,0:T(2,128)S(1)}, f32[1,1,1,2,16]{4,3,2,1,0:T(2,128)}, u32[]{:S(2)}) copy-start(f32[1,1,1,2,16]{4,3,2,1,0:T(2,128)} %param.15) | copy-start | bytes 388
  19.9 2.4 %copy-start.5 = (s32[1,1,1,16]{3,2,1,0:T(1,128)S(1)}, s32[1,1,1,16]{3,2,1,0:T(1,128)}, u32[]{:S(2)}) copy-start(s32[1,1,1,16]{3,2,1,0:T(1,128)} %param.13) | copy-start | bytes 196
  19.9 2.4 %copy-start.6 = (s32[1,1,1,16]{3,2,1,0:T(1,128)S(1)}, s32[1,1,1,16]{3,2,1,0:T(1,128)}, u32[]{:S(2)}) copy-start(s32[1,1,1,16]{3,2,1,0:T(1,128)} %param.14) | copy-start | bytes 196
  22.3 0.7 %copy-start.2 = (s32[1,2,4,1]{2,3,1,0:T(1,128)S(1)}, s32[1,2,4,1]{2,3,1,0:T(1,128)}, u32[]{:S(2)}) copy-start(s32[1,2,4,1]{2,3,1,0:T(1,128)} %param.9) | copy-start | bytes 100
  22.3 0.7 %copy-start.4 = (s32[1,1,1,16]{3,2,1,0:T(1,128)S(1)}, s32[1,1,1,16]{3,2,1,0:T(1,128)}, u32[]{:S(2)}) copy-start(s32[1,1,1,16]{3,2,1,0:T(1,128)} %param.12) | copy-start | bytes 196
  27.6 22.9 %all-to-all-start = ((f32[64,1,256]{2,1,0:T(1,128)}), f32[64,1,256]{2,1,0:T(1,128)S(1)}, u32[]{:S(2)}, u32[]{:S(2)}) async-start(f32[64,1,256]{2,1,0:T(1,128)} %get-tuple-element.17), calls=%async_computation | async-start | bytes 131072 | tf_op jit(solution)/shard_map/all_to_all | solution.py:287

commit v3 on v1

v3 whole, which is shorter than its diff:
```python
import functools

import jax
import jax.numpy as jnp
from jax import lax
from jax.experimental import pallas as pl
from jax.experimental.pallas import tpu as pltpu
from jax.sharding import PartitionSpec as P

TILE = 8
LOW = 8
HIGH = 9
WINDOW = TILE + 3
LANES = 128
PITCH = 16
GROUP = LANES // PITCH
FIELD = 32

VMEM = pl.BlockSpec(memory_space=pltpu.VMEM)
ANY = pl.BlockSpec(memory_space=pl.ANY)
HBM = pl.BlockSpec(memory_space=pltpu.HBM)


def lane_iota(shape):
    return lax.broadcasted_iota(jnp.int32, shape, len(shape) - 1)


def even_index(axis):
    return lax.axis_index(axis) % 2 == 0


def unpack(west, east, slot):
    lane = lane_iota(west.shape)
    if slot:
        west = pltpu.roll(west, LANES - PITCH * slot, 1)
        east = pltpu.roll(east, LANES - PITCH * slot, 1)
    return jnp.where(lane < LANES // 2, east, west)


def pack_kernel(cells_ref, rows_ref, even_ref, odd_ref, held_ref, sems):
    row_count, channels, lanes = rows_ref.shape
    copies = []
    for m in range(row_count // GROUP):
        part = (slice(None), pl.ds(m * GROUP, GROUP), slice(None))
        copies.append(pltpu.make_async_copy(cells_ref.at[part], held_ref.at[m], sems.at[m]))
        copies[m].start()
    even = even_index("lat")
    lane = lane_iota((channels, lanes))
    for m in range(row_count // GROUP):
        copies[m].wait()
        first = last = None
        for s in range(GROUP):
            row = held_ref[m, :, s, :]
            rows_ref[m * GROUP + s] = row
            turned = row if s == 0 else pltpu.roll(row, PITCH * s, 1)
            if s == 0:
                first = last = turned
            else:
                base = PITCH * s
                first = jnp.where((lane >= base) & (lane < base + HIGH), turned, first)
                last = jnp.where((lane >= base - LOW) & (lane < base), turned, last)
        even_ref[m] = jnp.where(even, last, first)
        odd_ref[m] = jnp.where(even, first, last)


def edge_kernel(rows_ref, even_ref, odd_ref, to_even_ref, to_odd_ref):
    row_count, channels, lanes = rows_ref.shape
    groups = row_count // GROUP
    even_lat, even_lon = even_index("lat"), even_index("lon")
    lane = lane_iota((channels, lanes))
    west = [jnp.where(even_lat, odd_ref[m], even_ref[m]) for m in (0, 1, groups - 1)]
    east = [jnp.where(even_lat, even_ref[m], odd_ref[m]) for m in (0, 1, groups - 1)]
    to_next = [rows_ref[row_count - LOW + i] for i in range(LOW)] + [west[2], east[2]]
    to_prev = [rows_ref[i] for i in range(HIGH)] + [west[0], east[0]]
    to_prev.append(jnp.where(lane < lanes // 2, east[1], west[1]))
    for i, up_row in enumerate(to_prev):
        down_row = to_next[i] if i < len(to_next) else up_row
        to_even_ref[i] = jnp.where(even_lon, down_row, up_row)
        to_odd_ref[i] = jnp.where(even_lon, up_row, down_row)


def prepare_kernel(
    fractions_ref, offsets_ref, count_ref, owner_ref, cell_ref, target_ref, frac_ref,
    even_ref, odd_ref, weights_ref, halo_ref, whole_ref, real_ref,
):
    for axis in range(2):
        x = fractions_ref[axis]
        weights_ref[4 * axis] = -x * (x - 1.0) * (x - 2.0) / 6.0
        weights_ref[4 * axis + 1] = (x + 1.0) * (x - 1.0) * (x - 2.0) / 2.0
        weights_ref[4 * axis + 2] = -(x + 1.0) * x * (x - 2.0) / 2.0
        weights_ref[4 * axis + 3] = (x + 1.0) * x * (x - 1.0) / 6.0
    even = even_index("lat")
    for m in range(halo_ref.shape[0] // GROUP):
        west = jnp.where(even, odd_ref[m], even_ref[m])
        east = jnp.where(even, even_ref[m], odd_ref[m])
        for s in range(GROUP):
            halo_ref[m * GROUP + s] = unpack(west, east, s)
    tiles, slots = offsets_ref.shape[2], owner_ref.shape[1]
    whole_ref[0:1, 0:tiles] = offsets_ref[0]
    whole_ref[1:2, 0:tiles] = offsets_ref[1]
    whole_ref[2:3, 0:1] = count_ref[...]
    whole_ref[3:4, 0:slots] = owner_ref[...]
    whole_ref[4:5, 0:slots] = cell_ref[...]
    whole_ref[5:6, 0:slots] = target_ref[...]
    real_ref[0:2, 0:slots] = frac_ref[...]


def advect_kernel(
    slots, whole_ref, real_ref, rows_ref, halo_ref, weights_ref, even_ref, odd_ref,
    advected_ref, message_ref,
    ext_ref, edge_ref, shifted_ref, ints_ref, frac_ref, sems,
):
    row_count, channels, lanes = rows_ref.shape
    copies = [
        pltpu.make_async_copy(whole_ref, ints_ref, sems.at[0]),
        pltpu.make_async_copy(real_ref, frac_ref, sems.at[1]),
    ]
    for copy in copies:
        copy.start()
    even = even_index("lon")
    prev = [jnp.where(even, odd_ref[i], even_ref[i]) for i in range(LOW + 2)]
    next_ = [jnp.where(even, even_ref[i], odd_ref[i]) for i in range(HIGH + 3)]
    for i in range(LOW):
        ext_ref[i] = prev[i]
        edge_ref[i] = unpack(prev[LOW], prev[LOW + 1], i)
    ext_ref[LOW : LOW + row_count] = rows_ref[...]
    edge_ref[LOW : LOW + row_count] = halo_ref[...]
    for i in range(HIGH):
        ext_ref[LOW + row_count + i] = next_[i]
        packed = (next_[HIGH], next_[HIGH + 1]) if i < GROUP else (next_[HIGH + 2],) * 2
        edge_ref[LOW + row_count + i] = unpack(*packed, i % GROUP)
    for copy in copies:
        copy.wait()

    lane = lane_iota((channels, lanes))
    for t in range(row_count // TILE):
        offset_lat = ints_ref[1, t]
        start = t * TILE + LOW - 1 + ints_ref[0, t]
        for b in range(4):
            shift = offset_lat - 1 + b
            inside = (lane >= shift) & (lane < LANES + shift)
            turn = (LANES - shift) & (LANES - 1)
            for j in range(WINDOW):
                mixed = jnp.where(inside, ext_ref[start + j], edge_ref[start + j])
                shifted_ref[t, b, j] = pltpu.roll(mixed, turn, 1)
        for i in range(TILE):
            row = t * TILE + i
            lat_weights = [weights_ref[4 + b, row : row + 1, :] for b in range(4)]
            total = None
            for a in range(4):
                inner = lat_weights[0] * shifted_ref[t, 0, i + a]
                for b in range(1, 4):
                    inner = inner + lat_weights[b] * shifted_ref[t, b, i + a]
                part = weights_ref[a, row : row + 1, :] * inner
                total = part if total is None else total + part
            advected_ref[row] = total

    channel = lax.broadcasted_iota(jnp.int32, (channels, lanes), 0)
    one_lane = lane_iota((1, lanes))
    capacity = slots // 2
    halves = capacity * FIELD // lanes
    per_row = lanes // FIELD
    sums = [jnp.zeros((channels, lanes), jnp.float32) for _ in range(2 * halves)]
    empty = jnp.where((one_lane & (FIELD - 1)) == channels, jnp.float32(lanes), jnp.float32(0.0))
    places = [empty for _ in range(2 * halves)]
    taken = [jnp.int32(0), jnp.int32(0)]
    at_value = lane - channel
    for k in range(slots):
        cell = ints_ref[4, k]
        r, c = cell >> 7, cell & (lanes - 1)
        a, b = frac_ref[0, k], frac_ref[1, k]
        near = jnp.where(one_lane == c, 1.0 - b, jnp.where(one_lane == c + 1, b, 0.0))
        value = jnp.sum(
            advected_ref[r] * ((1.0 - a) * near) + advected_ref[r + 1] * (a * near),
            axis=1,
            keepdims=True,
        )
        live = k < ints_ref[2, 0]
        side = (ints_ref[3, k] != 0).astype(jnp.int32)
        target = ints_ref[5, k].astype(jnp.float32)
        position = jnp.where(side == 0, taken[0], taken[1])
        taken[0] = taken[0] + jnp.where(live & (side == 0), 1, 0)
        taken[1] = taken[1] + jnp.where(live & (side == 1), 1, 0)
        base = (position % per_row) * FIELD
        here = jnp.where(live, side * halves + position // per_row, -1)
        for h in range(2 * halves):
            lane_base = jnp.where(here == h, base, -lanes)
            sums[h] = jnp.where(at_value == lane_base, value, sums[h])
            places[h] = jnp.where(one_lane == lane_base + channels, target, places[h])
    lon_count = message_ref.shape[0] // (2 * halves)
    other = (1 - lax.axis_index("panel")) * lon_count
    message_ref[...] = jnp.zeros_like(message_ref)
    for side in range(2):
        for h in range(halves):
            n = side * halves + h
            row = (other + side * (lon_count - 1)) * halves + h
            message_ref[pl.ds(row, 1), :] = jnp.sum(sums[n], axis=0, keepdims=True) + places[n]


def column_kernel(advected_ref, out_ref):
    row_count, channels, _ = advected_ref.shape
    for i in range(row_count):
        out_ref[pl.ds(i, channels, stride=row_count), :] = advected_ref[i]


def rim_kernel(lon_count, received_ref, given_ref, out_ref, rim_ref, sem):
    del given_ref
    channels, row_count, lanes = out_ref.shape
    lon = lax.axis_index("lon")

    @pl.when((lon == 0) | (lon == lon_count - 1))
    def _():
        entries = received_ref.shape[0] // 2
        other = (1 - lax.axis_index("panel")) * entries
        values = received_ref[pl.ds(other, entries), :]
        lane = lane_iota((entries, lanes))
        chosen = []
        for q in range(lanes // FIELD):
            at = q * FIELD + channels
            place = values[:, at : at + 1].astype(jnp.int32)
            chosen.append(jnp.where(lane == place, 1.0, 0.0))
        spread = lax.dot_general(
            values,
            jnp.concatenate(chosen, axis=1),
            (((0,), (0,)), ((), ())),
            precision=lax.Precision.HIGHEST,
            preferred_element_type=jnp.float32,
        )
        rim = spread[0:channels, 0:lanes]
        for q in range(1, lanes // FIELD):
            rim = rim + spread[q * FIELD : q * FIELD + channels, q * lanes : (q + 1) * lanes]
        rim_ref[...] = rim.reshape(channels, 1, lanes)
        row = jnp.where(lon == 0, 0, row_count - 1)
        copy = pltpu.make_async_copy(rim_ref, out_ref.at[:, pl.ds(row, 1), :], sem)
        copy.start()
        copy.wait()


def f32(*shape):
    return jax.ShapeDtypeStruct(shape, jnp.float32)


def swap(array, axis, first):
    pairs = []
    for i in range(first, lax.axis_size(axis) - 1, 2):
        pairs += [(i, i + 1), (i + 1, i)]
    return lax.ppermute(array, axis, pairs)


def params(mib):
    return pltpu.CompilerParams(vmem_limit_bytes=mib * 1024 * 1024)


def body(fields, offsets, fractions, send_count, send_owner, send_cell, send_target, send_frac):
    _, channels, row_count, lanes = fields.shape
    groups = row_count // GROUP
    lon_count = lax.axis_size("lon")
    slots = send_owner.shape[-1]
    width = slots // 2 * FIELD
    ext = LOW + row_count + HIGH

    strip = f32(groups, channels, lanes)
    rows, lat_even, lat_odd = pl.pallas_call(
        pack_kernel,
        out_shape=(f32(row_count, channels, lanes), strip, strip),
        in_specs=[HBM],
        out_specs=(VMEM,) * 3,
        scratch_shapes=[
            pltpu.VMEM((groups, channels, GROUP, lanes), jnp.float32),
            pltpu.SemaphoreType.DMA((groups,)),
        ],
        compiler_params=params(4),
        name="pack",
    )(fields[0])
    lat_even = swap(lat_even, "lat", 0)
    lat_odd = swap(lat_odd, "lat", 1)
    edge = f32(HIGH + 3, channels, lanes)
    lon_even, lon_odd = pl.pallas_call(
        edge_kernel,
        out_shape=(edge, edge),
        in_specs=[VMEM] * 3,
        out_specs=(VMEM, VMEM),
        compiler_params=params(2),
        name="edges",
    )(rows, lat_even, lat_odd)
    lon_even = swap(lon_even, "lon", 0)
    lon_odd = swap(lon_odd, "lon", 1)
    weights, halo, whole, real = pl.pallas_call(
        prepare_kernel,
        out_shape=(
            f32(8, row_count, lanes),
            f32(row_count, channels, lanes),
            jax.ShapeDtypeStruct((8, lanes), jnp.int32),
            f32(8, lanes),
        ),
        in_specs=[VMEM] * 9,
        out_specs=(VMEM,) * 4,
        cost_estimate=pl.CostEstimate(flops=400000, bytes_accessed=400000, transcendentals=0),
        compiler_params=params(2),
        name="prepare",
    )(
        fractions[0],
        offsets[0].transpose(0, 2, 1),
        send_count[0],
        send_owner[0, 0],
        send_cell[0, 0],
        send_target[0, 0],
        send_frac[0, 0, 0],
        lat_even,
        lat_odd,
    )
    advected, message = pl.pallas_call(
        functools.partial(advect_kernel, slots),
        out_shape=(
            f32(row_count, channels, lanes),
            f32(2 * lon_count * width // lanes, lanes),
        ),
        in_specs=[VMEM] * 7,
        out_specs=(VMEM, VMEM),
        scratch_shapes=[
            pltpu.VMEM((ext, channels, lanes), jnp.float32),
            pltpu.VMEM((ext, channels, lanes), jnp.float32),
            pltpu.VMEM((row_count // TILE, 4, WINDOW, channels, lanes), jnp.float32),
            pltpu.SMEM((8, lanes), jnp.int32),
            pltpu.SMEM((8, lanes), jnp.float32),
            pltpu.SemaphoreType.DMA((2,)),
        ],
        compiler_params=params(8),
        name="advect",
    )(whole, real, rows, halo, weights, lon_even, lon_odd)
    received = lax.all_to_all(
        message.reshape(2 * lon_count, 1, width), ("panel", "lon"), 0, 0, tiled=True
    )
    columns = pl.pallas_call(
        column_kernel,
        out_shape=f32(channels * row_count, lanes),
        in_specs=[VMEM],
        out_specs=VMEM,
        cost_estimate=pl.CostEstimate(flops=0, bytes_accessed=2000000, transcendentals=0),
        compiler_params=params(2),
        name="columns",
    )(advected)
    out = pl.pallas_call(
        functools.partial(rim_kernel, lon_count),
        out_shape=f32(channels, row_count, lanes),
        in_specs=[VMEM, ANY],
        out_specs=ANY,
        scratch_shapes=[
            pltpu.VMEM((channels, 1, lanes), jnp.float32),
            pltpu.SemaphoreType.DMA(()),
        ],
        input_output_aliases={1: 0},
        compiler_params=params(2),
        name="rim",
    )(received.reshape(message.shape), columns.reshape(channels, row_count, lanes))
    return out[None]


def solution(mesh):
    placed = (
        P("panel", None, "lon", "lat"),
        P("panel", None, "lon", "lat"),
        P("panel", None, "lon", "lat"),
        P("panel", "lon", "lat"),
        P("panel", "lon", "lat", None),
        P("panel", "lon", "lat", None),
        P("panel", "lon", "lat", None),
        P("panel", "lon", "lat", None, None),
    )
    return jax.shard_map(
        body, mesh=mesh, in_specs=placed, out_specs=P("panel", None, "lon", "lat"), check_vma=False
    )
```

time: 59.3 us -> 48.2 us (0.81)
  Pallas kernels: 14.4 us -> 5.52 us
  local copies, waits for them, and re-layouts: 3.54 us -> 1.68 us
  waiting for transfers between devices: 14.2 us -> 12.5 us
  starting transfers between devices: 25.9 us -> 27.4 us
    pallas_call x5, Pallas kernels: 12.3 us -> 4.42 us  [the longest x1 2.44 us: body(): pl.pallas_call(functools.partial(advect_kernel, slots), out_shape=(f32(ro...]
    ppermute x4, waiting for transfers between devices: 6.04 us -> 3.29 us  [swap(): return lax.ppermute(array, axis, pairs)]
    unnamed x26 -> x14, local copies, waits for them, and re-layouts: 3.54 us -> 1.68 us
    all_to_all x1, starting transfers between devices: 12.5 us -> 14.4 us  [body(): lax.all_to_all(message.reshape(2 * lon_count, 1, width), ('panel', 'lon')...]
    pallas_call x1, Pallas kernels: 2.1 us -> 1.1 us  [body(): pl.pallas_call(column_kernel, out_shape=f32(channels * row_count, lanes),...]
    all_to_all x1, waiting for transfers between devices: 8.17 us -> 9.17 us  [body(): lax.all_to_all(message.reshape(2 * lon_count, 1, width), ('panel', 'lon')...]
  transfers between devices with their start and end apart: 5 -> 5, of which waited for: 4 -> 3; matrix products, arithmetic and copies ran while one was open for 0% -> 0% of each run, Pallas kernels for 6% -> 3%
where the time goes in v3:
time: 48.2 us; the launch traced here: 47.8 us
  starting transfers between devices  27.4 us (57%)
  waiting for transfers between devices  12.5 us (26%)
  Pallas kernels  5.52 us (11%)
  local copies, waits for them, and re-layouts  1.68 us (3%)
  between operations  0.78 us (2%)
    all_to_all x1, starting transfers between devices, body(): lax.all_to_all(message.reshape(2 * lon_count, 1, width), ('panel', 'lon')...  14.4 us
    ppermute x4, starting transfers between devices, swap(): return lax.ppermute(array, axis, pairs)  13 us
    all_to_all x1, waiting for transfers between devices, body(): lax.all_to_all(message.reshape(2 * lon_count, 1, width), ('panel', 'lon')...  9.17 us
    ppermute x4, waiting for transfers between devices, swap(): return lax.ppermute(array, axis, pairs)  3.29 us
    pallas_call x1, Pallas kernels, body(): pl.pallas_call(functools.partial(advect_kernel, slots), out_shape=(f32(ro...  2.44 us
    unnamed x14, local copies, waits for them, and re-layouts  1.68 us
    pallas_call x1, Pallas kernels, body(): pl.pallas_call(column_kernel, out_shape=f32(channels * row_count, lanes),...  1.1 us
    pallas_call x1, Pallas kernels, body(): pl.pallas_call(functools.partial(rim_kernel, lon_count), out_shape=f32(ch...  1.09 us
  transfers between devices with their start and end apart: 5, of which 3 were waited for; matrix products, arithmetic and copies ran while one was open for 0% of the time, Pallas kernels for 3%

profile of v3, /device:TPU:192, one launch (start us, length us, event | category | flops | bytes accessed | tf_op | source)
XLA Modules:
  0.0 47.8 jit_solution(17585913764891790114)
XLA Ops:
  0.0 1.0 %copy-done = f32[1,24,32,128]{3,2,1,0:T(8,128)S(1)} copy-done((f32[1,24,32,128]{3,2,1,0:T(8,128)S(1)}, f32[1,24,32,128]{3,2,1,0:T(8,128)}, u32[]{:S(2)}) %copy-start) | copy-done | bytes 393240
  1.0 0.6 %pack.1 = (f32[32,24,128]{2,1,0:T(8,128)S(1)}, f32[4,24,128]{2,1,0:T(8,128)S(1)}, f32[4,24,128]{2,1,0:T(8,128)S(1)}) custom-call(f32[24,32,128]{2,1,0:T(8,128)S(1)} %bitcast.15), custom_call_target="tpu_custom_call" | custom-call | tf_op jit(solution)/shard_map/pack/pallas_call | solution.py:263
  1.6 1.9 %collective-permute-start = (f32[4,24,128]{2,1,0:T(8,128)S(1)}, f32[4,24,128]{2,1,0:T(8,128)S(1)}, u32[]{:S(2)}, u32[]{:S(2)}) collective-permute-start(f32[4,24,128]{2,1,0:T(8,128)S(1)} %get-tuple-element.16), channel_id=1, source_target_pairs={{0,1},{1,0},{2,3},{3,2},{4,5},{5,4},{6,7},{7,6},{8,9},{9,8},{10,11... | collective-permute-start | bytes 147464 | tf_op jit(solution)/shard_map/ppermute | solution.py:247
  3.6 7.0 %collective-permute-start.1 = (f32[4,24,128]{2,1,0:T(8,128)S(1)}, f32[4,24,128]{2,1,0:T(8,128)S(1)}, u32[]{:S(2)}, u32[]{:S(2)}) collective-permute-start(f32[4,24,128]{2,1,0:T(8,128)S(1)} %get-tuple-element.17), channel_id=1, source_target_pairs={{1,2},{2,1},{3,4},{4,3},{5,6},{6,5},{9,10},{10,9},{11,12},{12,11},... | collective-permute-start | bytes 147464 | tf_op jit(solution)/shard_map/ppermute | solution.py:247
  10.5 0.0 collective-permute-done.even_ref
  10.5 2.0 %collective-permute-done.1.odd_ref = f32[4,24,128]{2,1,0:T(8,128)S(1)} collective-permute-done((f32[4,24,128]{2,1,0:T(8,128)S(1)}, f32[4,24,128]{2,1,0:T(8,128)S(1)}, u32[]{:S(2)}, u32[]{:S(2)}) %collective-permute-start.1) | collective-permute-done | bytes 49184 | tf_op jit(solution)/shard_map/ppermute | solution.py:247
  12.6 3.5 %collective-permute-start.2 = (f32[12,24,128]{2,1,0:T(8,128)S(1)}, f32[12,24,128]{2,1,0:T(8,128)S(1)}, u32[]{:S(2)}, u32[]{:S(2)}) collective-permute-start(f32[12,24,128]{2,1,0:T(8,128)S(1)} %get-tuple-element.23), channel_id=1, source_target_pairs={{0,8},{8,0},{16,24},{24,16},{32,40},{40,32},{48,56},{56,48},{64,72... | collective-permute-start | bytes 442376 | tf_op jit(solution)/shard_map/ppermute | solution.py:247
  16.1 0.7 %collective-permute-start.3 = (f32[12,24,128]{2,1,0:T(8,128)S(1)}, f32[12,24,128]{2,1,0:T(8,128)S(1)}, u32[]{:S(2)}, u32[]{:S(2)}) collective-permute-start(f32[12,24,128]{2,1,0:T(8,128)S(1)} %get-tuple-element.24), channel_id=1, source_target_pairs={{8,16},{16,8},{24,32},{32,24},{40,48},{48,40},{56,64},{64,56},{72,... | collective-permute-start | bytes 442376 | tf_op jit(solution)/shard_map/ppermute | solution.py:247
  17.4 0.0 copy-start.3
  17.4 0.0 copy-start.5
  17.5 0.0 copy-start.6
  17.5 0.0 copy-start.2
  17.5 0.0 copy-start.4
  17.5 0.6 %copy-done.3 = f32[1,1,1,2,16]{4,3,2,1,0:T(2,128)S(1)} copy-done((f32[1,1,1,2,16]{4,3,2,1,0:T(2,128)S(1)}, f32[1,1,1,2,16]{4,3,2,1,0:T(2,128)}, u32[]{:S(2)}) %copy-start.3) | copy-done | bytes 152
  18.1 0.0 copy-done.6
  18.1 0.0 copy-done.2
  18.2 0.2 prepare.1
  18.4 1.2 %collective-permute-done.2.even_ref = f32[12,24,128]{2,1,0:T(8,128)S(1)} collective-permute-done((f32[12,24,128]{2,1,0:T(8,128)S(1)}, f32[12,24,128]{2,1,0:T(8,128)S(1)}, u32[]{:S(2)}, u32[]{:S(2)}) %collective-permute-start.2) | collective-permute-done | bytes 147488 | tf_op jit(solution)/shard_map/ppermute | solution.py:247
  19.6 0.0 collective-permute-done.3.odd_ref
  19.7 2.4 %advect.1 = (f32[32,24,128]{2,1,0:T(8,128)S(1)}, f32[128,128]{1,0:T(8,128)}) custom-call(s32[8,128]{1,0:T(8,128)S(1)} %get-tuple-element.18.whole_ref, f32[8,128]{1,0:T(8,128)S(1)} %get-tuple-element.19.real_ref, f32[32,24,128]{2,1,0:T(8,128)S(1)} %get-tuple-element.20.rows_ref, f32[32,24,128]{2,1,0:T(8,128)S(1)} %get-tuple-element.21.halo_ref, ...), custom_call_target="tpu_custom_call" | custom-call | tf_op jit(solution)/shard_map/advect/pallas_call | solution.py:312
  22.1 14.4 %all-to-all-start = ((f32[64,1,256]{2,1,0:T(1,128)}), f32[64,1,256]{2,1,0:T(1,128)S(1)}, u32[]{:S(2)}, u32[]{:S(2)}) async-start(f32[64,1,256]{2,1,0:T(1,128)} %bitcast.9), calls=%async_computation | async-start | bytes 131072 | tf_op jit(solution)/shard_map/all_to_all | solution.py:331
  36.5 1.1 %columns.1 = f32[768,128]{1,0:T(8,128)} custom-call(f32[32,24,128]{2,1,0:T(8,128)S(1)} %get-tuple-element.26.advected_ref), custom_call_target="tpu_custom_call" | custom-call | bytes 2000000 | tf_op jit(solution)/shard_map/columns/pallas_call | solution.py:334
  37.6 9.2 %all-to-all-done = f32[64,1,256]{2,1,0:T(1,128)S(1)} async-done(((f32[64,1,256]{2,1,0:T(1,128)}), f32[64,1,256]{2,1,0:T(1,128)S(1)}, u32[]{:S(2)}, u32[]{:S(2)}) %all-to-all-start) | async-done | bytes 65568 | tf_op jit(solution)/shard_map/all_to_all | solution.py:331
  46.7 1.1 %rim.1 = f32[24,32,128]{2,1,0:T(8,128)} custom-call(f32[128,128]{1,0:T(8,128)S(1)} %bitcast.16, f32[24,32,128]{2,1,0:T(8,128)} %bitcast.23), custom_call_target="tpu_custom_call", output_to_operand_aliasing={{}: (1, {})} | custom-call | tf_op jit(solution)/shard_map/rim/pallas_call | solution.py:343
  (6 shorter events, 0.0 us)
Async XLA Ops:
  0.0 1.0 %copy-start = (f32[1,24,32,128]{3,2,1,0:T(8,128)S(1)}, f32[1,24,32,128]{3,2,1,0:T(8,128)}, u32[]{:S(2)}) copy-start(f32[1,24,32,128]{3,2,1,0:T(8,128)} %param.8) | copy-start | bytes 1179652
  1.6 8.9 %collective-permute-start = (f32[4,24,128]{2,1,0:T(8,128)S(1)}, f32[4,24,128]{2,1,0:T(8,128)S(1)}, u32[]{:S(2)}, u32[]{:S(2)}) collective-permute-start(f32[4,24,128]{2,1,0:T(8,128)S(1)} %get-tuple-element.16), channel_id=1, source_target_pairs={{0,1},{1,0},{2,3},{3,2},{4,5},{5,4},{6,7},{7,6},{8,9},{9,8},{10,11... | collective-permute-start | bytes 147464 | tf_op jit(solution)/shard_map/ppermute | solution.py:247
  3.6 9.0 %collective-permute-start.1 = (f32[4,24,128]{2,1,0:T(8,128)S(1)}, f32[4,24,128]{2,1,0:T(8,128)S(1)}, u32[]{:S(2)}, u32[]{:S(2)}) collective-permute-start(f32[4,24,128]{2,1,0:T(8,128)S(1)} %get-tuple-element.17), channel_id=1, source_target_pairs={{1,2},{2,1},{3,4},{4,3},{5,6},{6,5},{9,10},{10,9},{11,12},{12,11},... | collective-permute-start | bytes 147464 | tf_op jit(solution)/shard_map/ppermute | solution.py:247
  12.6 4.9 %copy-start.1 = (f32[1,2,32,128]{3,2,1,0:T(8,128)S(1)}, f32[1,2,32,128]{3,2,1,0:T(8,128)}, u32[]{:S(2)}) copy-start(f32[1,2,32,128]{3,2,1,0:T(8,128)} %param.10) | copy-start | bytes 98308
  12.6 7.0 %collective-permute-start.2 = (f32[12,24,128]{2,1,0:T(8,128)S(1)}, f32[12,24,128]{2,1,0:T(8,128)S(1)}, u32[]{:S(2)}, u32[]{:S(2)}) collective-permute-start(f32[12,24,128]{2,1,0:T(8,128)S(1)} %get-tuple-element.23), channel_id=1, source_target_pairs={{0,8},{8,0},{16,24},{24,16},{32,40},{40,32},{48,56},{56,48},{64,72... | collective-permute-start | bytes 442376 | tf_op jit(solution)/shard_map/ppermute | solution.py:247
  16.1 3.5 %collective-permute-start.3 = (f32[12,24,128]{2,1,0:T(8,128)S(1)}, f32[12,24,128]{2,1,0:T(8,128)S(1)}, u32[]{:S(2)}, u32[]{:S(2)}) collective-permute-start(f32[12,24,128]{2,1,0:T(8,128)S(1)} %get-tuple-element.24), channel_id=1, source_target_pairs={{8,16},{16,8},{24,32},{32,24},{40,48},{48,40},{56,64},{64,56},{72,... | collective-permute-start | bytes 442376 | tf_op jit(solution)/shard_map/ppermute | solution.py:247
  17.4 0.7 %copy-start.3 = (f32[1,1,1,2,16]{4,3,2,1,0:T(2,128)S(1)}, f32[1,1,1,2,16]{4,3,2,1,0:T(2,128)}, u32[]{:S(2)}) copy-start(f32[1,1,1,2,16]{4,3,2,1,0:T(2,128)} %param.15) | copy-start | bytes 388
  17.4 0.7 %copy-start.5 = (s32[1,1,1,16]{3,2,1,0:T(1,128)S(1)}, s32[1,1,1,16]{3,2,1,0:T(1,128)}, u32[]{:S(2)}) copy-start(s32[1,1,1,16]{3,2,1,0:T(1,128)} %param.13) | copy-start | bytes 196
  17.5 0.7 %copy-start.6 = (s32[1,1,1,16]{3,2,1,0:T(1,128)S(1)}, s32[1,1,1,16]{3,2,1,0:T(1,128)}, u32[]{:S(2)}) copy-start(s32[1,1,1,16]{3,2,1,0:T(1,128)} %param.14) | copy-start | bytes 196
  17.5 0.7 %copy-start.2 = (s32[1,2,4,1]{2,3,1,0:T(1,128)S(1)}, s32[1,2,4,1]{2,3,1,0:T(1,128)}, u32[]{:S(2)}) copy-start(s32[1,2,4,1]{2,3,1,0:T(1,128)} %param.9) | copy-start | bytes 100
  17.5 0.7 %copy-start.4 = (s32[1,1,1,16]{3,2,1,0:T(1,128)S(1)}, s32[1,1,1,16]{3,2,1,0:T(1,128)}, u32[]{:S(2)}) copy-start(s32[1,1,1,16]{3,2,1,0:T(1,128)} %param.12) | copy-start | bytes 196
  22.1 24.6 %all-to-all-start = ((f32[64,1,256]{2,1,0:T(1,128)}), f32[64,1,256]{2,1,0:T(1,128)S(1)}, u32[]{:S(2)}, u32[]{:S(2)}) async-start(f32[64,1,256]{2,1,0:T(1,128)} %bitcast.9), calls=%async_computation | async-start | bytes 131072 | tf_op jit(solution)/shard_map/all_to_all | solution.py:331

commit v4 on v3

v4 whole, which is shorter than its diff:
```python
import functools

import jax
import jax.numpy as jnp
from jax import lax
from jax.experimental import pallas as pl
from jax.experimental.pallas import tpu as pltpu
from jax.sharding import PartitionSpec as P

TILE = 8
LOW = 8
HIGH = 9
WINDOW = TILE + 3
LANES = 128
PITCH = 8
GROUP = LANES // PITCH
FIRST = {"lon": 1, "lat": 0}
FIELD = 32

VMEM = pl.BlockSpec(memory_space=pltpu.VMEM)
ANY = pl.BlockSpec(memory_space=pl.ANY)
HBM = pl.BlockSpec(memory_space=pltpu.HBM)


def lane_iota(shape):
    return lax.broadcasted_iota(jnp.int32, shape, len(shape) - 1)


def up_first(axis):
    return lax.axis_index(axis) % 2 == FIRST[axis]


def params(mib):
    return pltpu.CompilerParams(vmem_limit_bytes=mib * 1024 * 1024)


def ends_kernel(cells_ref, first_step_ref, second_step_ref, head_ref, tail_ref, ninth_ref, sems):
    row_count = cells_ref.shape[1]
    copies = [
        pltpu.make_async_copy(cells_ref.at[:, 0:LOW, :], head_ref, sems.at[0]),
        pltpu.make_async_copy(cells_ref.at[:, row_count - LOW : row_count, :], tail_ref, sems.at[1]),
        pltpu.make_async_copy(cells_ref.at[:, LOW:HIGH, :], ninth_ref, sems.at[2]),
    ]
    for copy in copies:
        copy.start()
    up = up_first("lon")
    for copy in copies:
        copy.wait()
    for i in range(LOW):
        head, tail = head_ref[:, i, :], tail_ref[:, i, :]
        first_step_ref[i] = jnp.where(up, tail, head)
        second_step_ref[i] = jnp.where(up, head, tail)
    ninth = ninth_ref[:, 0, :]
    first_step_ref[LOW] = ninth
    second_step_ref[LOW] = ninth


def pack(rows, first, last, ninth):
    lane = lane_iota(rows[0][1].shape)
    for e, row in rows:
        g, base = e // GROUP, PITCH * (e % GROUP)
        turned = pltpu.roll(row, base, 1) if base else row
        first[g] = jnp.where((lane >= base) & (lane < base + PITCH), turned, first[g])
        below = (base - PITCH) % LANES
        last[g] = jnp.where((lane >= below) & (lane < below + PITCH), turned, last[g])
        ninth[g] = jnp.where(lane == (base + PITCH) % LANES, turned, ninth[g])


def own_kernel(*refs):
    count_ref, given, outputs, held, sems = refs[0], refs[1:8], refs[8:15], refs[15:22], refs[22]
    rows_ref, first_ref, last_ref, ninth_ref, weights_ref, whole_ref, real_ref = outputs
    fractions_ref, offsets_ref, owner_ref, cell_ref, target_ref, frac_ref, cells_ref = held
    copies = [pltpu.make_async_copy(given[n], held[n], sems.at[n]) for n in range(7)]
    for copy in copies:
        copy.start()
    row_count, channels, lanes = rows_ref.shape
    for copy in copies:
        copy.wait()
    rows = []
    for i in range(row_count):
        row = cells_ref[pl.ds(i, channels, stride=row_count), :]
        rows_ref[i] = row
        rows.append((i + LOW, row))
    empty = jnp.zeros((channels, lanes), jnp.float32)
    first, last, ninth = ([empty] * first_ref.shape[0] for _ in range(3))
    pack(rows, first, last, ninth)
    for g in range(first_ref.shape[0]):
        first_ref[g], last_ref[g], ninth_ref[g] = first[g], last[g], ninth[g]
    for axis in range(2):
        x = fractions_ref[axis]
        weights_ref[4 * axis] = -x * (x - 1.0) * (x - 2.0) / 6.0
        weights_ref[4 * axis + 1] = (x + 1.0) * (x - 1.0) * (x - 2.0) / 2.0
        weights_ref[4 * axis + 2] = -(x + 1.0) * x * (x - 2.0) / 2.0
        weights_ref[4 * axis + 3] = (x + 1.0) * x * (x - 1.0) / 6.0
    tiles, slots = offsets_ref.shape[2], owner_ref.shape[1]
    whole_ref[0:1, 0:tiles] = offsets_ref[0]
    whole_ref[1:2, 0:tiles] = offsets_ref[1]
    whole_ref[2:3, :] = jnp.full((1, lanes), count_ref[0, 0], jnp.int32)
    whole_ref[3:4, 0:slots] = owner_ref[...]
    whole_ref[4:5, 0:slots] = cell_ref[...]
    whole_ref[5:6, 0:slots] = target_ref[...]
    real_ref[0:2, 0:slots] = frac_ref[...]


def sides_kernel(
    from_first_ref, from_second_ref, first_ref, last_ref, ninth_ref, first_step_ref, second_step_ref
):
    groups, channels, lanes = first_ref.shape
    up = up_first("lon")
    prev = [jnp.where(up, from_second_ref[i], from_first_ref[i]) for i in range(LOW)]
    next_ = [jnp.where(up, from_first_ref[i], from_second_ref[i]) for i in range(HIGH)]
    first, last, ninth = ([ref[g] for g in range(groups)] for ref in (first_ref, last_ref, ninth_ref))
    after = groups * GROUP - LOW
    pack([(i, prev[i]) for i in range(LOW)], first, last, ninth)
    pack([(after + i, next_[i]) for i in range(LOW)], first, last, ninth)
    lane = lane_iota((channels, lanes))
    within = lane & (PITCH - 1)
    mixed = ninth[0]
    for g in range(1, groups):
        mixed = jnp.where(within == g, pltpu.roll(ninth[g], g, 1), mixed)
    low_part, high_part = pltpu.roll(next_[LOW], 3, 1), pltpu.roll(next_[LOW], 6, 1)
    mixed = jnp.where((lane >= 3) & (lane < 8), low_part, mixed)
    mixed = jnp.where((lane >= 11) & (lane < 15), high_part, mixed)
    first.append(mixed)
    last.append(next_[LOW])
    up = up_first("lat")
    for g in range(groups + 1):
        first_step_ref[g] = jnp.where(up, last[g], first[g])
        second_step_ref[g] = jnp.where(up, first[g], last[g])


def shift_of(ints_ref, t, b):
    return ints_ref[1, t] - 1 + b


def center_kernel(
    whole_ref, rows_ref, from_first_ref, from_second_ref, centers_ref, ext_ref, ints_ref, sem
):
    row_count, _, _ = rows_ref.shape
    copy = pltpu.make_async_copy(whole_ref, ints_ref, sem)
    copy.start()
    up = up_first("lon")
    for i in range(LOW):
        ext_ref[i] = jnp.where(up, from_second_ref[i], from_first_ref[i])
    ext_ref[LOW : LOW + row_count] = rows_ref[...]
    for i in range(HIGH):
        ext_ref[LOW + row_count + i] = jnp.where(up, from_first_ref[i], from_second_ref[i])
    copy.wait()
    for t in range(row_count // TILE):
        start = t * TILE + LOW - 1 + ints_ref[0, t]
        for b in range(4):
            turn = (LANES - shift_of(ints_ref, t, b)) & (LANES - 1)
            for j in range(WINDOW):
                centers_ref[t, b, j] = pltpu.roll(ext_ref[start + j], turn, 1)


def advect_kernel(
    slots, whole_ref, real_ref, centers_ref, weights_ref, from_first_ref, from_second_ref,
    advected_ref, message_ref,
    east_ref, west_ref, ninth_ref, shifted_ref, ints_ref, frac_ref, sems,
):
    row_count, channels, lanes = advected_ref.shape
    copies = [
        pltpu.make_async_copy(whole_ref, ints_ref, sems.at[0]),
        pltpu.make_async_copy(real_ref, frac_ref, sems.at[1]),
    ]
    for copy in copies:
        copy.start()
    lane = lane_iota((channels, lanes))
    up = up_first("lat")
    groups = east_ref.shape[0] - 1
    for g in range(groups + 1):
        west_ref[g] = jnp.where(up, from_second_ref[g], from_first_ref[g])
    for g in range(groups):
        east_ref[g] = jnp.where(up, from_first_ref[g], from_second_ref[g])
    mixed = jnp.where(up, from_first_ref[groups], from_second_ref[groups])
    ninth_ref[0] = mixed
    for g in range(1, groups):
        ninth_ref[g] = pltpu.roll(mixed, LANES - g, 1)
    last_row = jnp.where(lane < 5, pltpu.roll(mixed, LANES - 3, 1), pltpu.roll(mixed, LANES - 6, 1))
    east_ref[groups] = last_row
    ninth_ref[groups] = last_row
    for copy in copies:
        copy.wait()

    within = lane & (PITCH - 1)
    for t in range(row_count // TILE):
        offset_lat = ints_ref[1, t]
        start = t * TILE + LOW - 1 + ints_ref[0, t]
        from_east = within < offset_lat + 2
        for j in range(WINDOW):
            e = start + j
            g, base = e >> 4, PITCH * (e & (GROUP - 1))
            packed = jnp.where(from_east, east_ref[g], west_ref[g])
            beyond = jnp.where(offset_lat + 2 == HIGH, (base + PITCH) & (LANES - 1), -1)
            for b in range(4):
                shift = shift_of(ints_ref, t, b)
                inside = (lane >= -shift) & (lane < LANES - shift)
                if b == 3:
                    packed = jnp.where(lane == beyond, ninth_ref[g], packed)
                halo = pltpu.roll(packed, (2 * LANES - base - shift) & (LANES - 1), 1)
                shifted_ref[t, b, j] = jnp.where(inside, centers_ref[t, b, j], halo)
    for t in range(row_count // TILE):
        for i in range(TILE):
            row = t * TILE + i
            lat_weights = [weights_ref[4 + b, row : row + 1, :] for b in range(4)]
            total = None
            for a in range(4):
                inner = lat_weights[0] * shifted_ref[t, 0, i + a]
                for b in range(1, 4):
                    inner = inner + lat_weights[b] * shifted_ref[t, b, i + a]
                part = weights_ref[a, row : row + 1, :] * inner
                total = part if total is None else total + part
            advected_ref[row] = total

    channel = lax.broadcasted_iota(jnp.int32, (channels, lanes), 0)
    one_lane = lane_iota((1, lanes))
    capacity = slots // 2
    halves = capacity * FIELD // lanes
    per_row = lanes // FIELD
    sums = [jnp.zeros((channels, lanes), jnp.float32) for _ in range(2 * halves)]
    empty = jnp.where((one_lane & (FIELD - 1)) == channels, jnp.float32(lanes), jnp.float32(0.0))
    places = [empty for _ in range(2 * halves)]
    taken = [jnp.int32(0), jnp.int32(0)]
    at_value = lane - channel
    for k in range(slots):
        cell = ints_ref[4, k]
        r, c = cell >> 7, cell & (lanes - 1)
        a, b = frac_ref[0, k], frac_ref[1, k]
        near = jnp.where(one_lane == c, 1.0 - b, jnp.where(one_lane == c + 1, b, 0.0))
        value = jnp.sum(
            advected_ref[r] * ((1.0 - a) * near) + advected_ref[r + 1] * (a * near),
            axis=1,
            keepdims=True,
        )
        live = k < ints_ref[2, 0]
        side = (ints_ref[3, k] != 0).astype(jnp.int32)
        target = ints_ref[5, k].astype(jnp.float32)
        position = jnp.where(side == 0, taken[0], taken[1])
        taken[0] = taken[0] + jnp.where(live & (side == 0), 1, 0)
        taken[1] = taken[1] + jnp.where(live & (side == 1), 1, 0)
        base = (position % per_row) * FIELD
        here = jnp.where(live, side * halves + position // per_row, -1)
        for h in range(2 * halves):
            lane_base = jnp.where(here == h, base, -lanes)
            sums[h] = jnp.where(at_value == lane_base, value, sums[h])
            places[h] = jnp.where(one_lane == lane_base + channels, target, places[h])
    lon_count = message_ref.shape[0] // (2 * halves)
    other = (1 - lax.axis_index("panel")) * lon_count
    message_ref[...] = jnp.zeros_like(message_ref)
    for side in range(2):
        for h in range(halves):
            n = side * halves + h
            row = (other + side * (lon_count - 1)) * halves + h
            message_ref[pl.ds(row, 1), :] = jnp.sum(sums[n], axis=0, keepdims=True) + places[n]


def column_kernel(advected_ref, out_ref):
    row_count, channels, _ = advected_ref.shape
    for i in range(row_count):
        out_ref[pl.ds(i, channels, stride=row_count), :] = advected_ref[i]


def rim_kernel(lon_count, received_ref, given_ref, out_ref, rim_ref, sem):
    del given_ref
    channels, row_count, lanes = out_ref.shape
    lon = lax.axis_index("lon")

    @pl.when((lon == 0) | (lon == lon_count - 1))
    def _():
        entries = received_ref.shape[0] // 2
        other = (1 - lax.axis_index("panel")) * entries
        values = received_ref[pl.ds(other, entries), :]
        lane = lane_iota((entries, lanes))
        chosen = []
        for q in range(lanes // FIELD):
            at = q * FIELD + channels
            place = values[:, at : at + 1].astype(jnp.int32)
            chosen.append(jnp.where(lane == place, 1.0, 0.0))
        spread = lax.dot_general(
            values,
            jnp.concatenate(chosen, axis=1),
            (((0,), (0,)), ((), ())),
            precision=lax.Precision.HIGHEST,
            preferred_element_type=jnp.float32,
        )
        rim = spread[0:channels, 0:lanes]
        for q in range(1, lanes // FIELD):
            rim = rim + spread[q * FIELD : q * FIELD + channels, q * lanes : (q + 1) * lanes]
        rim_ref[...] = rim.reshape(channels, 1, lanes)
        row = jnp.where(lon == 0, 0, row_count - 1)
        copy = pltpu.make_async_copy(rim_ref, out_ref.at[:, pl.ds(row, 1), :], sem)
        copy.start()
        copy.wait()


def f32(*shape):
    return jax.ShapeDtypeStruct(shape, jnp.float32)


def swap(array, axis, first):
    pairs = []
    for i in range(first, lax.axis_size(axis) - 1, 2):
        pairs += [(i, i + 1), (i + 1, i)]
    return lax.ppermute(array, axis, pairs)


def body(fields, offsets, fractions, send_count, send_owner, send_cell, send_target, send_frac):
    _, channels, row_count, lanes = fields.shape
    groups = (LOW + row_count + LOW) // GROUP
    tiles = row_count // TILE
    lon_count = lax.axis_size("lon")
    slots = send_owner.shape[-1]
    width = slots // 2 * FIELD
    ext = LOW + row_count + HIGH

    ends = f32(HIGH, channels, lanes)
    lon_first, lon_second = pl.pallas_call(
        ends_kernel,
        out_shape=(ends, ends),
        in_specs=[HBM],
        out_specs=(VMEM, VMEM),
        scratch_shapes=[
            pltpu.VMEM((channels, LOW, lanes), jnp.float32),
            pltpu.VMEM((channels, LOW, lanes), jnp.float32),
            pltpu.VMEM((channels, HIGH - LOW, lanes), jnp.float32),
            pltpu.SemaphoreType.DMA((3,)),
        ],
        compiler_params=params(2),
        name="ends",
    )(pltpu.with_memory_space_constraint(fields[0], pltpu.HBM))
    lon_first = swap(lon_first, "lon", FIRST["lon"])
    lon_second = swap(lon_second, "lon", 1 - FIRST["lon"])
    arguments = (
        fractions[0],
        offsets[0].transpose(0, 2, 1),
        send_owner[0, 0],
        send_cell[0, 0],
        send_target[0, 0],
        send_frac[0, 0, 0],
        fields.reshape(channels * row_count, lanes),
    )
    part = f32(groups, channels, lanes)
    rows, first, last, ninth, weights, whole, real = pl.pallas_call(
        own_kernel,
        out_shape=(
            f32(row_count, channels, lanes),
            part,
            part,
            part,
            f32(8, row_count, lanes),
            jax.ShapeDtypeStruct((8, lanes), jnp.int32),
            f32(8, lanes),
        ),
        in_specs=[pl.BlockSpec(memory_space=pltpu.SMEM)] + [HBM] * 7,
        out_specs=(VMEM,) * 7,
        scratch_shapes=[pltpu.VMEM(given.shape, given.dtype) for given in arguments]
        + [pltpu.SemaphoreType.DMA((7,))],
        cost_estimate=pl.CostEstimate(flops=400000, bytes_accessed=800000, transcendentals=0),
        compiler_params=params(4),
        name="own",
    )(send_count[0], *[pltpu.with_memory_space_constraint(given, pltpu.HBM) for given in arguments])
    strips = f32(groups + 1, channels, lanes)
    lat_first, lat_second = pl.pallas_call(
        sides_kernel,
        out_shape=(strips, strips),
        in_specs=[VMEM] * 5,
        out_specs=(VMEM, VMEM),
        compiler_params=params(2),
        name="sides",
    )(lon_first, lon_second, first, last, ninth)
    lat_first = swap(lat_first, "lat", FIRST["lat"])
    lat_second = swap(lat_second, "lat", 1 - FIRST["lat"])
    centers = pl.pallas_call(
        center_kernel,
        out_shape=f32(tiles, 4, WINDOW, channels, lanes),
        in_specs=[VMEM] * 4,
        out_specs=VMEM,
        scratch_shapes=[
            pltpu.VMEM((ext, channels, lanes), jnp.float32),
            pltpu.SMEM((8, lanes), jnp.int32),
            pltpu.SemaphoreType.DMA(()),
        ],
        cost_estimate=pl.CostEstimate(flops=400000, bytes_accessed=3000000, transcendentals=0),
        compiler_params=params(4),
        name="centers",
    )(whole, rows, lon_first, lon_second)
    advected, message = pl.pallas_call(
        functools.partial(advect_kernel, slots),
        out_shape=(
            f32(row_count, channels, lanes),
            f32(2 * lon_count * width // lanes, lanes),
        ),
        in_specs=[VMEM] * 6,
        out_specs=(VMEM, VMEM),
        scratch_shapes=[
            pltpu.VMEM((groups + 1, channels, lanes), jnp.float32),
            pltpu.VMEM((groups + 1, channels, lanes), jnp.float32),
            pltpu.VMEM((groups + 1, channels, lanes), jnp.float32),
            pltpu.VMEM((tiles, 4, WINDOW, channels, lanes), jnp.float32),
            pltpu.SMEM((8, lanes), jnp.int32),
            pltpu.SMEM((8, lanes), jnp.float32),
            pltpu.SemaphoreType.DMA((2,)),
        ],
        compiler_params=params(8),
        name="advect",
    )(whole, real, centers, weights, lat_first, lat_second)
    received = lax.all_to_all(
        message.reshape(2 * lon_count, 1, width), ("panel", "lon"), 0, 0, tiled=True
    )
    columns = pl.pallas_call(
        column_kernel,
        out_shape=f32(channels * row_count, lanes),
        in_specs=[VMEM],
        out_specs=VMEM,
        cost_estimate=pl.CostEstimate(flops=0, bytes_accessed=2000000, transcendentals=0),
        compiler_params=params(2),
        name="columns",
    )(advected)
    out = pl.pallas_call(
        functools.partial(rim_kernel, lon_count),
        out_shape=f32(channels, row_count, lanes),
        in_specs=[VMEM, ANY],
        out_specs=ANY,
        scratch_shapes=[
            pltpu.VMEM((channels, 1, lanes), jnp.float32),
            pltpu.SemaphoreType.DMA(()),
        ],
        input_output_aliases={1: 0},
        compiler_params=params(2),
        name="rim",
    )(received.reshape(message.shape), columns.reshape(channels, row_count, lanes))
    return out[None]


def solution(mesh):
    placed = (
        P("panel", None, "lon", "lat"),
        P("panel", None, "lon", "lat"),
        P("panel", None, "lon", "lat"),
        P("panel", "lon", "lat"),
        P("panel", "lon", "lat", None),
        P("panel", "lon", "lat", None),
        P("panel", "lon", "lat", None),
        P("panel", "lon", "lat", None, None),
    )
    return jax.shard_map(
        body, mesh=mesh, in_specs=placed, out_specs=P("panel", None, "lon", "lat"), check_vma=False
    )
```

time: 48.2 us -> 46 us (0.954)
  Pallas kernels: 5.52 us -> 8.54 us
  waiting for transfers between devices: 12.5 us -> 10.6 us
  local copies, waits for them, and re-layouts: 1.68 us -> 0 us
  starting transfers between devices: 27.4 us -> 25.8 us
    all_to_all x1, starting transfers between devices: 14.4 us -> 9.96 us  [body(): lax.all_to_all(message.reshape(2 * lon_count, 1, width), ('panel', 'lon')...]
    pallas_call x3 -> x4, Pallas kernels: 0.9 us -> 4 us  [the longest x1 1.47 us: body(): pl.pallas_call(own_kernel, out_shape=(f32(row_count, channels, lanes), pa...]
    ppermute x4, starting transfers between devices: 13 us -> 15.8 us  [swap(): return lax.ppermute(array, axis, pairs)]
    ppermute x4, waiting for transfers between devices: 3.29 us -> 1.43 us  [swap(): return lax.ppermute(array, axis, pairs)]
    unnamed x14 -> x0, local copies, waits for them, and re-layouts: 1.68 us -> none
  transfers between devices with their start and end apart: 5 -> 5, of which waited for: 3 -> 3; matrix products, arithmetic and copies ran while one was open for 0% -> 0% of each run, Pallas kernels for 3% -> 8%
where the time goes in v4:
time: 46 us; the launch traced here: 45.7 us
  starting transfers between devices  25.8 us (56%)
  waiting for transfers between devices  10.6 us (23%)
  Pallas kernels  8.54 us (19%)
  between operations  0.74 us (2%)
    ppermute x4, starting transfers between devices, swap(): return lax.ppermute(array, axis, pairs)  15.8 us
    all_to_all x1, starting transfers between devices, body(): lax.all_to_all(message.reshape(2 * lon_count, 1, width), ('panel', 'lon')...  9.96 us
    all_to_all x1, waiting for transfers between devices, body(): lax.all_to_all(message.reshape(2 * lon_count, 1, width), ('panel', 'lon')...  9.17 us
    pallas_call x1, Pallas kernels, body(): pl.pallas_call(functools.partial(advect_kernel, slots), out_shape=(f32(ro...  2.34 us
    pallas_call x1, Pallas kernels, body(): pl.pallas_call(own_kernel, out_shape=(f32(row_count, channels, lanes), pa...  1.47 us
    ppermute x4, waiting for transfers between devices, swap(): return lax.ppermute(array, axis, pairs)  1.43 us
    pallas_call x1, Pallas kernels, body(): pl.pallas_call(center_kernel, out_shape=f32(tiles, 4, WINDOW, channels, l...  1.24 us
    pallas_call x1, Pallas kernels, body(): pl.pallas_call(ends_kernel, out_shape=(ends, ends), in_specs=[HBM], out_s...  1.12 us
  transfers between devices with their start and end apart: 5, of which 3 were waited for; matrix products, arithmetic and copies ran while one was open for 0% of the time, Pallas kernels for 8%

profile of v4, /device:TPU:192, one launch (start us, length us, event | category | flops | bytes accessed | tf_op | source)
XLA Modules:
  0.0 45.7 jit_solution(15375994536249319338)
XLA Ops:
  0.0 1.1 %ends.1 = (f32[9,24,128]{2,1,0:T(8,128)S(1)}, f32[9,24,128]{2,1,0:T(8,128)S(1)}) custom-call(f32[24,32,128]{2,1,0:T(8,128)} %bitcast.17), custom_call_target="tpu_custom_call" | custom-call | tf_op jit(solution)/shard_map/ends/pallas_call | solution.py:318
  1.1 0.7 %collective-permute-start = (f32[9,24,128]{2,1,0:T(8,128)S(1)}, f32[9,24,128]{2,1,0:T(8,128)S(1)}, u32[]{:S(2)}, u32[]{:S(2)}) collective-permute-start(f32[9,24,128]{2,1,0:T(8,128)S(1)} %get-tuple-element.21), channel_id=1, source_target_pairs={{8,16},{16,8},{24,32},{32,24},{40,48},{48,40},{56,64},{64,56},{72,... | collective-permute-start | bytes 331784 | tf_op jit(solution)/shard_map/ppermute | solution.py:305
  1.8 6.3 %collective-permute-start.1 = (f32[9,24,128]{2,1,0:T(8,128)S(1)}, f32[9,24,128]{2,1,0:T(8,128)S(1)}, u32[]{:S(2)}, u32[]{:S(2)}) collective-permute-start(f32[9,24,128]{2,1,0:T(8,128)S(1)} %get-tuple-element.22), channel_id=1, source_target_pairs={{0,8},{8,0},{16,24},{24,16},{32,40},{40,32},{48,56},{56,48},{64,72... | collective-permute-start | bytes 331784 | tf_op jit(solution)/shard_map/ppermute | solution.py:305
  8.8 1.5 %own.1 = (f32[32,24,128]{2,1,0:T(8,128)S(1)}, f32[3,24,128]{2,1,0:T(8,128)S(1)}, f32[3,24,128]{2,1,0:T(8,128)S(1)}, f32[3,24,128]{2,1,0:T(8,128)S(1)}, f32[8,32,...) custom-call(s32[1,1]{1,0:T(1,128)} %bitcast.15.refs_0_, f32[2,32,128]{2,1,0:T(8,128)} %bitcast.20, ...), custom_call_target="tpu_custom_call" | custom-call | flops 400000 | bytes 800000 | tf_op jit(solution)/shard_map/own/pallas_call | solution.py:344
  10.2 0.0 collective-permute-done.from_first_ref
  10.3 0.6 %collective-permute-done.1.from_second_ref = f32[9,24,128]{2,1,0:T(8,128)S(1)} collective-permute-done((f32[9,24,128]{2,1,0:T(8,128)S(1)}, f32[9,24,128]{2,1,0:T(8,128)S(1)}, u32[]{:S(2)}, u32[]{:S(2)}) %collective-permute-start.1) | collective-permute-done | bytes 110624 | tf_op jit(solution)/shard_map/ppermute | solution.py:305
  10.9 0.2 sides.1
  11.0 1.9 %collective-permute-start.2 = (f32[4,24,128]{2,1,0:T(8,128)S(1)}, f32[4,24,128]{2,1,0:T(8,128)S(1)}, u32[]{:S(2)}, u32[]{:S(2)}) collective-permute-start(f32[4,24,128]{2,1,0:T(8,128)S(1)} %get-tuple-element.27), channel_id=1, source_target_pairs={{0,1},{1,0},{2,3},{3,2},{4,5},{5,4},{6,7},{7,6},{8,9},{9,8},{10,11... | collective-permute-start | bytes 147464 | tf_op jit(solution)/shard_map/ppermute | solution.py:305
  13.0 7.0 %collective-permute-start.3 = (f32[4,24,128]{2,1,0:T(8,128)S(1)}, f32[4,24,128]{2,1,0:T(8,128)S(1)}, u32[]{:S(2)}, u32[]{:S(2)}) collective-permute-start(f32[4,24,128]{2,1,0:T(8,128)S(1)} %get-tuple-element.28), channel_id=1, source_target_pairs={{1,2},{2,1},{3,4},{4,3},{5,6},{6,5},{9,10},{10,9},{11,12},{12,11},... | collective-permute-start | bytes 147464 | tf_op jit(solution)/shard_map/ppermute | solution.py:305
  19.9 1.2 %centers.1.centers_ref = f32[4,4,11,24,128]{4,3,2,1,0:T(8,128)S(1)} custom-call(s32[8,128]{1,0:T(8,128)S(1)} %get-tuple-element.18.whole_ref, f32[32,24,128]{2,1,0:T(8,128)S(1)} %get-tuple-element.20.rows_ref, f32[9,24,128]{2,1,0:T(8,128)S(1)} %collective-permute-done.from_first_ref, f32[9,24,128]{2,1,0:T(8,128)S(1)} %collective-permute-done.1.from_second_ref), custom_call_target="tpu_custom_call" | custom-call | flops 400000 | bytes 3000000 | tf_op jit(solution)/shard_map/centers/pallas_call | solution.py:374
  21.2 0.0 collective-permute-done.2.from_first_ref
  21.2 0.8 %collective-permute-done.3.from_second_ref = f32[4,24,128]{2,1,0:T(8,128)S(1)} collective-permute-done((f32[4,24,128]{2,1,0:T(8,128)S(1)}, f32[4,24,128]{2,1,0:T(8,128)S(1)}, u32[]{:S(2)}, u32[]{:S(2)}) %collective-permute-start.3) | collective-permute-done | bytes 49184 | tf_op jit(solution)/shard_map/ppermute | solution.py:305
  22.0 2.3 %advect.1 = (f32[32,24,128]{2,1,0:T(8,128)S(1)}, f32[128,128]{1,0:T(8,128)}) custom-call(s32[8,128]{1,0:T(8,128)S(1)} %get-tuple-element.18.whole_ref, f32[8,128]{1,0:T(8,128)S(1)} %get-tuple-element.19.real_ref, f32[4,4,11,24,128]{4,3,2,1,0:T(8,128)S(1)} %centers.1.centers_ref, f32[8,32,128]{2,1,0:T(8,128)S(1)} %get-tuple-element.23.weights_ref, ...), custom_call_target="tpu_custom_call" | custom-call | tf_op jit(solution)/shard_map/advect/pallas_call | solution.py:388
  24.3 10.0 %all-to-all-start = ((f32[64,1,256]{2,1,0:T(1,128)}), f32[64,1,256]{2,1,0:T(1,128)S(1)}, u32[]{:S(2)}, u32[]{:S(2)}) async-start(f32[64,1,256]{2,1,0:T(1,128)} %bitcast.10), calls=%async_computation | async-start | bytes 131072 | tf_op jit(solution)/shard_map/all_to_all | solution.py:408
  34.3 1.1 %columns.1 = f32[768,128]{1,0:T(8,128)} custom-call(f32[32,24,128]{2,1,0:T(8,128)S(1)} %get-tuple-element.30.advected_ref), custom_call_target="tpu_custom_call" | custom-call | bytes 2000000 | tf_op jit(solution)/shard_map/columns/pallas_call | solution.py:411
  35.4 9.2 %all-to-all-done = f32[64,1,256]{2,1,0:T(1,128)S(1)} async-done(((f32[64,1,256]{2,1,0:T(1,128)}), f32[64,1,256]{2,1,0:T(1,128)S(1)}, u32[]{:S(2)}, u32[]{:S(2)}) %all-to-all-start) | async-done | bytes 65568 | tf_op jit(solution)/shard_map/all_to_all | solution.py:408
  44.6 1.1 %rim.1 = f32[24,32,128]{2,1,0:T(8,128)} custom-call(f32[128,128]{1,0:T(8,128)S(1)} %bitcast.16, f32[24,32,128]{2,1,0:T(8,128)} %bitcast.19), custom_call_target="tpu_custom_call", output_to_operand_aliasing={{}: (1, {})} | custom-call | tf_op jit(solution)/shard_map/rim/pallas_call | solution.py:420
Async XLA Ops:
  1.1 9.1 %collective-permute-start = (f32[9,24,128]{2,1,0:T(8,128)S(1)}, f32[9,24,128]{2,1,0:T(8,128)S(1)}, u32[]{:S(2)}, u32[]{:S(2)}) collective-permute-start(f32[9,24,128]{2,1,0:T(8,128)S(1)} %get-tuple-element.21), channel_id=1, source_target_pairs={{8,16},{16,8},{24,32},{32,24},{40,48},{48,40},{56,64},{64,56},{72,... | collective-permute-start | bytes 331784 | tf_op jit(solution)/shard_map/ppermute | solution.py:305
  1.8 9.1 %collective-permute-start.1 = (f32[9,24,128]{2,1,0:T(8,128)S(1)}, f32[9,24,128]{2,1,0:T(8,128)S(1)}, u32[]{:S(2)}, u32[]{:S(2)}) collective-permute-start(f32[9,24,128]{2,1,0:T(8,128)S(1)} %get-tuple-element.22), channel_id=1, source_target_pairs={{0,8},{8,0},{16,24},{24,16},{32,40},{40,32},{48,56},{56,48},{64,72... | collective-permute-start | bytes 331784 | tf_op jit(solution)/shard_map/ppermute | solution.py:305
  11.0 10.1 %collective-permute-start.2 = (f32[4,24,128]{2,1,0:T(8,128)S(1)}, f32[4,24,128]{2,1,0:T(8,128)S(1)}, u32[]{:S(2)}, u32[]{:S(2)}) collective-permute-start(f32[4,24,128]{2,1,0:T(8,128)S(1)} %get-tuple-element.27), channel_id=1, source_target_pairs={{0,1},{1,0},{2,3},{3,2},{4,5},{5,4},{6,7},{7,6},{8,9},{9,8},{10,11... | collective-permute-start | bytes 147464 | tf_op jit(solution)/shard_map/ppermute | solution.py:305
  13.0 9.0 %collective-permute-start.3 = (f32[4,24,128]{2,1,0:T(8,128)S(1)}, f32[4,24,128]{2,1,0:T(8,128)S(1)}, u32[]{:S(2)}, u32[]{:S(2)}) collective-permute-start(f32[4,24,128]{2,1,0:T(8,128)S(1)} %get-tuple-element.28), channel_id=1, source_target_pairs={{1,2},{2,1},{3,4},{4,3},{5,6},{6,5},{9,10},{10,9},{11,12},{12,11},... | collective-permute-start | bytes 147464 | tf_op jit(solution)/shard_map/ppermute | solution.py:305
  24.3 20.2 %all-to-all-start = ((f32[64,1,256]{2,1,0:T(1,128)}), f32[64,1,256]{2,1,0:T(1,128)S(1)}, u32[]{:S(2)}, u32[]{:S(2)}) async-start(f32[64,1,256]{2,1,0:T(1,128)} %bitcast.10), calls=%async_computation | async-start | bytes 131072 | tf_op jit(solution)/shard_map/all_to_all | solution.py:408

commit v5 on v4

--- a/solution.py
+++ b/solution.py
@@ -15,15 +15,25 @@
 PITCH = 8
 GROUP = LANES // PITCH
 FIRST = {"lon": 1, "lat": 0}
+ROOT = (1, 20)
 FIELD = 32
 
 VMEM = pl.BlockSpec(memory_space=pltpu.VMEM)
 ANY = pl.BlockSpec(memory_space=pl.ANY)
 HBM = pl.BlockSpec(memory_space=pltpu.HBM)
+SMEM = pl.BlockSpec(memory_space=pltpu.SMEM)
 
 
 def lane_iota(shape):
     return lax.broadcasted_iota(jnp.int32, shape, len(shape) - 1)
+
+
+def place_of(panel, lon, lon_count):
+    return (panel ^ ROOT[0]) * lon_count + (lon + lon_count - ROOT[1] % lon_count) % lon_count
+
+
+def placed_in(array, space):
+    return pltpu.with_memory_space_constraint(array, space)
 
 
 def up_first(axis):
@@ -66,16 +76,27 @@
         ninth[g] = jnp.where(lane == (base + PITCH) % LANES, turned, ninth[g])
 
 
-def own_kernel(*refs):
-    count_ref, given, outputs, held, sems = refs[0], refs[1:8], refs[8:15], refs[15:22], refs[22]
-    rows_ref, first_ref, last_ref, ninth_ref, weights_ref, whole_ref, real_ref = outputs
-    fractions_ref, offsets_ref, owner_ref, cell_ref, target_ref, frac_ref, cells_ref = held
-    copies = [pltpu.make_async_copy(given[n], held[n], sems.at[n]) for n in range(7)]
+def own_kernel(
+    count_ref, fractions_in, cells_in, offsets_in, owner_in, cell_in, target_in, frac_in,
+    rows_ref, first_ref, last_ref, ninth_ref, weights_ref,
+    count_out, offsets_out, owner_out, cell_out, target_out, frac_out,
+    fractions_ref, cells_ref, sems,
+):
+    moves = (
+        (cells_in, cells_ref),
+        (fractions_in, fractions_ref),
+        (offsets_in, offsets_out),
+        (owner_in, owner_out),
+        (cell_in, cell_out),
+        (target_in, target_out),
+        (frac_in, frac_out),
+    )
+    copies = [pltpu.make_async_copy(*move, sems.at[n]) for n, move in enumerate(moves)]
     for copy in copies:
         copy.start()
+    count_out[0, 0] = count_ref[0, 0]
     row_count, channels, lanes = rows_ref.shape
-    for copy in copies:
-        copy.wait()
+    copies[0].wait()
     rows = []
     for i in range(row_count):
         row = cells_ref[pl.ds(i, channels, stride=row_count), :]
@@ -86,20 +107,15 @@
     pack(rows, first, last, ninth)
     for g in range(first_ref.shape[0]):
         first_ref[g], last_ref[g], ninth_ref[g] = first[g], last[g], ninth[g]
+    copies[1].wait()
     for axis in range(2):
         x = fractions_ref[axis]
         weights_ref[4 * axis] = -x * (x - 1.0) * (x - 2.0) / 6.0
         weights_ref[4 * axis + 1] = (x + 1.0) * (x - 1.0) * (x - 2.0) / 2.0
         weights_ref[4 * axis + 2] = -(x + 1.0) * x * (x - 2.0) / 2.0
         weights_ref[4 * axis + 3] = (x + 1.0) * x * (x - 1.0) / 6.0
-    tiles, slots = offsets_ref.shape[2], owner_ref.shape[1]
-    whole_ref[0:1, 0:tiles] = offsets_ref[0]
-    whole_ref[1:2, 0:tiles] = offsets_ref[1]
-    whole_ref[2:3, :] = jnp.full((1, lanes), count_ref[0, 0], jnp.int32)
-    whole_ref[3:4, 0:slots] = owner_ref[...]
-    whole_ref[4:5, 0:slots] = cell_ref[...]
-    whole_ref[5:6, 0:slots] = target_ref[...]
-    real_ref[0:2, 0:slots] = frac_ref[...]
+    for copy in copies[2:]:
+        copy.wait()
 
 
 def sides_kernel(
@@ -129,43 +145,35 @@
         second_step_ref[g] = jnp.where(up, first[g], last[g])
 
 
-def shift_of(ints_ref, t, b):
-    return ints_ref[1, t] - 1 + b
+def shift_of(offsets_ref, t, b):
+    return offsets_ref[1, 0, t] - 1 + b
 
 
 def center_kernel(
-    whole_ref, rows_ref, from_first_ref, from_second_ref, centers_ref, ext_ref, ints_ref, sem
+    offsets_ref, rows_ref, from_first_ref, from_second_ref, centers_ref, ext_ref
 ):
     row_count, _, _ = rows_ref.shape
-    copy = pltpu.make_async_copy(whole_ref, ints_ref, sem)
-    copy.start()
     up = up_first("lon")
     for i in range(LOW):
         ext_ref[i] = jnp.where(up, from_second_ref[i], from_first_ref[i])
     ext_ref[LOW : LOW + row_count] = rows_ref[...]
     for i in range(HIGH):
         ext_ref[LOW + row_count + i] = jnp.where(up, from_first_ref[i], from_second_ref[i])
-    copy.wait()
     for t in range(row_count // TILE):
-        start = t * TILE + LOW - 1 + ints_ref[0, t]
+        start = t * TILE + LOW - 1 + offsets_ref[0, 0, t]
         for b in range(4):
-            turn = (LANES - shift_of(ints_ref, t, b)) & (LANES - 1)
+            turn = (LANES - shift_of(offsets_ref, t, b)) & (LANES - 1)
             for j in range(WINDOW):
                 centers_ref[t, b, j] = pltpu.roll(ext_ref[start + j], turn, 1)
 
 
 def advect_kernel(
-    slots, whole_ref, real_ref, centers_ref, weights_ref, from_first_ref, from_second_ref,
+    count_ref, offsets_ref, owner_ref, cell_ref, target_ref, frac_ref, centers_ref, weights_ref, from_first_ref, from_second_ref,
     advected_ref, message_ref,
-    east_ref, west_ref, ninth_ref, shifted_ref, ints_ref, frac_ref, sems,
+    east_ref, west_ref, ninth_ref, shifted_ref,
 ):
     row_count, channels, lanes = advected_ref.shape
-    copies = [
-        pltpu.make_async_copy(whole_ref, ints_ref, sems.at[0]),
-        pltpu.make_async_copy(real_ref, frac_ref, sems.at[1]),
-    ]
-    for copy in copies:
-        copy.start()
+    slots = owner_ref.shape[1]
     lane = lane_iota((channels, lanes))
     up = up_first("lat")
     groups = east_ref.shape[0] - 1
@@ -180,13 +188,11 @@
     last_row = jnp.where(lane < 5, pltpu.roll(mixed, LANES - 3, 1), pltpu.roll(mixed, LANES - 6, 1))
     east_ref[groups] = last_row
     ninth_ref[groups] = last_row
-    for copy in copies:
-        copy.wait()
 
     within = lane & (PITCH - 1)
     for t in range(row_count // TILE):
-        offset_lat = ints_ref[1, t]
-        start = t * TILE + LOW - 1 + ints_ref[0, t]
+        offset_lat = offsets_ref[1, 0, t]
+        start = t * TILE + LOW - 1 + offsets_ref[0, 0, t]
         from_east = within < offset_lat + 2
         for j in range(WINDOW):
             e = start + j
@@ -194,7 +200,7 @@
             packed = jnp.where(from_east, east_ref[g], west_ref[g])
             beyond = jnp.where(offset_lat + 2 == HIGH, (base + PITCH) & (LANES - 1), -1)
             for b in range(4):
-                shift = shift_of(ints_ref, t, b)
+                shift = shift_of(offsets_ref, t, b)
                 inside = (lane >= -shift) & (lane < LANES - shift)
                 if b == 3:
                     packed = jnp.where(lane == beyond, ninth_ref[g], packed)
@@ -224,7 +230,7 @@
     taken = [jnp.int32(0), jnp.int32(0)]
     at_value = lane - channel
     for k in range(slots):
-        cell = ints_ref[4, k]
+        cell = cell_ref[0, k]
         r, c = cell >> 7, cell & (lanes - 1)
         a, b = frac_ref[0, k], frac_ref[1, k]
         near = jnp.where(one_lane == c, 1.0 - b, jnp.where(one_lane == c + 1, b, 0.0))
@@ -233,9 +239,9 @@
             axis=1,
             keepdims=True,
         )
-        live = k < ints_ref[2, 0]
-        side = (ints_ref[3, k] != 0).astype(jnp.int32)
-        target = ints_ref[5, k].astype(jnp.float32)
+        live = k < count_ref[0, 0]
+        side = (owner_ref[0, k] != 0).astype(jnp.int32)
+        target = target_ref[0, k].astype(jnp.float32)
         position = jnp.where(side == 0, taken[0], taken[1])
         taken[0] = taken[0] + jnp.where(live & (side == 0), 1, 0)
         taken[1] = taken[1] + jnp.where(live & (side == 1), 1, 0)
@@ -246,12 +252,12 @@
             sums[h] = jnp.where(at_value == lane_base, value, sums[h])
             places[h] = jnp.where(one_lane == lane_base + channels, target, places[h])
     lon_count = message_ref.shape[0] // (2 * halves)
-    other = (1 - lax.axis_index("panel")) * lon_count
+    other = 1 - lax.axis_index("panel")
     message_ref[...] = jnp.zeros_like(message_ref)
     for side in range(2):
         for h in range(halves):
             n = side * halves + h
-            row = (other + side * (lon_count - 1)) * halves + h
+            row = place_of(other, side * (lon_count - 1), lon_count) * halves + h
             message_ref[pl.ds(row, 1), :] = jnp.sum(sums[n], axis=0, keepdims=True) + places[n]
 
 
@@ -269,8 +275,8 @@
     @pl.when((lon == 0) | (lon == lon_count - 1))
     def _():
         entries = received_ref.shape[0] // 2
-        other = (1 - lax.axis_index("panel")) * entries
-        values = received_ref[pl.ds(other, entries), :]
+        other = (1 - lax.axis_index("panel")) ^ ROOT[0]
+        values = received_ref[pl.ds(other * entries, entries), :]
         lane = lane_iota((entries, lanes))
         chosen = []
         for q in range(lanes // FIELD):
@@ -328,20 +334,19 @@
         ],
         compiler_params=params(2),
         name="ends",
-    )(pltpu.with_memory_space_constraint(fields[0], pltpu.HBM))
+    )(placed_in(fields[0], pltpu.HBM))
     lon_first = swap(lon_first, "lon", FIRST["lon"])
     lon_second = swap(lon_second, "lon", 1 - FIRST["lon"])
-    arguments = (
-        fractions[0],
+    small = (
         offsets[0].transpose(0, 2, 1),
         send_owner[0, 0],
         send_cell[0, 0],
         send_target[0, 0],
         send_frac[0, 0, 0],
-        fields.reshape(channels * row_count, lanes),
     )
+    large = (fractions[0], fields.reshape(channels * row_count, lanes))
     part = f32(groups, channels, lanes)
-    rows, first, last, ninth, weights, whole, real = pl.pallas_call(
+    rows, first, last, ninth, weights, *small = pl.pallas_call(
         own_kernel,
         out_shape=(
             f32(row_count, channels, lanes),
@@ -349,17 +354,17 @@
             part,
             part,
             f32(8, row_count, lanes),
-            jax.ShapeDtypeStruct((8, lanes), jnp.int32),
-            f32(8, lanes),
+            *(pltpu.SMEM(given.shape, given.dtype) for given in (send_count[0], *small)),
         ),
-        in_specs=[pl.BlockSpec(memory_space=pltpu.SMEM)] + [HBM] * 7,
-        out_specs=(VMEM,) * 7,
-        scratch_shapes=[pltpu.VMEM(given.shape, given.dtype) for given in arguments]
+        in_specs=[SMEM] + [HBM] * 7,
+        out_specs=(VMEM,) * 5 + (SMEM,) * 6,
+        scratch_shapes=[pltpu.VMEM(given.shape, given.dtype) for given in large]
         + [pltpu.SemaphoreType.DMA((7,))],
         cost_estimate=pl.CostEstimate(flops=400000, bytes_accessed=800000, transcendentals=0),
         compiler_params=params(4),
         name="own",
-    )(send_count[0], *[pltpu.with_memory_space_constraint(given, pltpu.HBM) for given in arguments])
+    )(send_count[0], *(placed_in(given, pltpu.HBM) for given in large + small))
+    small = [placed_in(given, pltpu.SMEM) for given in small]
     strips = f32(groups + 1, channels, lanes)
     lat_first, lat_second = pl.pallas_call(
         sides_kernel,
@@ -374,39 +379,41 @@
     centers = pl.pallas_call(
         center_kernel,
         out_shape=f32(tiles, 4, WINDOW, channels, lanes),
-        in_specs=[VMEM] * 4,
+        in_specs=[SMEM] + [VMEM] * 3,
         out_specs=VMEM,
-        scratch_shapes=[
-            pltpu.VMEM((ext, channels, lanes), jnp.float32),
-            pltpu.SMEM((8, lanes), jnp.int32),
-            pltpu.SemaphoreType.DMA(()),
-        ],
+        scratch_shapes=[pltpu.VMEM((ext, channels, lanes), jnp.float32)],
         cost_estimate=pl.CostEstimate(flops=400000, bytes_accessed=3000000, transcendentals=0),
         compiler_params=params(4),
         name="centers",
-    )(whole, rows, lon_first, lon_second)
+    )(small[1], rows, lon_first, lon_second)
     advected, message = pl.pallas_call(
-        functools.partial(advect_kernel, slots),
+        advect_kernel,
         out_shape=(
             f32(row_count, channels, lanes),
             f32(2 * lon_count * width // lanes, lanes),
         ),
-        in_specs=[VMEM] * 6,
+        in_specs=[SMEM] * 6 + [VMEM] * 4,
         out_specs=(VMEM, VMEM),
         scratch_shapes=[
             pltpu.VMEM((groups + 1, channels, lanes), jnp.float32),
             pltpu.VMEM((groups + 1, channels, lanes), jnp.float32),
             pltpu.VMEM((groups + 1, channels, lanes), jnp.float32),
             pltpu.VMEM((tiles, 4, WINDOW, channels, lanes), jnp.float32),
-            pltpu.SMEM((8, lanes), jnp.int32),
-            pltpu.SMEM((8, lanes), jnp.float32),
-            pltpu.SemaphoreType.DMA((2,)),
         ],
         compiler_params=params(8),
         name="advect",
-    )(whole, real, centers, weights, lat_first, lat_second)
+    )(*small, centers, weights, lat_first, lat_second)
+    group = [0] * (2 * lon_count)
+    for panel in range(2):
+        for lon in range(lon_count):
+            group[place_of(panel, lon, lon_count)] = panel * lon_count + lon
     received = lax.all_to_all(
-        message.reshape(2 * lon_count, 1, width), ("panel", "lon"), 0, 0, tiled=True
+        message.reshape(2 * lon_count, 1, width),
+        ("panel", "lon"),
+        0,
+        0,
+        tiled=True,
+        axis_index_groups=[group],
     )
     columns = pl.pallas_call(
         column_kernel,

time: 46 us -> 41.2 us (0.90)
  waiting for transfers between devices: 10.6 us -> 3.62 us
  starting transfers between devices: 25.8 us -> 29.1 us
  Pallas kernels: 8.54 us -> 7.29 us
    all_to_all x1, waiting for transfers between devices: 9.17 us -> 1.57 us  [body(): lax.all_to_all(message.reshape(2 * lon_count, 1, width), ('panel', 'lon')...]
    all_to_all x1, starting transfers between devices: 9.96 us -> 13.3 us  [body(): lax.all_to_all(message.reshape(2 * lon_count, 1, width), ('panel', 'lon')...]
    pallas_call x1, Pallas kernels: 2.34 us -> 1.71 us  [body(): pl.pallas_call(advect_kernel, out_shape=(f32(row_count, channels, lanes),...]
    ppermute x4, waiting for transfers between devices: 1.43 us -> 2.04 us  [swap(): return lax.ppermute(array, axis, pairs)]
    pallas_call x1, Pallas kernels: 1.24 us -> 0.67 us  [body(): pl.pallas_call(center_kernel, out_shape=f32(tiles, 4, WINDOW, channels, l...]
where the time goes in v5:
time: 41.2 us; the launch traced here: 40.8 us
  starting transfers between devices  29.1 us (71%)
  Pallas kernels  7.29 us (18%)
  waiting for transfers between devices  3.62 us (9%)
  between operations  0.72 us (2%)
    ppermute x4, starting transfers between devices, swap(): return lax.ppermute(array, axis, pairs)  15.8 us
    all_to_all x1, starting transfers between devices, body(): lax.all_to_all(message.reshape(2 * lon_count, 1, width), ('panel', 'lon')...  13.3 us
    ppermute x4, waiting for transfers between devices, swap(): return lax.ppermute(array, axis, pairs)  2.04 us
    pallas_call x1, Pallas kernels, body(): pl.pallas_call(advect_kernel, out_shape=(f32(row_count, channels, lanes),...  1.71 us
    all_to_all x1, waiting for transfers between devices, body(): lax.all_to_all(message.reshape(2 * lon_count, 1, width), ('panel', 'lon')...  1.57 us
    pallas_call x1, Pallas kernels, body(): pl.pallas_call(own_kernel, out_shape=(f32(row_count, channels, lanes), pa...  1.43 us
    pallas_call x1, Pallas kernels, body(): pl.pallas_call(ends_kernel, out_shape=(ends, ends), in_specs=[HBM], out_s...  1.12 us
    pallas_call x1, Pallas kernels, body(): pl.pallas_call(column_kernel, out_shape=f32(channels * row_count, lanes),...  1.1 us
  transfers between devices with their start and end apart: 5, of which 3 were waited for; matrix products, arithmetic and copies ran while one was open for 0% of the time, Pallas kernels for 8%

profile of v5, /device:TPU:192, one launch (start us, length us, event | category | flops | bytes accessed | tf_op | source)
XLA Modules:
  0.0 40.8 jit_solution(5445641504361175104)
XLA Ops:
  0.0 1.1 %ends.1 = (f32[9,24,128]{2,1,0:T(8,128)S(1)}, f32[9,24,128]{2,1,0:T(8,128)S(1)}) custom-call(f32[24,32,128]{2,1,0:T(8,128)} %bitcast.17), custom_call_target="tpu_custom_call" | custom-call | tf_op jit(solution)/shard_map/ends/pallas_call | solution.py:324
  1.1 0.7 %collective-permute-start = (f32[9,24,128]{2,1,0:T(8,128)S(1)}, f32[9,24,128]{2,1,0:T(8,128)S(1)}, u32[]{:S(2)}, u32[]{:S(2)}) collective-permute-start(f32[9,24,128]{2,1,0:T(8,128)S(1)} %get-tuple-element.29), channel_id=1, source_target_pairs={{8,16},{16,8},{24,32},{32,24},{40,48},{48,40},{56,64},{64,56},{72,... | collective-permute-start | bytes 331784 | tf_op jit(solution)/shard_map/ppermute | solution.py:311
  1.8 6.3 %collective-permute-start.1 = (f32[9,24,128]{2,1,0:T(8,128)S(1)}, f32[9,24,128]{2,1,0:T(8,128)S(1)}, u32[]{:S(2)}, u32[]{:S(2)}) collective-permute-start(f32[9,24,128]{2,1,0:T(8,128)S(1)} %get-tuple-element.30), channel_id=1, source_target_pairs={{0,8},{8,0},{16,24},{24,16},{32,40},{40,32},{48,56},{56,48},{64,72... | collective-permute-start | bytes 331784 | tf_op jit(solution)/shard_map/ppermute | solution.py:311
  8.8 1.4 %own.1 = (f32[32,24,128]{2,1,0:T(8,128)S(1)}, f32[3,24,128]{2,1,0:T(8,128)S(1)}, f32[3,24,128]{2,1,0:T(8,128)S(1)}, f32[3,24,128]{2,1,0:T(8,128)S(1)}, f32[8,32,...) custom-call(s32[1,1]{1,0:T(1,128)} %bitcast.15.count_ref, ...), custom_call_target="tpu_custom_call" | custom-call | flops 400000 | bytes 800000 | tf_op jit(solution)/shard_map/own/pallas_call | solution.py:349
  10.2 0.0 collective-permute-done.from_first_ref
  10.2 0.7 %collective-permute-done.1.from_second_ref = f32[9,24,128]{2,1,0:T(8,128)S(1)} collective-permute-done((f32[9,24,128]{2,1,0:T(8,128)S(1)}, f32[9,24,128]{2,1,0:T(8,128)S(1)}, u32[]{:S(2)}, u32[]{:S(2)}) %collective-permute-start.1) | collective-permute-done | bytes 110624 | tf_op jit(solution)/shard_map/ppermute | solution.py:311
  10.9 0.2 sides.1
  11.0 1.9 %collective-permute-start.2 = (f32[4,24,128]{2,1,0:T(8,128)S(1)}, f32[4,24,128]{2,1,0:T(8,128)S(1)}, u32[]{:S(2)}, u32[]{:S(2)}) collective-permute-start(f32[4,24,128]{2,1,0:T(8,128)S(1)} %get-tuple-element.35), channel_id=1, source_target_pairs={{0,1},{1,0},{2,3},{3,2},{4,5},{5,4},{6,7},{7,6},{8,9},{9,8},{10,11... | collective-permute-start | bytes 147464 | tf_op jit(solution)/shard_map/ppermute | solution.py:311
  13.0 7.0 %collective-permute-start.3 = (f32[4,24,128]{2,1,0:T(8,128)S(1)}, f32[4,24,128]{2,1,0:T(8,128)S(1)}, u32[]{:S(2)}, u32[]{:S(2)}) collective-permute-start(f32[4,24,128]{2,1,0:T(8,128)S(1)} %get-tuple-element.36), channel_id=1, source_target_pairs={{1,2},{2,1},{3,4},{4,3},{5,6},{6,5},{9,10},{10,9},{11,12},{12,11},... | collective-permute-start | bytes 147464 | tf_op jit(solution)/shard_map/ppermute | solution.py:311
  19.9 0.7 %centers.1.centers_ref = f32[4,4,11,24,128]{4,3,2,1,0:T(8,128)S(1)} custom-call(s32[2,1,4]{2,1,0:T(1,128)S(4)} %get-tuple-element.23.offsets_ref, f32[32,24,128]{2,1,0:T(8,128)S(1)} %get-tuple-element.28.rows_ref, f32[9,24,128]{2,1,0:T(8,128)S(1)} %collective-permute-done.from_first_ref, f32[9,24,128]{2,1,0:T(8,128)S(1)} %collective-permute-done.1.from_second_ref), custom_call_target="tpu_custom_call" | custom-call | flops 400000 | bytes 3000000 | tf_op jit(solution)/shard_map/centers/pallas_call | solution.py:379
  20.6 0.0 collective-permute-done.2.from_first_ref
  20.6 1.4 %collective-permute-done.3.from_second_ref = f32[4,24,128]{2,1,0:T(8,128)S(1)} collective-permute-done((f32[4,24,128]{2,1,0:T(8,128)S(1)}, f32[4,24,128]{2,1,0:T(8,128)S(1)}, u32[]{:S(2)}, u32[]{:S(2)}) %collective-permute-start.3) | collective-permute-done | bytes 49184 | tf_op jit(solution)/shard_map/ppermute | solution.py:311
  22.0 1.7 %advect.1 = (f32[32,24,128]{2,1,0:T(8,128)S(1)}, f32[128,128]{1,0:T(8,128)}) custom-call(s32[1,1]{1,0:T(1,128)S(4)} %get-tuple-element.22.count_ref, s32[2,1,4]{2,1,0:T(1,128)S(4)} %get-tuple-element.23.offsets_ref, s32[1,16]{1,0:T(1,128)S(4)} %get-tuple-element.24.owner_ref, s32[1,16]{1,0:T(1,128)S(4)} %get-tuple-element.25.cell_ref, ...), custom_call_target="tpu_custom_call" | custom-call | tf_op jit(solution)/shard_map/advect/pallas_call | solution.py:389
  23.7 13.3 %all-to-all-start = ((f32[64,1,256]{2,1,0:T(1,128)}), f32[64,1,256]{2,1,0:T(1,128)S(1)}, u32[]{:S(2)}, u32[]{:S(2)}) async-start(f32[64,1,256]{2,1,0:T(1,128)} %bitcast.10), calls=%async_computation | async-start | bytes 131072 | tf_op jit(solution)/shard_map/all_to_all | solution.py:410
  37.0 1.1 %columns.1 = f32[768,128]{1,0:T(8,128)} custom-call(f32[32,24,128]{2,1,0:T(8,128)S(1)} %get-tuple-element.38.advected_ref), custom_call_target="tpu_custom_call" | custom-call | bytes 2000000 | tf_op jit(solution)/shard_map/columns/pallas_call | solution.py:418
  38.1 1.6 %all-to-all-done = f32[64,1,256]{2,1,0:T(1,128)S(1)} async-done(((f32[64,1,256]{2,1,0:T(1,128)}), f32[64,1,256]{2,1,0:T(1,128)S(1)}, u32[]{:S(2)}, u32[]{:S(2)}) %all-to-all-start) | async-done | bytes 65568 | tf_op jit(solution)/shard_map/all_to_all | solution.py:410
  39.7 1.1 %rim.1 = f32[24,32,128]{2,1,0:T(8,128)} custom-call(f32[128,128]{1,0:T(8,128)S(1)} %bitcast.16, f32[24,32,128]{2,1,0:T(8,128)} %bitcast.19), custom_call_target="tpu_custom_call", output_to_operand_aliasing={{}: (1, {})} | custom-call | tf_op jit(solution)/shard_map/rim/pallas_call | solution.py:427
Async XLA Ops:
  1.1 9.1 %collective-permute-start = (f32[9,24,128]{2,1,0:T(8,128)S(1)}, f32[9,24,128]{2,1,0:T(8,128)S(1)}, u32[]{:S(2)}, u32[]{:S(2)}) collective-permute-start(f32[9,24,128]{2,1,0:T(8,128)S(1)} %get-tuple-element.29), channel_id=1, source_target_pairs={{8,16},{16,8},{24,32},{32,24},{40,48},{48,40},{56,64},{64,56},{72,... | collective-permute-start | bytes 331784 | tf_op jit(solution)/shard_map/ppermute | solution.py:311
  1.8 9.1 %collective-permute-start.1 = (f32[9,24,128]{2,1,0:T(8,128)S(1)}, f32[9,24,128]{2,1,0:T(8,128)S(1)}, u32[]{:S(2)}, u32[]{:S(2)}) collective-permute-start(f32[9,24,128]{2,1,0:T(8,128)S(1)} %get-tuple-element.30), channel_id=1, source_target_pairs={{0,8},{8,0},{16,24},{24,16},{32,40},{40,32},{48,56},{56,48},{64,72... | collective-permute-start | bytes 331784 | tf_op jit(solution)/shard_map/ppermute | solution.py:311
  11.0 9.6 %collective-permute-start.2 = (f32[4,24,128]{2,1,0:T(8,128)S(1)}, f32[4,24,128]{2,1,0:T(8,128)S(1)}, u32[]{:S(2)}, u32[]{:S(2)}) collective-permute-start(f32[4,24,128]{2,1,0:T(8,128)S(1)} %get-tuple-element.35), channel_id=1, source_target_pairs={{0,1},{1,0},{2,3},{3,2},{4,5},{5,4},{6,7},{7,6},{8,9},{9,8},{10,11... | collective-permute-start | bytes 147464 | tf_op jit(solution)/shard_map/ppermute | solution.py:311
  13.0 9.0 %collective-permute-start.3 = (f32[4,24,128]{2,1,0:T(8,128)S(1)}, f32[4,24,128]{2,1,0:T(8,128)S(1)}, u32[]{:S(2)}, u32[]{:S(2)}) collective-permute-start(f32[4,24,128]{2,1,0:T(8,128)S(1)} %get-tuple-element.36), channel_id=1, source_target_pairs={{1,2},{2,1},{3,4},{4,3},{5,6},{6,5},{9,10},{10,9},{11,12},{12,11},... | collective-permute-start | bytes 147464 | tf_op jit(solution)/shard_map/ppermute | solution.py:311
  23.7 16.0 %all-to-all-start = ((f32[64,1,256]{2,1,0:T(1,128)}), f32[64,1,256]{2,1,0:T(1,128)S(1)}, u32[]{:S(2)}, u32[]{:S(2)}) async-start(f32[64,1,256]{2,1,0:T(1,128)} %bitcast.10), calls=%async_computation | async-start | bytes 131072 | tf_op jit(solution)/shard_map/all_to_all | solution.py:410

commit v6 on v5

--- a/solution.py
+++ b/solution.py
@@ -169,8 +169,8 @@
 
 def advect_kernel(
     count_ref, offsets_ref, owner_ref, cell_ref, target_ref, frac_ref, centers_ref, weights_ref, from_first_ref, from_second_ref,
-    advected_ref, message_ref,
-    east_ref, west_ref, ninth_ref, shifted_ref,
+    columns_ref, message_ref,
+    advected_ref, east_ref, west_ref, ninth_ref, shifted_ref,
 ):
     row_count, channels, lanes = advected_ref.shape
     slots = owner_ref.shape[1]
@@ -218,6 +218,7 @@
                 part = weights_ref[a, row : row + 1, :] * inner
                 total = part if total is None else total + part
             advected_ref[row] = total
+            columns_ref[pl.ds(row, channels, stride=row_count), :] = total
 
     channel = lax.broadcasted_iota(jnp.int32, (channels, lanes), 0)
     one_lane = lane_iota((1, lanes))
@@ -261,16 +262,23 @@
             message_ref[pl.ds(row, 1), :] = jnp.sum(sums[n], axis=0, keepdims=True) + places[n]
 
 
-def column_kernel(advected_ref, out_ref):
-    row_count, channels, _ = advected_ref.shape
-    for i in range(row_count):
-        out_ref[pl.ds(i, channels, stride=row_count), :] = advected_ref[i]
-
-
-def rim_kernel(lon_count, received_ref, given_ref, out_ref, rim_ref, sem):
-    del given_ref
+def finish_kernel(lon_count, received_ref, columns_ref, out_ref, held_ref, sems):
     channels, row_count, lanes = out_ref.shape
+    tiles = row_count // TILE
     lon = lax.axis_index("lon")
+
+    def tile_of(ref, t):
+        return ref.at[:, pl.ds(pl.multiple_of(t * TILE, TILE), TILE), :]
+
+    changed = jnp.where(lon == 0, 0, tiles - 1)
+    copies = []
+    for n in range(tiles - 1):
+        t = n + jnp.where(lon == 0, 1, 0)
+        copies.append(
+            pltpu.make_async_copy(tile_of(columns_ref, t), tile_of(out_ref, t), sems.at[n])
+        )
+        copies[n].start()
+    held_ref[...] = columns_ref[:, pl.ds(pl.multiple_of(changed * TILE, TILE), TILE), :]
 
     @pl.when((lon == 0) | (lon == lon_count - 1))
     def _():
@@ -293,10 +301,12 @@
         rim = spread[0:channels, 0:lanes]
         for q in range(1, lanes // FIELD):
             rim = rim + spread[q * FIELD : q * FIELD + channels, q * lanes : (q + 1) * lanes]
-        rim_ref[...] = rim.reshape(channels, 1, lanes)
-        row = jnp.where(lon == 0, 0, row_count - 1)
-        copy = pltpu.make_async_copy(rim_ref, out_ref.at[:, pl.ds(row, 1), :], sem)
-        copy.start()
+        row = jnp.where(lon == 0, 0, TILE - 1)
+        held_ref[:, pl.ds(row, 1), :] = rim.reshape(channels, 1, lanes)
+
+    copies.append(pltpu.make_async_copy(held_ref, tile_of(out_ref, changed), sems.at[tiles - 1]))
+    copies[tiles - 1].start()
+    for copy in copies:
         copy.wait()
 
 
@@ -386,15 +396,16 @@
         compiler_params=params(4),
         name="centers",
     )(small[1], rows, lon_first, lon_second)
-    advected, message = pl.pallas_call(
+    columns, message = pl.pallas_call(
         advect_kernel,
         out_shape=(
-            f32(row_count, channels, lanes),
+            pltpu.VMEM((channels * row_count, lanes), jnp.float32),
             f32(2 * lon_count * width // lanes, lanes),
         ),
         in_specs=[SMEM] * 6 + [VMEM] * 4,
         out_specs=(VMEM, VMEM),
         scratch_shapes=[
+            pltpu.VMEM((row_count, channels, lanes), jnp.float32),
             pltpu.VMEM((groups + 1, channels, lanes), jnp.float32),
             pltpu.VMEM((groups + 1, channels, lanes), jnp.float32),
             pltpu.VMEM((groups + 1, channels, lanes), jnp.float32),
@@ -415,27 +426,17 @@
         tiled=True,
         axis_index_groups=[group],
     )
-    columns = pl.pallas_call(
-        column_kernel,
-        out_shape=f32(channels * row_count, lanes),
-        in_specs=[VMEM],
-        out_specs=VMEM,
-        cost_estimate=pl.CostEstimate(flops=0, bytes_accessed=2000000, transcendentals=0),
+    out = pl.pallas_call(
+        functools.partial(finish_kernel, lon_count),
+        out_shape=pltpu.HBM((channels, row_count, lanes), jnp.float32),
+        in_specs=[VMEM, VMEM],
+        out_specs=HBM,
+        scratch_shapes=[
+            pltpu.VMEM((channels, TILE, lanes), jnp.float32),
+            pltpu.SemaphoreType.DMA((tiles,)),
+        ],
         compiler_params=params(2),
-        name="columns",
-    )(advected)
-    out = pl.pallas_call(
-        functools.partial(rim_kernel, lon_count),
-        out_shape=f32(channels, row_count, lanes),
-        in_specs=[VMEM, ANY],
-        out_specs=ANY,
-        scratch_shapes=[
-            pltpu.VMEM((channels, 1, lanes), jnp.float32),
-            pltpu.SemaphoreType.DMA(()),
-        ],
-        input_output_aliases={1: 0},
-        compiler_params=params(2),
-        name="rim",
+        name="finish",
     )(received.reshape(message.shape), columns.reshape(channels, row_count, lanes))
     return out[None]
 

time: 41.2 us -> 40.8 us (level)
  blocking collectives: 0 us -> 15.8 us
  starting transfers between devices: 29.1 us -> 15.8 us
  waiting for transfers between devices: 3.62 us -> 2.04 us
  Pallas kernels: 7.29 us -> 5.92 us
    all_to_all x0 -> x1, blocking collectives: none -> 15.8 us  [body(): lax.all_to_all(message.reshape(2 * lon_count, 1, width), ('panel', 'lon')...]
    all_to_all x1 -> x0, starting transfers between devices: 13.3 us -> none  [body(): lax.all_to_all(message.reshape(2 * lon_count, 1, width), ('panel', 'lon')...]
    all_to_all x1 -> x0, waiting for transfers between devices: 1.57 us -> none  [body(): lax.all_to_all(message.reshape(2 * lon_count, 1, width), ('panel', 'lon')...]
    pallas_call x3 -> x2, Pallas kernels: 3.9 us -> 2.53 us  [the longest x1 1.36 us: body(): pl.pallas_call(advect_kernel, out_shape=(pltpu.VMEM((channels * row_count...]
  transfers between devices with their start and end apart: 5 -> 4, of which waited for: 3 -> 2; matrix products, arithmetic and copies ran while one was open for 0% -> 0% of each run, Pallas kernels for 8% -> 5%
where the time goes in v6:
time: 40.8 us; the launch traced here: 40.3 us
  starting transfers between devices  15.8 us (39%)
  blocking collectives  15.8 us (39%)
  Pallas kernels  5.92 us (15%)
  waiting for transfers between devices  2.04 us (5%)
  between operations  0.72 us (2%)
    ppermute x4, starting transfers between devices, swap(): return lax.ppermute(array, axis, pairs)  15.8 us
    all_to_all x1, blocking collectives, body(): lax.all_to_all(message.reshape(2 * lon_count, 1, width), ('panel', 'lon')...  15.8 us
    ppermute x4, waiting for transfers between devices, swap(): return lax.ppermute(array, axis, pairs)  2.04 us
    pallas_call x1, Pallas kernels, body(): pl.pallas_call(own_kernel, out_shape=(f32(row_count, channels, lanes), pa...  1.43 us
    pallas_call x1, Pallas kernels, body(): pl.pallas_call(advect_kernel, out_shape=(pltpu.VMEM((channels * row_count...  1.36 us
    pallas_call x1, Pallas kernels, body(): pl.pallas_call(functools.partial(finish_kernel, lon_count), out_shape=plt...  1.17 us
    pallas_call x1, Pallas kernels, body(): pl.pallas_call(ends_kernel, out_shape=(ends, ends), in_specs=[HBM], out_s...  1.12 us
  transfers between devices with their start and end apart: 4, of which 2 were waited for; matrix products, arithmetic and copies ran while one was open for 0% of the time, Pallas kernels for 5%

profile of v6, /device:TPU:192, one launch (start us, length us, event | category | flops | bytes accessed | tf_op | source)
XLA Modules:
  0.0 40.3 jit_solution(2261181591849486561)
XLA Ops:
  0.0 1.1 %ends.1 = (f32[9,24,128]{2,1,0:T(8,128)S(1)}, f32[9,24,128]{2,1,0:T(8,128)S(1)}) custom-call(f32[24,32,128]{2,1,0:T(8,128)} %bitcast.19), custom_call_target="tpu_custom_call" | custom-call | tf_op jit(solution)/shard_map/ends/pallas_call | solution.py:334
  1.1 0.7 %collective-permute-start = (f32[9,24,128]{2,1,0:T(8,128)S(1)}, f32[9,24,128]{2,1,0:T(8,128)S(1)}, u32[]{:S(2)}, u32[]{:S(2)}) collective-permute-start(f32[9,24,128]{2,1,0:T(8,128)S(1)} %get-tuple-element.29), channel_id=1, source_target_pairs={{8,16},{16,8},{24,32},{32,24},{40,48},{48,40},{56,64},{64,56},{72,... | collective-permute-start | bytes 331784 | tf_op jit(solution)/shard_map/ppermute | solution.py:321
  1.8 6.3 %collective-permute-start.1 = (f32[9,24,128]{2,1,0:T(8,128)S(1)}, f32[9,24,128]{2,1,0:T(8,128)S(1)}, u32[]{:S(2)}, u32[]{:S(2)}) collective-permute-start(f32[9,24,128]{2,1,0:T(8,128)S(1)} %get-tuple-element.30), channel_id=1, source_target_pairs={{0,8},{8,0},{16,24},{24,16},{32,40},{40,32},{48,56},{56,48},{64,72... | collective-permute-start | bytes 331784 | tf_op jit(solution)/shard_map/ppermute | solution.py:321
  8.8 1.4 %own.1 = (f32[32,24,128]{2,1,0:T(8,128)S(1)}, f32[3,24,128]{2,1,0:T(8,128)S(1)}, f32[3,24,128]{2,1,0:T(8,128)S(1)}, f32[3,24,128]{2,1,0:T(8,128)S(1)}, f32[8,32,...) custom-call(s32[1,1]{1,0:T(1,128)} %bitcast.15.count_ref, ...), custom_call_target="tpu_custom_call" | custom-call | flops 400000 | bytes 800000 | tf_op jit(solution)/shard_map/own/pallas_call | solution.py:359
  10.2 0.0 collective-permute-done.from_first_ref
  10.2 0.7 %collective-permute-done.1.from_second_ref = f32[9,24,128]{2,1,0:T(8,128)S(1)} collective-permute-done((f32[9,24,128]{2,1,0:T(8,128)S(1)}, f32[9,24,128]{2,1,0:T(8,128)S(1)}, u32[]{:S(2)}, u32[]{:S(2)}) %collective-permute-start.1) | collective-permute-done | bytes 110624 | tf_op jit(solution)/shard_map/ppermute | solution.py:321
  10.9 0.2 sides.1
  11.0 1.9 %collective-permute-start.2 = (f32[4,24,128]{2,1,0:T(8,128)S(1)}, f32[4,24,128]{2,1,0:T(8,128)S(1)}, u32[]{:S(2)}, u32[]{:S(2)}) collective-permute-start(f32[4,24,128]{2,1,0:T(8,128)S(1)} %get-tuple-element.35), channel_id=1, source_target_pairs={{0,1},{1,0},{2,3},{3,2},{4,5},{5,4},{6,7},{7,6},{8,9},{9,8},{10,11... | collective-permute-start | bytes 147464 | tf_op jit(solution)/shard_map/ppermute | solution.py:321
  13.0 7.0 %collective-permute-start.3 = (f32[4,24,128]{2,1,0:T(8,128)S(1)}, f32[4,24,128]{2,1,0:T(8,128)S(1)}, u32[]{:S(2)}, u32[]{:S(2)}) collective-permute-start(f32[4,24,128]{2,1,0:T(8,128)S(1)} %get-tuple-element.36), channel_id=1, source_target_pairs={{1,2},{2,1},{3,4},{4,3},{5,6},{6,5},{9,10},{10,9},{11,12},{12,11},... | collective-permute-start | bytes 147464 | tf_op jit(solution)/shard_map/ppermute | solution.py:321
  19.9 0.7 %centers.1.centers_ref = f32[4,4,11,24,128]{4,3,2,1,0:T(8,128)S(1)} custom-call(s32[2,1,4]{2,1,0:T(1,128)S(4)} %get-tuple-element.23.offsets_ref, f32[32,24,128]{2,1,0:T(8,128)S(1)} %get-tuple-element.28.rows_ref, f32[9,24,128]{2,1,0:T(8,128)S(1)} %collective-permute-done.from_first_ref, f32[9,24,128]{2,1,0:T(8,128)S(1)} %collective-permute-done.1.from_second_ref), custom_call_target="tpu_custom_call" | custom-call | flops 400000 | bytes 3000000 | tf_op jit(solution)/shard_map/centers/pallas_call | solution.py:389
  20.6 0.0 collective-permute-done.2.from_first_ref
  20.6 1.4 %collective-permute-done.3.from_second_ref = f32[4,24,128]{2,1,0:T(8,128)S(1)} collective-permute-done((f32[4,24,128]{2,1,0:T(8,128)S(1)}, f32[4,24,128]{2,1,0:T(8,128)S(1)}, u32[]{:S(2)}, u32[]{:S(2)}) %collective-permute-start.3) | collective-permute-done | bytes 49184 | tf_op jit(solution)/shard_map/ppermute | solution.py:321
  22.0 1.4 %advect.1 = (f32[768,128]{1,0:T(8,128)S(1)}, f32[128,128]{1,0:T(8,128)S(1)}) custom-call(s32[1,1]{1,0:T(1,128)S(4)} %get-tuple-element.22.count_ref, s32[2,1,4]{2,1,0:T(1,128)S(4)} %get-tuple-element.23.offsets_ref, s32[1,16]{1,0:T(1,128)S(4)} %get-tuple-element.24.owner_ref, s32[1,16]{1,0:T(1,128)S(4)} %get-tuple-element.25.cell_ref, ...), custom_call_target="tpu_custom_call" | custom-call | tf_op jit(solution)/shard_map/advect/pallas_call | solution.py:399
  23.4 15.8 %all_to_all.5 = f32[64,1,256]{2,1,0:T(1,128)S(1)} all-to-all(f32[64,1,256]{2,1,0:T(1,128)S(1)} %bitcast.18), channel_id=1, replica_groups={{416,424,432,440,448,456,464,472,480,488,496,504,256,264,272,280,288,29..., dimensions={0} | all-to-all | bytes 131072 | tf_op jit(solution)/shard_map/all_to_all | solution.py:421
  39.1 1.2 %finish.1 = f32[24,32,128]{2,1,0:T(8,128)} custom-call(f32[128,128]{1,0:T(8,128)S(1)} %bitcast.17, f32[24,32,128]{2,1,0:T(8,128)S(1)} %bitcast.16), custom_call_target="tpu_custom_call" | custom-call | tf_op jit(solution)/shard_map/finish/pallas_call | solution.py:429
Async XLA Ops:
  1.1 9.1 %collective-permute-start = (f32[9,24,128]{2,1,0:T(8,128)S(1)}, f32[9,24,128]{2,1,0:T(8,128)S(1)}, u32[]{:S(2)}, u32[]{:S(2)}) collective-permute-start(f32[9,24,128]{2,1,0:T(8,128)S(1)} %get-tuple-element.29), channel_id=1, source_target_pairs={{8,16},{16,8},{24,32},{32,24},{40,48},{48,40},{56,64},{64,56},{72,... | collective-permute-start | bytes 331784 | tf_op jit(solution)/shard_map/ppermute | solution.py:321
  1.8 9.1 %collective-permute-start.1 = (f32[9,24,128]{2,1,0:T(8,128)S(1)}, f32[9,24,128]{2,1,0:T(8,128)S(1)}, u32[]{:S(2)}, u32[]{:S(2)}) collective-permute-start(f32[9,24,128]{2,1,0:T(8,128)S(1)} %get-tuple-element.30), channel_id=1, source_target_pairs={{0,8},{8,0},{16,24},{24,16},{32,40},{40,32},{48,56},{56,48},{64,72... | collective-permute-start | bytes 331784 | tf_op jit(solution)/shard_map/ppermute | solution.py:321
  11.0 9.6 %collective-permute-start.2 = (f32[4,24,128]{2,1,0:T(8,128)S(1)}, f32[4,24,128]{2,1,0:T(8,128)S(1)}, u32[]{:S(2)}, u32[]{:S(2)}) collective-permute-start(f32[4,24,128]{2,1,0:T(8,128)S(1)} %get-tuple-element.35), channel_id=1, source_target_pairs={{0,1},{1,0},{2,3},{3,2},{4,5},{5,4},{6,7},{7,6},{8,9},{9,8},{10,11... | collective-permute-start | bytes 147464 | tf_op jit(solution)/shard_map/ppermute | solution.py:321
  13.0 9.0 %collective-permute-start.3 = (f32[4,24,128]{2,1,0:T(8,128)S(1)}, f32[4,24,128]{2,1,0:T(8,128)S(1)}, u32[]{:S(2)}, u32[]{:S(2)}) collective-permute-start(f32[4,24,128]{2,1,0:T(8,128)S(1)} %get-tuple-element.36), channel_id=1, source_target_pairs={{1,2},{2,1},{3,4},{4,3},{5,6},{6,5},{9,10},{10,9},{11,12},{12,11},... | collective-permute-start | bytes 147464 | tf_op jit(solution)/shard_map/ppermute | solution.py:321

commit v7 on v6

--- a/solution.py
+++ b/solution.py
@@ -44,25 +44,20 @@
     return pltpu.CompilerParams(vmem_limit_bytes=mib * 1024 * 1024)
 
 
-def ends_kernel(cells_ref, first_step_ref, second_step_ref, head_ref, tail_ref, ninth_ref, sems):
+def ends_kernel(cells_ref, first_step_ref, second_step_ref, sems):
     row_count = cells_ref.shape[1]
-    copies = [
-        pltpu.make_async_copy(cells_ref.at[:, 0:LOW, :], head_ref, sems.at[0]),
-        pltpu.make_async_copy(cells_ref.at[:, row_count - LOW : row_count, :], tail_ref, sems.at[1]),
-        pltpu.make_async_copy(cells_ref.at[:, LOW:HIGH, :], ninth_ref, sems.at[2]),
-    ]
-    for copy in copies:
-        copy.start()
     up = up_first("lon")
+    copies = []
+    for step, out_ref in enumerate((first_step_ref, second_step_ref)):
+        upward = up if step == 0 else jnp.logical_not(up)
+        for i in range(HIGH):
+            row = jnp.where(upward, min(row_count - LOW + i, row_count - 1), i)
+            copies.append(
+                pltpu.make_async_copy(cells_ref.at[:, row, :], out_ref.at[i], sems.at[step, i])
+            )
+            copies[-1].start()
     for copy in copies:
         copy.wait()
-    for i in range(LOW):
-        head, tail = head_ref[:, i, :], tail_ref[:, i, :]
-        first_step_ref[i] = jnp.where(up, tail, head)
-        second_step_ref[i] = jnp.where(up, head, tail)
-    ninth = ninth_ref[:, 0, :]
-    first_step_ref[LOW] = ninth
-    second_step_ref[LOW] = ninth
 
 
 def pack(rows, first, last, ninth):
@@ -170,7 +165,7 @@
 def advect_kernel(
     count_ref, offsets_ref, owner_ref, cell_ref, target_ref, frac_ref, centers_ref, weights_ref, from_first_ref, from_second_ref,
     columns_ref, message_ref,
-    advected_ref, east_ref, west_ref, ninth_ref, shifted_ref,
+    advected_ref, east_ref, west_ref, ninth_ref,
 ):
     row_count, channels, lanes = advected_ref.shape
     slots = owner_ref.shape[1]
@@ -194,31 +189,32 @@
         offset_lat = offsets_ref[1, 0, t]
         start = t * TILE + LOW - 1 + offsets_ref[0, 0, t]
         from_east = within < offset_lat + 2
+        weights, sums = {}, {}
         for j in range(WINDOW):
             e = start + j
             g, base = e >> 4, PITCH * (e & (GROUP - 1))
             packed = jnp.where(from_east, east_ref[g], west_ref[g])
             beyond = jnp.where(offset_lat + 2 == HIGH, (base + PITCH) & (LANES - 1), -1)
+            shifted = []
             for b in range(4):
                 shift = shift_of(offsets_ref, t, b)
                 inside = (lane >= -shift) & (lane < LANES - shift)
                 if b == 3:
                     packed = jnp.where(lane == beyond, ninth_ref[g], packed)
                 halo = pltpu.roll(packed, (2 * LANES - base - shift) & (LANES - 1), 1)
-                shifted_ref[t, b, j] = jnp.where(inside, centers_ref[t, b, j], halo)
-    for t in range(row_count // TILE):
-        for i in range(TILE):
-            row = t * TILE + i
-            lat_weights = [weights_ref[4 + b, row : row + 1, :] for b in range(4)]
-            total = None
-            for a in range(4):
-                inner = lat_weights[0] * shifted_ref[t, 0, i + a]
+                shifted.append(jnp.where(inside, centers_ref[t, b, j], halo))
+            for i in range(max(j - 3, 0), min(j, TILE - 1) + 1):
+                row, a = t * TILE + i, j - i
+                if a == 0:
+                    weights[i] = [weights_ref[4 + b, row : row + 1, :] for b in range(4)]
+                inner = weights[i][0] * shifted[0]
                 for b in range(1, 4):
-                    inner = inner + lat_weights[b] * shifted_ref[t, b, i + a]
+                    inner = inner + weights[i][b] * shifted[b]
                 part = weights_ref[a, row : row + 1, :] * inner
-                total = part if total is None else total + part
-            advected_ref[row] = total
-            columns_ref[pl.ds(row, channels, stride=row_count), :] = total
+                sums[i] = part if a == 0 else sums[i] + part
+                if a == 3:
+                    advected_ref[row] = sums[i]
+                    columns_ref[pl.ds(row, channels, stride=row_count), :] = sums[i]
 
     channel = lax.broadcasted_iota(jnp.int32, (channels, lanes), 0)
     one_lane = lane_iota((1, lanes))
@@ -336,12 +332,7 @@
         out_shape=(ends, ends),
         in_specs=[HBM],
         out_specs=(VMEM, VMEM),
-        scratch_shapes=[
-            pltpu.VMEM((channels, LOW, lanes), jnp.float32),
-            pltpu.VMEM((channels, LOW, lanes), jnp.float32),
-            pltpu.VMEM((channels, HIGH - LOW, lanes), jnp.float32),
-            pltpu.SemaphoreType.DMA((3,)),
-        ],
+        scratch_shapes=[pltpu.SemaphoreType.DMA((2, HIGH))],
         compiler_params=params(2),
         name="ends",
     )(placed_in(fields[0], pltpu.HBM))
@@ -409,7 +400,6 @@
             pltpu.VMEM((groups + 1, channels, lanes), jnp.float32),
             pltpu.VMEM((groups + 1, channels, lanes), jnp.float32),
             pltpu.VMEM((groups + 1, channels, lanes), jnp.float32),
-            pltpu.VMEM((tiles, 4, WINDOW, channels, lanes), jnp.float32),
         ],
         compiler_params=params(8),
         name="advect",

time: 40.8 us -> 40.7 us (level)
  no operation moved by 1% of the time
where the time goes in v7:
time: 40.7 us; the launch traced here: 40.2 us
  starting transfers between devices  15.8 us (39%)
  blocking collectives  15.8 us (39%)
  Pallas kernels  5.8 us (14%)
  waiting for transfers between devices  2.04 us (5%)
  between operations  0.72 us (2%)
    ppermute x4, starting transfers between devices, swap(): return lax.ppermute(array, axis, pairs)  15.8 us
    all_to_all x1, blocking collectives, body(): lax.all_to_all(message.reshape(2 * lon_count, 1, width), ('panel', 'lon')...  15.8 us
    ppermute x4, waiting for transfers between devices, swap(): return lax.ppermute(array, axis, pairs)  2.04 us
    pallas_call x1, Pallas kernels, body(): pl.pallas_call(own_kernel, out_shape=(f32(row_count, channels, lanes), pa...  1.43 us
    pallas_call x1, Pallas kernels, body(): pl.pallas_call(advect_kernel, out_shape=(pltpu.VMEM((channels * row_count...  1.31 us
    pallas_call x1, Pallas kernels, body(): pl.pallas_call(functools.partial(finish_kernel, lon_count), out_shape=plt...  1.16 us
    pallas_call x1, Pallas kernels, body(): pl.pallas_call(ends_kernel, out_shape=(ends, ends), in_specs=[HBM], out_s...  1.05 us
  transfers between devices with their start and end apart: 4, of which 2 were waited for; matrix products, arithmetic and copies ran while one was open for 0% of the time, Pallas kernels for 5%

profile of v7, /device:TPU:192, one launch (start us, length us, event | category | flops | bytes accessed | tf_op | source)
XLA Modules:
  0.0 40.2 jit_solution(14858661492216417741)
XLA Ops:
  0.0 1.1 %ends.1 = (f32[9,24,128]{2,1,0:T(8,128)S(1)}, f32[9,24,128]{2,1,0:T(8,128)S(1)}) custom-call(f32[24,32,128]{2,1,0:T(8,128)} %bitcast.19), custom_call_target="tpu_custom_call" | custom-call | tf_op jit(solution)/shard_map/ends/pallas_call | solution.py:330
  1.1 0.7 %collective-permute-start = (f32[9,24,128]{2,1,0:T(8,128)S(1)}, f32[9,24,128]{2,1,0:T(8,128)S(1)}, u32[]{:S(2)}, u32[]{:S(2)}) collective-permute-start(f32[9,24,128]{2,1,0:T(8,128)S(1)} %get-tuple-element.29), channel_id=1, source_target_pairs={{8,16},{16,8},{24,32},{32,24},{40,48},{48,40},{56,64},{64,56},{72,... | collective-permute-start | bytes 331784 | tf_op jit(solution)/shard_map/ppermute | solution.py:317
  1.7 6.3 %collective-permute-start.1 = (f32[9,24,128]{2,1,0:T(8,128)S(1)}, f32[9,24,128]{2,1,0:T(8,128)S(1)}, u32[]{:S(2)}, u32[]{:S(2)}) collective-permute-start(f32[9,24,128]{2,1,0:T(8,128)S(1)} %get-tuple-element.30), channel_id=1, source_target_pairs={{0,8},{8,0},{16,24},{24,16},{32,40},{40,32},{48,56},{56,48},{64,72... | collective-permute-start | bytes 331784 | tf_op jit(solution)/shard_map/ppermute | solution.py:317
  8.7 1.4 %own.1 = (f32[32,24,128]{2,1,0:T(8,128)S(1)}, f32[3,24,128]{2,1,0:T(8,128)S(1)}, f32[3,24,128]{2,1,0:T(8,128)S(1)}, f32[3,24,128]{2,1,0:T(8,128)S(1)}, f32[8,32,...) custom-call(s32[1,1]{1,0:T(1,128)} %bitcast.15.count_ref, ...), custom_call_target="tpu_custom_call" | custom-call | flops 400000 | bytes 800000 | tf_op jit(solution)/shard_map/own/pallas_call | solution.py:350
  10.1 0.0 collective-permute-done.from_first_ref
  10.1 0.7 %collective-permute-done.1.from_second_ref = f32[9,24,128]{2,1,0:T(8,128)S(1)} collective-permute-done((f32[9,24,128]{2,1,0:T(8,128)S(1)}, f32[9,24,128]{2,1,0:T(8,128)S(1)}, u32[]{:S(2)}, u32[]{:S(2)}) %collective-permute-start.1) | collective-permute-done | bytes 110624 | tf_op jit(solution)/shard_map/ppermute | solution.py:317
  10.8 0.2 sides.1
  11.0 1.9 %collective-permute-start.2 = (f32[4,24,128]{2,1,0:T(8,128)S(1)}, f32[4,24,128]{2,1,0:T(8,128)S(1)}, u32[]{:S(2)}, u32[]{:S(2)}) collective-permute-start(f32[4,24,128]{2,1,0:T(8,128)S(1)} %get-tuple-element.35), channel_id=1, source_target_pairs={{0,1},{1,0},{2,3},{3,2},{4,5},{5,4},{6,7},{7,6},{8,9},{9,8},{10,11... | collective-permute-start | bytes 147464 | tf_op jit(solution)/shard_map/ppermute | solution.py:317
  12.9 7.0 %collective-permute-start.3 = (f32[4,24,128]{2,1,0:T(8,128)S(1)}, f32[4,24,128]{2,1,0:T(8,128)S(1)}, u32[]{:S(2)}, u32[]{:S(2)}) collective-permute-start(f32[4,24,128]{2,1,0:T(8,128)S(1)} %get-tuple-element.36), channel_id=1, source_target_pairs={{1,2},{2,1},{3,4},{4,3},{5,6},{6,5},{9,10},{10,9},{11,12},{12,11},... | collective-permute-start | bytes 147464 | tf_op jit(solution)/shard_map/ppermute | solution.py:317
  19.9 0.7 %centers.1.centers_ref = f32[4,4,11,24,128]{4,3,2,1,0:T(8,128)S(1)} custom-call(s32[2,1,4]{2,1,0:T(1,128)S(4)} %get-tuple-element.23.offsets_ref, f32[32,24,128]{2,1,0:T(8,128)S(1)} %get-tuple-element.28.rows_ref, f32[9,24,128]{2,1,0:T(8,128)S(1)} %collective-permute-done.from_first_ref, f32[9,24,128]{2,1,0:T(8,128)S(1)} %collective-permute-done.1.from_second_ref), custom_call_target="tpu_custom_call" | custom-call | flops 400000 | bytes 3000000 | tf_op jit(solution)/shard_map/centers/pallas_call | solution.py:380
  20.5 0.0 collective-permute-done.2.from_first_ref
  20.5 1.4 %collective-permute-done.3.from_second_ref = f32[4,24,128]{2,1,0:T(8,128)S(1)} collective-permute-done((f32[4,24,128]{2,1,0:T(8,128)S(1)}, f32[4,24,128]{2,1,0:T(8,128)S(1)}, u32[]{:S(2)}, u32[]{:S(2)}) %collective-permute-start.3) | collective-permute-done | bytes 49184 | tf_op jit(solution)/shard_map/ppermute | solution.py:317
  21.9 1.3 %advect.1 = (f32[768,128]{1,0:T(8,128)S(1)}, f32[128,128]{1,0:T(8,128)S(1)}) custom-call(s32[1,1]{1,0:T(1,128)S(4)} %get-tuple-element.22.count_ref, s32[2,1,4]{2,1,0:T(1,128)S(4)} %get-tuple-element.23.offsets_ref, s32[1,16]{1,0:T(1,128)S(4)} %get-tuple-element.24.owner_ref, s32[1,16]{1,0:T(1,128)S(4)} %get-tuple-element.25.cell_ref, ...), custom_call_target="tpu_custom_call" | custom-call | tf_op jit(solution)/shard_map/advect/pallas_call | solution.py:390
  23.2 15.8 %all_to_all.5 = f32[64,1,256]{2,1,0:T(1,128)S(1)} all-to-all(f32[64,1,256]{2,1,0:T(1,128)S(1)} %bitcast.18), channel_id=1, replica_groups={{416,424,432,440,448,456,464,472,480,488,496,504,256,264,272,280,288,29..., dimensions={0} | all-to-all | bytes 131072 | tf_op jit(solution)/shard_map/all_to_all | solution.py:411
  39.0 1.2 %finish.1 = f32[24,32,128]{2,1,0:T(8,128)} custom-call(f32[128,128]{1,0:T(8,128)S(1)} %bitcast.17, f32[24,32,128]{2,1,0:T(8,128)S(1)} %bitcast.16), custom_call_target="tpu_custom_call" | custom-call | tf_op jit(solution)/shard_map/finish/pallas_call | solution.py:419
Async XLA Ops:
  1.1 9.1 %collective-permute-start = (f32[9,24,128]{2,1,0:T(8,128)S(1)}, f32[9,24,128]{2,1,0:T(8,128)S(1)}, u32[]{:S(2)}, u32[]{:S(2)}) collective-permute-start(f32[9,24,128]{2,1,0:T(8,128)S(1)} %get-tuple-element.29), channel_id=1, source_target_pairs={{8,16},{16,8},{24,32},{32,24},{40,48},{48,40},{56,64},{64,56},{72,... | collective-permute-start | bytes 331784 | tf_op jit(solution)/shard_map/ppermute | solution.py:317
  1.7 9.1 %collective-permute-start.1 = (f32[9,24,128]{2,1,0:T(8,128)S(1)}, f32[9,24,128]{2,1,0:T(8,128)S(1)}, u32[]{:S(2)}, u32[]{:S(2)}) collective-permute-start(f32[9,24,128]{2,1,0:T(8,128)S(1)} %get-tuple-element.30), channel_id=1, source_target_pairs={{0,8},{8,0},{16,24},{24,16},{32,40},{40,32},{48,56},{56,48},{64,72... | collective-permute-start | bytes 331784 | tf_op jit(solution)/shard_map/ppermute | solution.py:317
  11.0 9.6 %collective-permute-start.2 = (f32[4,24,128]{2,1,0:T(8,128)S(1)}, f32[4,24,128]{2,1,0:T(8,128)S(1)}, u32[]{:S(2)}, u32[]{:S(2)}) collective-permute-start(f32[4,24,128]{2,1,0:T(8,128)S(1)} %get-tuple-element.35), channel_id=1, source_target_pairs={{0,1},{1,0},{2,3},{3,2},{4,5},{5,4},{6,7},{7,6},{8,9},{9,8},{10,11... | collective-permute-start | bytes 147464 | tf_op jit(solution)/shard_map/ppermute | solution.py:317
  12.9 9.0 %collective-permute-start.3 = (f32[4,24,128]{2,1,0:T(8,128)S(1)}, f32[4,24,128]{2,1,0:T(8,128)S(1)}, u32[]{:S(2)}, u32[]{:S(2)}) collective-permute-start(f32[4,24,128]{2,1,0:T(8,128)S(1)} %get-tuple-element.36), channel_id=1, source_target_pairs={{1,2},{2,1},{3,4},{4,3},{5,6},{6,5},{9,10},{10,9},{11,12},{12,11},... | collective-permute-start | bytes 147464 | tf_op jit(solution)/shard_map/ppermute | solution.py:317

commit v8 on v7

--- a/solution.py
+++ b/solution.py
@@ -165,7 +165,7 @@
 def advect_kernel(
     count_ref, offsets_ref, owner_ref, cell_ref, target_ref, frac_ref, centers_ref, weights_ref, from_first_ref, from_second_ref,
     columns_ref, message_ref,
-    advected_ref, east_ref, west_ref, ninth_ref,
+    advected_ref, east_ref, west_ref, ninth_ref, sums_ref, places_ref,
 ):
     row_count, channels, lanes = advected_ref.shape
     slots = owner_ref.shape[1]
@@ -221,9 +221,10 @@
     capacity = slots // 2
     halves = capacity * FIELD // lanes
     per_row = lanes // FIELD
-    sums = [jnp.zeros((channels, lanes), jnp.float32) for _ in range(2 * halves)]
+    sums_ref[...] = jnp.zeros_like(sums_ref)
     empty = jnp.where((one_lane & (FIELD - 1)) == channels, jnp.float32(lanes), jnp.float32(0.0))
-    places = [empty for _ in range(2 * halves)]
+    for h in range(2 * halves + 1):
+        places_ref[h] = empty
     taken = [jnp.int32(0), jnp.int32(0)]
     at_value = lane - channel
     for k in range(slots):
@@ -242,12 +243,11 @@
         position = jnp.where(side == 0, taken[0], taken[1])
         taken[0] = taken[0] + jnp.where(live & (side == 0), 1, 0)
         taken[1] = taken[1] + jnp.where(live & (side == 1), 1, 0)
-        base = (position % per_row) * FIELD
-        here = jnp.where(live, side * halves + position // per_row, -1)
-        for h in range(2 * halves):
-            lane_base = jnp.where(here == h, base, -lanes)
-            sums[h] = jnp.where(at_value == lane_base, value, sums[h])
-            places[h] = jnp.where(one_lane == lane_base + channels, target, places[h])
+        base = (position & (per_row - 1)) * FIELD
+        half = position >> (per_row.bit_length() - 1)
+        here = jnp.where(live, side * halves + half, 2 * halves)
+        sums_ref[here] = jnp.where(at_value == base, value, sums_ref[here])
+        places_ref[here] = jnp.where(one_lane == base + channels, target, places_ref[here])
     lon_count = message_ref.shape[0] // (2 * halves)
     other = 1 - lax.axis_index("panel")
     message_ref[...] = jnp.zeros_like(message_ref)
@@ -255,7 +255,9 @@
         for h in range(halves):
             n = side * halves + h
             row = place_of(other, side * (lon_count - 1), lon_count) * halves + h
-            message_ref[pl.ds(row, 1), :] = jnp.sum(sums[n], axis=0, keepdims=True) + places[n]
+            message_ref[pl.ds(row, 1), :] = (
+                jnp.sum(sums_ref[n], axis=0, keepdims=True) + places_ref[n]
+            )
 
 
 def finish_kernel(lon_count, received_ref, columns_ref, out_ref, held_ref, sems):
@@ -400,6 +402,8 @@
             pltpu.VMEM((groups + 1, channels, lanes), jnp.float32),
             pltpu.VMEM((groups + 1, channels, lanes), jnp.float32),
             pltpu.VMEM((groups + 1, channels, lanes), jnp.float32),
+            pltpu.VMEM((2 * (width // lanes) + 1, channels, lanes), jnp.float32),
+            pltpu.VMEM((2 * (width // lanes) + 1, 1, lanes), jnp.float32),
         ],
         compiler_params=params(8),
         name="advect",

time: 40.7 us -> 40.7 us (level)
  no operation moved by 1% of the time
where the time goes in v8:
time: 40.7 us; the launch traced here: 40.2 us
  starting transfers between devices  15.8 us (39%)
  blocking collectives  15.7 us (39%)
  Pallas kernels  5.82 us (14%)
  waiting for transfers between devices  2.04 us (5%)
  between operations  0.72 us (2%)
    ppermute x4, starting transfers between devices, swap(): return lax.ppermute(array, axis, pairs)  15.8 us
    all_to_all x1, blocking collectives, body(): lax.all_to_all(message.reshape(2 * lon_count, 1, width), ('panel', 'lon')...  15.7 us
    ppermute x4, waiting for transfers between devices, swap(): return lax.ppermute(array, axis, pairs)  2.04 us
    pallas_call x1, Pallas kernels, body(): pl.pallas_call(own_kernel, out_shape=(f32(row_count, channels, lanes), pa...  1.43 us
    pallas_call x1, Pallas kernels, body(): pl.pallas_call(advect_kernel, out_shape=(pltpu.VMEM((channels * row_count...  1.33 us
    pallas_call x1, Pallas kernels, body(): pl.pallas_call(functools.partial(finish_kernel, lon_count), out_shape=plt...  1.16 us
    pallas_call x1, Pallas kernels, body(): pl.pallas_call(ends_kernel, out_shape=(ends, ends), in_specs=[HBM], out_s...  1.05 us
  transfers between devices with their start and end apart: 4, of which 2 were waited for; matrix products, arithmetic and copies ran while one was open for 0% of the time, Pallas kernels for 5%

profile of v8, /device:TPU:192, one launch (start us, length us, event | category | flops | bytes accessed | tf_op | source)
XLA Modules:
  0.0 40.2 jit_solution(8245143680082178452)
XLA Ops:
  0.0 1.1 %ends.1 = (f32[9,24,128]{2,1,0:T(8,128)S(1)}, f32[9,24,128]{2,1,0:T(8,128)S(1)}) custom-call(f32[24,32,128]{2,1,0:T(8,128)} %bitcast.19), custom_call_target="tpu_custom_call" | custom-call | tf_op jit(solution)/shard_map/ends/pallas_call | solution.py:332
  1.1 0.7 %collective-permute-start = (f32[9,24,128]{2,1,0:T(8,128)S(1)}, f32[9,24,128]{2,1,0:T(8,128)S(1)}, u32[]{:S(2)}, u32[]{:S(2)}) collective-permute-start(f32[9,24,128]{2,1,0:T(8,128)S(1)} %get-tuple-element.29), channel_id=1, source_target_pairs={{8,16},{16,8},{24,32},{32,24},{40,48},{48,40},{56,64},{64,56},{72,... | collective-permute-start | bytes 331784 | tf_op jit(solution)/shard_map/ppermute | solution.py:319
  1.7 6.3 %collective-permute-start.1 = (f32[9,24,128]{2,1,0:T(8,128)S(1)}, f32[9,24,128]{2,1,0:T(8,128)S(1)}, u32[]{:S(2)}, u32[]{:S(2)}) collective-permute-start(f32[9,24,128]{2,1,0:T(8,128)S(1)} %get-tuple-element.30), channel_id=1, source_target_pairs={{0,8},{8,0},{16,24},{24,16},{32,40},{40,32},{48,56},{56,48},{64,72... | collective-permute-start | bytes 331784 | tf_op jit(solution)/shard_map/ppermute | solution.py:319
  8.7 1.4 %own.1 = (f32[32,24,128]{2,1,0:T(8,128)S(1)}, f32[3,24,128]{2,1,0:T(8,128)S(1)}, f32[3,24,128]{2,1,0:T(8,128)S(1)}, f32[3,24,128]{2,1,0:T(8,128)S(1)}, f32[8,32,...) custom-call(s32[1,1]{1,0:T(1,128)} %bitcast.15.count_ref, ...), custom_call_target="tpu_custom_call" | custom-call | flops 400000 | bytes 800000 | tf_op jit(solution)/shard_map/own/pallas_call | solution.py:352
  10.1 0.0 collective-permute-done.from_first_ref
  10.1 0.7 %collective-permute-done.1.from_second_ref = f32[9,24,128]{2,1,0:T(8,128)S(1)} collective-permute-done((f32[9,24,128]{2,1,0:T(8,128)S(1)}, f32[9,24,128]{2,1,0:T(8,128)S(1)}, u32[]{:S(2)}, u32[]{:S(2)}) %collective-permute-start.1) | collective-permute-done | bytes 110624 | tf_op jit(solution)/shard_map/ppermute | solution.py:319
  10.8 0.2 sides.1
  11.0 1.9 %collective-permute-start.2 = (f32[4,24,128]{2,1,0:T(8,128)S(1)}, f32[4,24,128]{2,1,0:T(8,128)S(1)}, u32[]{:S(2)}, u32[]{:S(2)}) collective-permute-start(f32[4,24,128]{2,1,0:T(8,128)S(1)} %get-tuple-element.35), channel_id=1, source_target_pairs={{0,1},{1,0},{2,3},{3,2},{4,5},{5,4},{6,7},{7,6},{8,9},{9,8},{10,11... | collective-permute-start | bytes 147464 | tf_op jit(solution)/shard_map/ppermute | solution.py:319
  12.9 7.0 %collective-permute-start.3 = (f32[4,24,128]{2,1,0:T(8,128)S(1)}, f32[4,24,128]{2,1,0:T(8,128)S(1)}, u32[]{:S(2)}, u32[]{:S(2)}) collective-permute-start(f32[4,24,128]{2,1,0:T(8,128)S(1)} %get-tuple-element.36), channel_id=1, source_target_pairs={{1,2},{2,1},{3,4},{4,3},{5,6},{6,5},{9,10},{10,9},{11,12},{12,11},... | collective-permute-start | bytes 147464 | tf_op jit(solution)/shard_map/ppermute | solution.py:319
  19.9 0.7 %centers.1.centers_ref = f32[4,4,11,24,128]{4,3,2,1,0:T(8,128)S(1)} custom-call(s32[2,1,4]{2,1,0:T(1,128)S(4)} %get-tuple-element.23.offsets_ref, f32[32,24,128]{2,1,0:T(8,128)S(1)} %get-tuple-element.28.rows_ref, f32[9,24,128]{2,1,0:T(8,128)S(1)} %collective-permute-done.from_first_ref, f32[9,24,128]{2,1,0:T(8,128)S(1)} %collective-permute-done.1.from_second_ref), custom_call_target="tpu_custom_call" | custom-call | flops 400000 | bytes 3000000 | tf_op jit(solution)/shard_map/centers/pallas_call | solution.py:382
  20.5 0.0 collective-permute-done.2.from_first_ref
  20.5 1.4 %collective-permute-done.3.from_second_ref = f32[4,24,128]{2,1,0:T(8,128)S(1)} collective-permute-done((f32[4,24,128]{2,1,0:T(8,128)S(1)}, f32[4,24,128]{2,1,0:T(8,128)S(1)}, u32[]{:S(2)}, u32[]{:S(2)}) %collective-permute-start.3) | collective-permute-done | bytes 49184 | tf_op jit(solution)/shard_map/ppermute | solution.py:319
  21.9 1.3 %advect.1 = (f32[768,128]{1,0:T(8,128)S(1)}, f32[128,128]{1,0:T(8,128)S(1)}) custom-call(s32[1,1]{1,0:T(1,128)S(4)} %get-tuple-element.22.count_ref, s32[2,1,4]{2,1,0:T(1,128)S(4)} %get-tuple-element.23.offsets_ref, s32[1,16]{1,0:T(1,128)S(4)} %get-tuple-element.24.owner_ref, s32[1,16]{1,0:T(1,128)S(4)} %get-tuple-element.25.cell_ref, ...), custom_call_target="tpu_custom_call" | custom-call | tf_op jit(solution)/shard_map/advect/pallas_call | solution.py:392
  23.3 15.7 %all_to_all.5 = f32[64,1,256]{2,1,0:T(1,128)S(1)} all-to-all(f32[64,1,256]{2,1,0:T(1,128)S(1)} %bitcast.18), channel_id=1, replica_groups={{416,424,432,440,448,456,464,472,480,488,496,504,256,264,272,280,288,29..., dimensions={0} | all-to-all | bytes 131072 | tf_op jit(solution)/shard_map/all_to_all | solution.py:415
  39.0 1.2 %finish.1 = f32[24,32,128]{2,1,0:T(8,128)} custom-call(f32[128,128]{1,0:T(8,128)S(1)} %bitcast.17, f32[24,32,128]{2,1,0:T(8,128)S(1)} %bitcast.16), custom_call_target="tpu_custom_call" | custom-call | tf_op jit(solution)/shard_map/finish/pallas_call | solution.py:423
Async XLA Ops:
  1.1 9.1 %collective-permute-start = (f32[9,24,128]{2,1,0:T(8,128)S(1)}, f32[9,24,128]{2,1,0:T(8,128)S(1)}, u32[]{:S(2)}, u32[]{:S(2)}) collective-permute-start(f32[9,24,128]{2,1,0:T(8,128)S(1)} %get-tuple-element.29), channel_id=1, source_target_pairs={{8,16},{16,8},{24,32},{32,24},{40,48},{48,40},{56,64},{64,56},{72,... | collective-permute-start | bytes 331784 | tf_op jit(solution)/shard_map/ppermute | solution.py:319
  1.7 9.1 %collective-permute-start.1 = (f32[9,24,128]{2,1,0:T(8,128)S(1)}, f32[9,24,128]{2,1,0:T(8,128)S(1)}, u32[]{:S(2)}, u32[]{:S(2)}) collective-permute-start(f32[9,24,128]{2,1,0:T(8,128)S(1)} %get-tuple-element.30), channel_id=1, source_target_pairs={{0,8},{8,0},{16,24},{24,16},{32,40},{40,32},{48,56},{56,48},{64,72... | collective-permute-start | bytes 331784 | tf_op jit(solution)/shard_map/ppermute | solution.py:319
  11.0 9.6 %collective-permute-start.2 = (f32[4,24,128]{2,1,0:T(8,128)S(1)}, f32[4,24,128]{2,1,0:T(8,128)S(1)}, u32[]{:S(2)}, u32[]{:S(2)}) collective-permute-start(f32[4,24,128]{2,1,0:T(8,128)S(1)} %get-tuple-element.35), channel_id=1, source_target_pairs={{0,1},{1,0},{2,3},{3,2},{4,5},{5,4},{6,7},{7,6},{8,9},{9,8},{10,11... | collective-permute-start | bytes 147464 | tf_op jit(solution)/shard_map/ppermute | solution.py:319
  12.9 9.0 %collective-permute-start.3 = (f32[4,24,128]{2,1,0:T(8,128)S(1)}, f32[4,24,128]{2,1,0:T(8,128)S(1)}, u32[]{:S(2)}, u32[]{:S(2)}) collective-permute-start(f32[4,24,128]{2,1,0:T(8,128)S(1)} %get-tuple-element.36), channel_id=1, source_target_pairs={{1,2},{2,1},{3,4},{4,3},{5,6},{6,5},{9,10},{10,9},{11,12},{12,11},... | collective-permute-start | bytes 147464 | tf_op jit(solution)/shard_map/ppermute | solution.py:319

commit v9 on v7

--- a/solution.py
+++ b/solution.py
@@ -262,19 +262,21 @@
     channels, row_count, lanes = out_ref.shape
     tiles = row_count // TILE
     lon = lax.axis_index("lon")
-
-    def tile_of(ref, t):
-        return ref.at[:, pl.ds(pl.multiple_of(t * TILE, TILE), TILE), :]
-
-    changed = jnp.where(lon == 0, 0, tiles - 1)
+    lowest = lon == 0
+
+    def copy_rows(n, first, count):
+        rows = (slice(None), pl.ds(first, count), slice(None))
+        return pltpu.make_async_copy(columns_ref.at[rows], out_ref.at[rows], sems.at[n])
+
     copies = []
     for n in range(tiles - 1):
-        t = n + jnp.where(lon == 0, 1, 0)
-        copies.append(
-            pltpu.make_async_copy(tile_of(columns_ref, t), tile_of(out_ref, t), sems.at[n])
-        )
-        copies[n].start()
-    held_ref[...] = columns_ref[:, pl.ds(pl.multiple_of(changed * TILE, TILE), TILE), :]
+        first = (n + jnp.where(lowest, 1, 0)) * TILE
+        copies.append(copy_rows(n, pl.multiple_of(first, TILE), TILE))
+    copies.append(copy_rows(tiles - 1, jnp.where(lowest, 1, row_count - TILE), TILE - 1))
+    for copy in copies:
+        copy.start()
+    changed = jnp.where(lowest, 0, row_count - 1)
+    held_ref[...] = columns_ref[:, pl.ds(changed, 1), :]
 
     @pl.when((lon == 0) | (lon == lon_count - 1))
     def _():
@@ -297,11 +299,11 @@
         rim = spread[0:channels, 0:lanes]
         for q in range(1, lanes // FIELD):
             rim = rim + spread[q * FIELD : q * FIELD + channels, q * lanes : (q + 1) * lanes]
-        row = jnp.where(lon == 0, 0, TILE - 1)
-        held_ref[:, pl.ds(row, 1), :] = rim.reshape(channels, 1, lanes)
-
-    copies.append(pltpu.make_async_copy(held_ref, tile_of(out_ref, changed), sems.at[tiles - 1]))
-    copies[tiles - 1].start()
+        held_ref[...] = rim.reshape(channels, 1, lanes)
+
+    target = out_ref.at[:, pl.ds(changed, 1), :]
+    copies.append(pltpu.make_async_copy(held_ref, target, sems.at[tiles]))
+    copies[tiles].start()
     for copy in copies:
         copy.wait()
 
@@ -422,8 +424,8 @@
         in_specs=[VMEM, VMEM],
         out_specs=HBM,
         scratch_shapes=[
-            pltpu.VMEM((channels, TILE, lanes), jnp.float32),
-            pltpu.SemaphoreType.DMA((tiles,)),
+            pltpu.VMEM((channels, 1, lanes), jnp.float32),
+            pltpu.SemaphoreType.DMA((tiles + 1,)),
         ],
         compiler_params=params(2),
         name="finish",

time: 40.7 us -> 40.6 us (level)
  no operation moved by 1% of the time
where the time goes in v9:
time: 40.6 us; the launch traced here: 40.2 us
  starting transfers between devices  15.8 us (39%)
  blocking collectives  15.8 us (39%)
  Pallas kernels  5.77 us (14%)
  waiting for transfers between devices  2.04 us (5%)
  between operations  0.72 us (2%)
    ppermute x4, starting transfers between devices, swap(): return lax.ppermute(array, axis, pairs)  15.8 us
    all_to_all x1, blocking collectives, body(): lax.all_to_all(message.reshape(2 * lon_count, 1, width), ('panel', 'lon')...  15.8 us
    ppermute x4, waiting for transfers between devices, swap(): return lax.ppermute(array, axis, pairs)  2.04 us
    pallas_call x1, Pallas kernels, body(): pl.pallas_call(own_kernel, out_shape=(f32(row_count, channels, lanes), pa...  1.43 us
    pallas_call x1, Pallas kernels, body(): pl.pallas_call(advect_kernel, out_shape=(pltpu.VMEM((channels * row_count...  1.31 us
    pallas_call x1, Pallas kernels, body(): pl.pallas_call(functools.partial(finish_kernel, lon_count), out_shape=plt...  1.13 us
    pallas_call x1, Pallas kernels, body(): pl.pallas_call(ends_kernel, out_shape=(ends, ends), in_specs=[HBM], out_s...  1.05 us
  transfers between devices with their start and end apart: 4, of which 2 were waited for; matrix products, arithmetic and copies ran while one was open for 0% of the time, Pallas kernels for 5%

profile of v9, /device:TPU:192, one launch (start us, length us, event | category | flops | bytes accessed | tf_op | source)
XLA Modules:
  0.0 40.2 jit_solution(11327875920353715757)
XLA Ops:
  0.0 1.1 %ends.1 = (f32[9,24,128]{2,1,0:T(8,128)S(1)}, f32[9,24,128]{2,1,0:T(8,128)S(1)}) custom-call(f32[24,32,128]{2,1,0:T(8,128)} %bitcast.19), custom_call_target="tpu_custom_call" | custom-call | tf_op jit(solution)/shard_map/ends/pallas_call | solution.py:332
  1.1 0.7 %collective-permute-start = (f32[9,24,128]{2,1,0:T(8,128)S(1)}, f32[9,24,128]{2,1,0:T(8,128)S(1)}, u32[]{:S(2)}, u32[]{:S(2)}) collective-permute-start(f32[9,24,128]{2,1,0:T(8,128)S(1)} %get-tuple-element.29), channel_id=1, source_target_pairs={{8,16},{16,8},{24,32},{32,24},{40,48},{48,40},{56,64},{64,56},{72,... | collective-permute-start | bytes 331784 | tf_op jit(solution)/shard_map/ppermute | solution.py:319
  1.7 6.3 %collective-permute-start.1 = (f32[9,24,128]{2,1,0:T(8,128)S(1)}, f32[9,24,128]{2,1,0:T(8,128)S(1)}, u32[]{:S(2)}, u32[]{:S(2)}) collective-permute-start(f32[9,24,128]{2,1,0:T(8,128)S(1)} %get-tuple-element.30), channel_id=1, source_target_pairs={{0,8},{8,0},{16,24},{24,16},{32,40},{40,32},{48,56},{56,48},{64,72... | collective-permute-start | bytes 331784 | tf_op jit(solution)/shard_map/ppermute | solution.py:319
  8.7 1.4 %own.1 = (f32[32,24,128]{2,1,0:T(8,128)S(1)}, f32[3,24,128]{2,1,0:T(8,128)S(1)}, f32[3,24,128]{2,1,0:T(8,128)S(1)}, f32[3,24,128]{2,1,0:T(8,128)S(1)}, f32[8,32,...) custom-call(s32[1,1]{1,0:T(1,128)} %bitcast.15.count_ref, ...), custom_call_target="tpu_custom_call" | custom-call | flops 400000 | bytes 800000 | tf_op jit(solution)/shard_map/own/pallas_call | solution.py:352
  10.1 0.0 collective-permute-done.from_first_ref
  10.1 0.7 %collective-permute-done.1.from_second_ref = f32[9,24,128]{2,1,0:T(8,128)S(1)} collective-permute-done((f32[9,24,128]{2,1,0:T(8,128)S(1)}, f32[9,24,128]{2,1,0:T(8,128)S(1)}, u32[]{:S(2)}, u32[]{:S(2)}) %collective-permute-start.1) | collective-permute-done | bytes 110624 | tf_op jit(solution)/shard_map/ppermute | solution.py:319
  10.8 0.2 sides.1
  11.0 1.9 %collective-permute-start.2 = (f32[4,24,128]{2,1,0:T(8,128)S(1)}, f32[4,24,128]{2,1,0:T(8,128)S(1)}, u32[]{:S(2)}, u32[]{:S(2)}) collective-permute-start(f32[4,24,128]{2,1,0:T(8,128)S(1)} %get-tuple-element.35), channel_id=1, source_target_pairs={{0,1},{1,0},{2,3},{3,2},{4,5},{5,4},{6,7},{7,6},{8,9},{9,8},{10,11... | collective-permute-start | bytes 147464 | tf_op jit(solution)/shard_map/ppermute | solution.py:319
  12.9 7.0 %collective-permute-start.3 = (f32[4,24,128]{2,1,0:T(8,128)S(1)}, f32[4,24,128]{2,1,0:T(8,128)S(1)}, u32[]{:S(2)}, u32[]{:S(2)}) collective-permute-start(f32[4,24,128]{2,1,0:T(8,128)S(1)} %get-tuple-element.36), channel_id=1, source_target_pairs={{1,2},{2,1},{3,4},{4,3},{5,6},{6,5},{9,10},{10,9},{11,12},{12,11},... | collective-permute-start | bytes 147464 | tf_op jit(solution)/shard_map/ppermute | solution.py:319
  19.9 0.7 %centers.1.centers_ref = f32[4,4,11,24,128]{4,3,2,1,0:T(8,128)S(1)} custom-call(s32[2,1,4]{2,1,0:T(1,128)S(4)} %get-tuple-element.23.offsets_ref, f32[32,24,128]{2,1,0:T(8,128)S(1)} %get-tuple-element.28.rows_ref, f32[9,24,128]{2,1,0:T(8,128)S(1)} %collective-permute-done.from_first_ref, f32[9,24,128]{2,1,0:T(8,128)S(1)} %collective-permute-done.1.from_second_ref), custom_call_target="tpu_custom_call" | custom-call | flops 400000 | bytes 3000000 | tf_op jit(solution)/shard_map/centers/pallas_call | solution.py:382
  20.5 0.0 collective-permute-done.2.from_first_ref
  20.5 1.4 %collective-permute-done.3.from_second_ref = f32[4,24,128]{2,1,0:T(8,128)S(1)} collective-permute-done((f32[4,24,128]{2,1,0:T(8,128)S(1)}, f32[4,24,128]{2,1,0:T(8,128)S(1)}, u32[]{:S(2)}, u32[]{:S(2)}) %collective-permute-start.3) | collective-permute-done | bytes 49184 | tf_op jit(solution)/shard_map/ppermute | solution.py:319
  21.9 1.3 %advect.1 = (f32[768,128]{1,0:T(8,128)S(1)}, f32[128,128]{1,0:T(8,128)S(1)}) custom-call(s32[1,1]{1,0:T(1,128)S(4)} %get-tuple-element.22.count_ref, s32[2,1,4]{2,1,0:T(1,128)S(4)} %get-tuple-element.23.offsets_ref, s32[1,16]{1,0:T(1,128)S(4)} %get-tuple-element.24.owner_ref, s32[1,16]{1,0:T(1,128)S(4)} %get-tuple-element.25.cell_ref, ...), custom_call_target="tpu_custom_call" | custom-call | tf_op jit(solution)/shard_map/advect/pallas_call | solution.py:392
  23.2 15.8 %all_to_all.5 = f32[64,1,256]{2,1,0:T(1,128)S(1)} all-to-all(f32[64,1,256]{2,1,0:T(1,128)S(1)} %bitcast.18), channel_id=1, replica_groups={{416,424,432,440,448,456,464,472,480,488,496,504,256,264,272,280,288,29..., dimensions={0} | all-to-all | bytes 131072 | tf_op jit(solution)/shard_map/all_to_all | solution.py:413
  39.0 1.1 %finish.1 = f32[24,32,128]{2,1,0:T(8,128)} custom-call(f32[128,128]{1,0:T(8,128)S(1)} %bitcast.17, f32[24,32,128]{2,1,0:T(8,128)S(1)} %bitcast.16), custom_call_target="tpu_custom_call" | custom-call | tf_op jit(solution)/shard_map/finish/pallas_call | solution.py:421
Async XLA Ops:
  1.1 9.1 %collective-permute-start = (f32[9,24,128]{2,1,0:T(8,128)S(1)}, f32[9,24,128]{2,1,0:T(8,128)S(1)}, u32[]{:S(2)}, u32[]{:S(2)}) collective-permute-start(f32[9,24,128]{2,1,0:T(8,128)S(1)} %get-tuple-element.29), channel_id=1, source_target_pairs={{8,16},{16,8},{24,32},{32,24},{40,48},{48,40},{56,64},{64,56},{72,... | collective-permute-start | bytes 331784 | tf_op jit(solution)/shard_map/ppermute | solution.py:319
  1.7 9.1 %collective-permute-start.1 = (f32[9,24,128]{2,1,0:T(8,128)S(1)}, f32[9,24,128]{2,1,0:T(8,128)S(1)}, u32[]{:S(2)}, u32[]{:S(2)}) collective-permute-start(f32[9,24,128]{2,1,0:T(8,128)S(1)} %get-tuple-element.30), channel_id=1, source_target_pairs={{0,8},{8,0},{16,24},{24,16},{32,40},{40,32},{48,56},{56,48},{64,72... | collective-permute-start | bytes 331784 | tf_op jit(solution)/shard_map/ppermute | solution.py:319
  11.0 9.6 %collective-permute-start.2 = (f32[4,24,128]{2,1,0:T(8,128)S(1)}, f32[4,24,128]{2,1,0:T(8,128)S(1)}, u32[]{:S(2)}, u32[]{:S(2)}) collective-permute-start(f32[4,24,128]{2,1,0:T(8,128)S(1)} %get-tuple-element.35), channel_id=1, source_target_pairs={{0,1},{1,0},{2,3},{3,2},{4,5},{5,4},{6,7},{7,6},{8,9},{9,8},{10,11... | collective-permute-start | bytes 147464 | tf_op jit(solution)/shard_map/ppermute | solution.py:319
  12.9 9.0 %collective-permute-start.3 = (f32[4,24,128]{2,1,0:T(8,128)S(1)}, f32[4,24,128]{2,1,0:T(8,128)S(1)}, u32[]{:S(2)}, u32[]{:S(2)}) collective-permute-start(f32[4,24,128]{2,1,0:T(8,128)S(1)} %get-tuple-element.36), channel_id=1, source_target_pairs={{1,2},{2,1},{3,4},{4,3},{5,6},{6,5},{9,10},{10,9},{11,12},{12,11},... | collective-permute-start | bytes 147464 | tf_op jit(solution)/shard_map/ppermute | solution.py:319
